TPU v7x, 256 devices: a whole 4x4x8 slice. The times are simulated.
256 devices in a mesh: dx: 16 (over z_lo, x, core), dy: 4 (over z_hi), band: 4 (over y).
Axes of the slice: x: 4, y: 4, z: 8 (z_hi: 4, z_lo: 2; z = z_hi * 2 + z_lo), core: 2. Of those that a mesh axis runs over, the one named last changes fastest.
Arguments:
- band_fields: float32 [8, 80, 320, 320], P('band', 'dx', 'dy'), may hold values from -36 to 36
- potential: float32 [80, 320, 320], P('dx', 'dy'), may hold values from -2 to 1
- cutoff: float32 [1], replicated, may hold values from 1 to 2
- upper_bound: float32 [1], replicated, may hold values from 11 to 12.5
Outputs:
- rotated: float32 [8, 80, 320, 320], P('band', 'dx', 'dy')
All inputs are finite; a program needn't handle non-finite values.
Results may differ from a plain program's by a relative error of at most 0.000075.
Values sent between devices are 32-bit elements; how exact they have to be, the bound alone decides.
No kernel may reach another device: no remote copies, remote signals or barrier semaphores. Data moves between devices by JAX's collectives and lax.ppermute only.
A program may use at most 64 MiB of HBM per device.

v0:
```python
import functools

import jax
import jax.numpy as jnp
from jax import lax
from jax.experimental import pallas as pl
from jax.experimental.pallas import tpu as pltpu
from jax.sharding import PartitionSpec as P

BANDS = 2
LAYERS = 5
WIDTH = 4
GROUPS = 4
F32 = jnp.float32

stencil_weights = (-205.0 / 72.0, 8.0 / 5.0, -1.0 / 5.0, 8.0 / 315.0, -1.0 / 560.0)

STATE = (BANDS, LAYERS, 3, 10, 8, 128)
SIDE = (BANDS, WIDTH, 25, 8, 128)
EDGE = (BANDS, 64, 128)
PIECE = (BANDS, 32, 8, 128)


def call(kernel, outs, scratch=(), in_specs=None, cost=4_000_000):
    kwargs = {} if in_specs is None else {"in_specs": in_specs}
    return pl.pallas_call(
        kernel,
        out_shape=tuple(jax.ShapeDtypeStruct(shape, F32) for shape in outs),
        scratch_shapes=[pltpu.VMEM(shape, F32) for shape in scratch],
        compiler_params=pltpu.CompilerParams(vmem_limit_bytes=16 * 1024 * 1024),
        cost_estimate=pl.CostEstimate(flops=cost, bytes_accessed=4_000_000, transcendentals=0),
        **kwargs,
    )


def lanes():
    return lax.broadcasted_iota(jnp.int32, (8, 128), 1)


def sublanes():
    return lax.broadcasted_iota(jnp.int32, (8, 128), 0)


def pair(low, high):
    return jnp.where(lanes() < 64, low, pltpu.roll(high, 64, 1))


def bounds(cutoff_ref, upper_ref):
    low = jnp.broadcast_to(cutoff_ref[...], (8, 128))
    high = jnp.broadcast_to(upper_ref[...], (8, 128))
    return 0.5 * (low + high), 1.0 / (0.5 * (high - low))


def send_sides(tiles, band, layer, low_ref, high_ref):
    for tile in range(2):
        for j in range(10):
            if layer < WIDTH:
                low_ref[band, layer, tile * 10 + j] = tiles[tile][j]
            if layer >= 1:
                high_ref[band, layer - 1, tile * 10 + j] = tiles[tile][j]
    for j in range(5):
        both = pair(tiles[2][j], tiles[2][j + 5])
        if layer < WIDTH:
            low_ref[band, layer, 20 + j] = both
        if layer >= 1:
            high_ref[band, layer - 1, 20 + j] = both


def send_edges(tiles, band, layer, low_ref, high_ref):
    for tile in range(3):
        for j in range(4):
            row = j * 16 + layer * 3 + tile
            low_ref[band, row : row + 1, :] = tiles[tile][j][0:1]
            high_ref[band, row : row + 1, :] = tiles[tile][6 + j][7:8]


def clear_edges(band, *refs):
    for ref in refs:
        for j in range(4):
            ref[band, j * 16 + 15 : j * 16 + 16, :] = jnp.zeros((1, 128), F32)


def parity(axis):
    return lax.rem(lax.axis_index(axis), 2)


def by_parity(axis, body, first, second):
    @pl.when(parity(axis) == 0)
    def even():
        body(first, second)

    @pl.when(parity(axis) == 1)
    def odd():
        body(second, first)


def hand_edges(edge_ref, inner_ref, outer_ref):
    def copy(low_ref, high_ref):
        low_ref[...] = edge_ref[0]
        high_ref[...] = edge_ref[1]

    by_parity("dy", copy, outer_ref, inner_ref)


def split_kernel(field_ref, state_ref, far_ref, near_ref, inner_ref, outer_ref, stage_ref, edge_ref):
    def body(side_low_ref, side_high_ref):
        def one_band(band, carry):
            for layer in range(LAYERS):
                for tile in range(2):
                    stage_ref[tile] = field_ref[band, layer, :, tile * 128 : tile * 128 + 128]
                stage_ref[2, :, 0:64] = field_ref[band, layer, :, 256:320]
                tiles = [[stage_ref[tile, pl.ds(j, 8, stride=10), :] for j in range(10)] for tile in range(3)]
                for tile in range(3):
                    for j in range(10):
                        state_ref[band, layer, tile, j] = tiles[tile][j]
                send_sides(tiles, band, layer, side_low_ref, side_high_ref)
                send_edges(tiles, band, layer, edge_ref.at[0], edge_ref.at[1])
            clear_edges(band, edge_ref.at[0], edge_ref.at[1])
            return carry

        lax.fori_loop(0, BANDS, one_band, 0)

    by_parity("dx", body, far_ref, near_ref)
    hand_edges(edge_ref, inner_ref, outer_ref)


def inner_kernel(first, *refs):
    if first:
        state_ref, potential_ref, cutoff_ref, upper_ref, out_ref, diagonal_ref, wide_ref, stage_ref = refs
    else:
        state_ref, previous_ref, diagonal_ref, cutoff_ref, upper_ref, out_ref, wide_ref = refs
    center, per_half_width = bounds(cutoff_ref, upper_ref)
    if first:
        shift = center + 1.5 * stencil_weights[0]
        for layer in range(LAYERS):
            for tile in range(2):
                stage_ref[tile] = potential_ref[layer, :, tile * 128 : tile * 128 + 128]
            stage_ref[2, :, 0:64] = potential_ref[layer, :, 256:320]
            for tile in range(3):
                for j in range(10):
                    cells = stage_ref[tile, pl.ds(j, 8, stride=10), :]
                    diagonal_ref[layer, tile, j] = 2.0 * ((cells - shift) * per_half_width)
    factor = 1.0 if first else 2.0
    weights = [None] + [(-0.5 * factor * stencil_weights[k]) * per_half_width for k in range(1, 5)]
    lane = lanes()
    row = sublanes()

    def one_band(band, carry):
        def widen(j, carry):
            for layer in range(LAYERS):
                tiles = [state_ref[band, layer, tile, j] for tile in range(3)]
                tiles[2] = jnp.where(
                    lane < 64,
                    tiles[2],
                    jnp.where(lane < 96, pltpu.roll(tiles[0], 64, 1), pltpu.roll(tiles[2], 64, 1)),
                )
                for tile in range(3):
                    wide_ref[layer, tile, j + 4] = tiles[tile]
            return carry

        lax.fori_loop(0, 10, widen, 0)

        def wrap(j, carry):
            for layer in range(LAYERS):
                for tile in range(3):
                    above = wide_ref[layer, tile, j + 4]
                    wide_ref[layer, tile, j + 14] = jnp.where(row < 7, pltpu.roll(above, 7, 0), 0.0)
                    below = wide_ref[layer, tile, j + 10]
                    wide_ref[layer, tile, j] = jnp.where(row > 0, pltpu.roll(below, 1, 0), 0.0)
            return carry

        lax.fori_loop(0, 4, wrap, 0)

        def rows(j, carry):
            mids = [[wide_ref[layer, tile, j + 4] for tile in range(3)] for layer in range(LAYERS)]
            for layer in range(LAYERS):
                mid = mids[layer]
                lefts = [pltpu.roll(mid[tile], 1, 1) for tile in range(3)]
                lefts = [jnp.where(lane < 1, lefts[(tile + 2) % 3], lefts[tile]) for tile in range(3)]
                rights = [pltpu.roll(mid[tile], 127, 1) for tile in range(3)]
                rights = [jnp.where(lane < 127, rights[tile], rights[(tile + 1) % 3]) for tile in range(3)]
                ups, downs = [], []
                for tile in range(3):
                    centre = weights[3] * mid[tile]
                    ups.append(centre + weights[2] * lefts[tile] + weights[4] * rights[tile])
                    downs.append(centre + weights[4] * lefts[tile] + weights[2] * rights[tile])
                ups = [pltpu.roll(up, 125, 1) for up in ups]
                downs = [pltpu.roll(down, 3, 1) for down in downs]
                for tile in range(3):
                    up = ups[2] if tile == 2 else jnp.where(lane < 125, ups[tile], ups[tile + 1])
                    total = up + jnp.where(lane < 3, downs[(tile + 2) % 3], downs[tile])
                    for k in range(1, 5):
                        part = wide_ref[layer, tile, j + 4 + k] + wide_ref[layer, tile, j + 4 - k]
                        if k == 1:
                            part += lefts[tile] + rights[tile]
                        if layer + k < LAYERS:
                            part += mids[layer + k][tile]
                        if layer - k >= 0:
                            part += mids[layer - k][tile]
                        total += weights[k] * part
                    diagonal = diagonal_ref[layer, tile, j] * mid[tile]
                    if first:
                        out_ref[band, layer, tile, j] = total + 0.5 * diagonal
                    else:
                        out_ref[band, layer, tile, j] = total + (diagonal - previous_ref[band, layer, tile, j])
            return carry

        return lax.fori_loop(0, 10, rows, carry)

    lax.fori_loop(0, BANDS, one_band, 0)


def outer_kernel(first, last, *refs):
    part_ref, far_in_ref, near_in_ref, inner_in_ref, outer_in_ref, cutoff_ref, upper_ref, *refs = refs
    if last:
        *piece_refs, rim_ref, whole_ref = refs
        state_ref, far_ref, near_ref, edge_ref = None, None, None, None
    else:
        state_ref, far_ref, near_ref, inner_ref, outer_ref, rim_ref, edge_ref = refs
        whole_ref = None
    _, per_half_width = bounds(cutoff_ref, upper_ref)
    factor = 1.0 if first else 2.0
    weights = [None] + [(-0.5 * factor * stencil_weights[k]) * per_half_width for k in range(1, 5)]

    def rims(below_ref, above_ref):
        def one_band(band, carry):
            for half in range(2):
                below = [below_ref[band, 16 * j + 8 * half : 16 * j + 8 * half + 8, :] for j in range(4)]
                above = [above_ref[band, 16 * j + 8 * half : 16 * j + 8 * half + 8, :] for j in range(4)]
                for j in range(4):
                    rim_ref[band, 0, j, 8 * half : 8 * half + 8, :] = sum(
                        weights[k] * below[4 + j - k] for k in range(j + 1, 5)
                    )
                    rim_ref[band, 1, j, 8 * half : 8 * half + 8, :] = sum(
                        weights[k] * above[j + 6 + k - 10] for k in range(4 - j, 5)
                    )
            return carry

        lax.fori_loop(0, BANDS, one_band, 0)

    by_parity("dy", rims, outer_in_ref, inner_in_ref)

    def body(low, high):
        add_outside(weights, part_ref, rim_ref, low, high, state_ref, edge_ref, whole_ref)

    by_parity("dx", body, (far_in_ref, far_ref), (near_in_ref, near_ref))
    if last:
        deal(whole_ref, piece_refs)
    else:
        hand_edges(edge_ref, inner_ref, outer_ref)


def add_outside(weights, part_ref, rim_ref, low, high, state_ref, edge_ref, whole_ref):
    low_ref, side_low_ref = low
    high_ref, side_high_ref = high
    last = whole_ref is not None
    row = sublanes()

    def one_band(band, carry):
        for layer in range(LAYERS):
            outside = []
            for v in range(25):
                terms = [weights[layer + 4 - i] * low_ref[band, i, v] for i in range(layer, 4)]
                terms += [weights[5 + i - layer] * high_ref[band, i, v] for i in range(layer)]
                outside.append((terms[0] + terms[1]) + (terms[2] + terms[3]))
            tiles = []
            for tile in range(3):
                cells = []
                for j in range(10):
                    if tile < 2:
                        extra = outside[tile * 10 + j]
                    elif j < 5:
                        extra = outside[20 + j]
                    else:
                        extra = pltpu.roll(outside[15 + j], 64, 1)
                    cell = part_ref[band, layer, tile, j] + extra
                    at = layer * 3 + tile
                    if j < 4:
                        cell += jnp.where(row == 0, rim_ref[band, 0, j, at : at + 1, :], 0.0)
                    if j >= 6:
                        cell += jnp.where(row == 7, rim_ref[band, 1, j - 6, at : at + 1, :], 0.0)
                    cells.append(cell)
                tiles.append(cells)
            if last:
                packed = tiles[0] + tiles[1] + [pair(tiles[2][j], tiles[2][j + 5]) for j in range(5)]
                for v in range(25):
                    place = layer * 25 + v
                    whole_ref[place // 32, band, place % 32] = packed[v]
            else:
                for tile in range(3):
                    for j in range(10):
                        state_ref[band, layer, tile, j] = tiles[tile][j]
                send_sides(tiles, band, layer, side_low_ref, side_high_ref)
                send_edges(tiles, band, layer, edge_ref.at[0], edge_ref.at[1])
        if last:
            for place in range(125, 128):
                whole_ref[place // 32, band, place % 32] = jnp.zeros((8, 128), F32)
        else:
            clear_edges(band, edge_ref.at[0], edge_ref.at[1])
        return carry

    lax.fori_loop(0, BANDS, one_band, 0)


def deal(whole_ref, piece_refs):
    for step, piece_ref in enumerate(piece_refs):
        piece_ref[...] = whole_ref[lax.axis_index("band") ^ step]


def collect(piece_refs, whole_ref):
    for step, piece_ref in enumerate(piece_refs):
        whole_ref[lax.axis_index("band") ^ step] = piece_ref[...]


PAIRS = [(a, b) for a in range(GROUPS * BANDS) for b in range(a + 1)]


def overlap_kernel(*refs):
    *piece_refs, whole_ref, sums_ref, row_ref = refs
    collect(piece_refs, whole_ref)

    def accumulate(at, totals):
        cells = [whole_ref[a // BANDS, a % BANDS, at] for a in range(GROUPS * BANDS)]
        return tuple(total + cells[a] * cells[b] for total, (a, b) in zip(totals, PAIRS))

    totals = lax.fori_loop(0, 32, accumulate, tuple(jnp.zeros((8, 128), F32) for _ in PAIRS))
    row_ref[...] = jnp.zeros_like(row_ref)
    for at, total in enumerate(totals):
        row_ref[at : at + 1, :] = jnp.sum(total, axis=0, keepdims=True)
    sums = lax.dot_general(
        jnp.ones((8, 128), F32),
        row_ref[...],
        (((1,), (1,)), ((), ())),
        precision=lax.Precision.HIGHEST,
        preferred_element_type=F32,
    )
    sums_ref[...] = jnp.broadcast_to(sums[0:1].reshape(1, 1, 128), sums_ref.shape)


def rotate_kernel(cell_count, whole_ref, sums_ref, *refs):
    *piece_refs, turned_ref = refs
    count = sums_ref.shape[0] // 8
    parts = [jnp.sum(sums_ref[i * count : (i + 1) * count], axis=0) for i in range(8)]
    while len(parts) > 1:
        parts = [parts[i] + parts[i + 1] for i in range(0, len(parts), 2)]
    row = parts[0] * (1.0 / cell_count)
    extent = GROUPS * BANDS
    matrix = {}
    for at, place in enumerate(PAIRS):
        matrix[place] = jnp.broadcast_to(row[:, at : at + 1], (8, 128))
    factor = {}
    scale = []
    for b in range(extent):
        running = matrix[b, b]
        for s in range(b):
            running = running - factor[b, s] * factor[b, s]
        scale.append(1.0 / jnp.sqrt(running))
        for a in range(b + 1, extent):
            running = matrix[a, b]
            for s in range(b):
                running = running - factor[a, s] * factor[b, s]
            factor[a, b] = running * scale[b]
    inverse = {}
    for target in range(extent):
        inverse[target, target] = scale[target]
        for a in range(target):
            running = factor[target, a] * inverse[a, a]
            for source in range(a + 1, target):
                running = running + factor[target, source] * inverse[source, a]
            inverse[target, a] = -running * scale[target]

    def turn(at, carry):
        cells = [whole_ref[a // BANDS, a % BANDS, at] for a in range(extent)]
        for j in range(extent):
            total = inverse[j, 0] * cells[0]
            for a in range(1, j + 1):
                total = total + inverse[j, a] * cells[a]
            turned_ref[j // BANDS, j % BANDS, at] = total
        return carry

    lax.fori_loop(0, 32, turn, 0)
    deal(turned_ref, piece_refs)


def merge_kernel(*refs):
    *piece_refs, out_ref, whole_ref, stage_ref = refs
    collect(piece_refs, whole_ref)

    def one_band(band, carry):
        for layer in range(LAYERS):
            for v in range(25):
                place = layer * 25 + v
                cell = whole_ref[place // 32, band, place % 32]
                if v < 20:
                    stage_ref[v // 10, pl.ds(v % 10, 8, stride=10), :] = cell
                else:
                    stage_ref[2, pl.ds(v - 20, 8, stride=10), :] = cell
                    stage_ref[2, pl.ds(v - 15, 8, stride=10), :] = pltpu.roll(cell, 64, 1)
            for tile in range(2):
                out_ref[band, layer, :, tile * 128 : tile * 128 + 128] = stage_ref[tile]
            out_ref[band, layer, :, 256:320] = stage_ref[2, :, 0:64]
        return carry

    lax.fori_loop(0, BANDS, one_band, 0)


def swapped(array, axis, partner):
    return lax.ppermute(array, axis, [(i, partner(i)) for i in range(lax.axis_size(axis))])


def beside(array, axis, offset):
    count = lax.axis_size(axis)
    return swapped(array, axis, lambda i: (i + (offset if i % 2 == 0 else -offset)) % count)


def exchange(pieces):
    moved = {step: swapped(pieces[step], "band", lambda i: i ^ step) for step in (2, 1, 3)}
    return [pieces[0], moved[1], moved[2], moved[3]]


def local(band_fields, potential, cutoff, upper_bound):
    devices = lax.axis_size("dx") * lax.axis_size("dy") * lax.axis_size("band")
    cell_count = float(LAYERS * 80 * 320 * lax.axis_size("dx") * lax.axis_size("dy"))
    cutoff = cutoff.reshape(1, 1)
    upper_bound = upper_bound.reshape(1, 1)
    stage = (3, 80, 128)
    edges = (2,) + EDGE
    state, far, near, inner, outer = call(
        split_kernel, (STATE, SIDE, SIDE, EDGE, EDGE), scratch=(stage, edges)
    )(band_fields)
    previous = diagonal = None
    for step in range(4):
        first, last = step == 0, step == 3
        far = beside(far, "dx", -1)
        near = beside(near, "dx", 1)
        inner = beside(inner, "dy", 1)
        outer = beside(outer, "dy", -1)
        wide = (LAYERS, 3, 18, 8, 128)
        if first:
            part, diagonal = call(
                functools.partial(inner_kernel, True), (STATE, STATE[1:]), scratch=(wide, stage)
            )(state, potential, cutoff, upper_bound)
        else:
            (part,) = call(functools.partial(inner_kernel, False), (STATE,), scratch=(wide,))(
                state, previous, diagonal, cutoff, upper_bound
            )
        previous = state
        arguments = (part, far, near, inner, outer, cutoff, upper_bound)
        rim = (BANDS, 2, 4, 16, 128)
        if last:
            pieces = call(
                functools.partial(outer_kernel, first, last),
                (PIECE,) * 4,
                scratch=(rim, (GROUPS,) + PIECE),
            )(*arguments)
        else:
            state, far, near, inner, outer = call(
                functools.partial(outer_kernel, first, last),
                (STATE, SIDE, SIDE, EDGE, EDGE),
                scratch=(rim, edges),
            )(*arguments)
    pieces = exchange(pieces)
    whole, sums = call(overlap_kernel, ((GROUPS,) + PIECE, (devices, 1, 128)), scratch=((128, 128),))(*pieces)
    sums = lax.all_to_all(sums, ("dx", "dy", "band"), 0, 0)
    pieces = call(
        functools.partial(rotate_kernel, cell_count), (PIECE,) * 4, scratch=((GROUPS,) + PIECE,)
    )(whole, sums)
    pieces = exchange(pieces)
    (rotated,) = call(
        merge_kernel, ((BANDS, LAYERS, 80, 320),), scratch=((GROUPS,) + PIECE, stage)
    )(*pieces)
    return rotated


def solution(mesh):
    in_specs = (P("band", "dx", "dy", None), P("dx", "dy", None), P(), P())
    out_specs = P("band", "dx", "dy", None)
    return jax.shard_map(local, mesh=mesh, in_specs=in_specs, out_specs=out_specs, check_vma=False)
```

profile of v0, /device:TPU:1, one launch (start us, length us, event | category | flops | bytes accessed | tf_op | source)
XLA Modules:
  0.0 131.2 jit_solution(13456994837719663386)
XLA Ops:
  1.7 2.7 %collective-permute-start = (f32[2,4,25,8,128]{4,3,2,1,0:T(8,128)S(1)}, f32[2,4,25,8,128]{4,3,2,1,0:T(8,128)S(1)}, u32[]{:S(2)}, u32[]{:S(2)}) collective-permute-start(f32[2,4,25,8,128]{4,3,2,1,0:T(8,128)S(1)} %get-tuple-element.39), channel_id=1, source_target_pairs={{0,240},{16,32},{32,16},{48,64},{64,48},{80,96},{96,80},{112,128},... | collective-permute-start | bytes 2457608 | tf_op jit(solution)/shard_map/ppermute | solution.py:408
  4.4 2.5 %collective-permute-start.1 = (f32[2,4,25,8,128]{4,3,2,1,0:T(8,128)S(1)}, f32[2,4,25,8,128]{4,3,2,1,0:T(8,128)S(1)}, u32[]{:S(2)}, u32[]{:S(2)}) collective-permute-start(f32[2,4,25,8,128]{4,3,2,1,0:T(8,128)S(1)} %get-tuple-element.40), channel_id=1, source_target_pairs={{0,16},{16,0},{32,48},{48,32},{64,80},{80,64},{96,112},{112,96},{1... | collective-permute-start | bytes 2457608 | tf_op jit(solution)/shard_map/ppermute | solution.py:408
  6.8 3.0 %collective-permute-start.2 = (f32[2,64,128]{2,1,0:T(8,128)S(1)}, f32[2,64,128]{2,1,0:T(8,128)S(1)}, u32[]{:S(2)}, u32[]{:S(2)}) collective-permute-start(f32[2,64,128]{2,1,0:T(8,128)S(1)} %get-tuple-element.41), channel_id=1, source_target_pairs={{0,4},{4,0},{8,12},{12,8},{1,5},{5,1},{9,13},{13,9},{2,6},{6,2},{1... | collective-permute-start | bytes 196616 | tf_op jit(solution)/shard_map/ppermute | solution.py:408
  9.8 3.3 %collective-permute-start.3 = (f32[2,64,128]{2,1,0:T(8,128)S(1)}, f32[2,64,128]{2,1,0:T(8,128)S(1)}, u32[]{:S(2)}, u32[]{:S(2)}) collective-permute-start(f32[2,64,128]{2,1,0:T(8,128)S(1)} %get-tuple-element.42), channel_id=1, source_target_pairs={{0,12},{4,8},{8,4},{12,0},{1,13},{5,9},{9,5},{13,1},{2,14},{6,10},... | collective-permute-start | bytes 196616 | tf_op jit(solution)/shard_map/ppermute | solution.py:408
  14.5 5.8 %shard_map.47 = (f32[2,5,3,10,8,128]{5,4,3,2,1,0:T(8,128)S(1)}, f32[5,3,10,8,128]{4,3,2,1,0:T(8,128)S(1)}) custom-call(f32[2,5,3,10,8,128]{5,4,3,2,1,0:T(8,128)S(1)} %get-tuple-element.37.refs_0_.refs_1_, f32[5,80,320]{2,1,0:T(8,128)S(1)} %copy-done.1, f32[1,1]{1,0:T(1,128)} %bitcast.2.refs_2_, f32[1,1]{1,0:T(1,128)} %bitcast.10.refs_3_), custom_call_target="tpu_custom_call" | custom-call | flops 4000000 | bytes 4000000 | tf_op jit(solution)/shard_map/pallas_call | solution.py:440
  21.9 4.5 %collective-permute-start.5 = (f32[2,4,25,8,128]{4,3,2,1,0:T(8,128)S(1)}, f32[2,4,25,8,128]{4,3,2,1,0:T(8,128)S(1)}, u32[]{:S(2)}, u32[]{:S(2)}) collective-permute-start(f32[2,4,25,8,128]{4,3,2,1,0:T(8,128)S(1)} %get-tuple-element.46), channel_id=1, source_target_pairs={{0,16},{16,0},{32,48},{48,32},{64,80},{80,64},{96,112},{112,96},{1... | collective-permute-start | bytes 2457608 | tf_op jit(solution)/shard_map/ppermute | solution.py:408
  27.8 2.2 %collective-permute-start.7 = (f32[2,64,128]{2,1,0:T(8,128)S(1)}, f32[2,64,128]{2,1,0:T(8,128)S(1)}, u32[]{:S(2)}, u32[]{:S(2)}) collective-permute-start(f32[2,64,128]{2,1,0:T(8,128)S(1)} %get-tuple-element.48), channel_id=1, source_target_pairs={{0,12},{4,8},{8,4},{12,0},{1,13},{5,9},{9,5},{13,1},{2,14},{6,10},... | collective-permute-start | bytes 196616 | tf_op jit(solution)/shard_map/ppermute | solution.py:408
  30.0 5.8 %shard_map.49.refs_0_ = f32[2,5,3,10,8,128]{5,4,3,2,1,0:T(8,128)S(1)} custom-call(f32[2,5,3,10,8,128]{5,4,3,2,1,0:T(8,128)S(1)} %get-tuple-element.43.refs_0_.refs_1_, f32[2,5,3,10,8,128]{5,4,3,2,1,0:T(8,128)S(1)} %get-tuple-element.37.refs_0_.refs_1_, f32[5,3,10,8,128]{4,3,2,1,0:T(8,128)S(1)} %get-tuple-element.44.refs_2_, f32[1,1]{1,0:T(1,128)} %bitcast.4.refs_3_, ...), custom_call_target="tpu_custom_call" | custom-call | flops 4000000 | bytes 4000000 | tf_op jit(solution)/shard_map/pallas_call | solution.py:444
  36.8 6.4 %collective-permute-start.9 = (f32[2,4,25,8,128]{4,3,2,1,0:T(8,128)S(1)}, f32[2,4,25,8,128]{4,3,2,1,0:T(8,128)S(1)}, u32[]{:S(2)}, u32[]{:S(2)}) collective-permute-start(f32[2,4,25,8,128]{4,3,2,1,0:T(8,128)S(1)} %get-tuple-element.51), channel_id=1, source_target_pairs={{0,16},{16,0},{32,48},{48,32},{64,80},{80,64},{96,112},{112,96},{1... | collective-permute-start | bytes 2457608 | tf_op jit(solution)/shard_map/ppermute | solution.py:408
  43.2 1.8 %collective-permute-start.10 = (f32[2,64,128]{2,1,0:T(8,128)S(1)}, f32[2,64,128]{2,1,0:T(8,128)S(1)}, u32[]{:S(2)}, u32[]{:S(2)}) collective-permute-start(f32[2,64,128]{2,1,0:T(8,128)S(1)} %get-tuple-element.52), channel_id=1, source_target_pairs={{0,4},{4,0},{8,12},{12,8},{1,5},{5,1},{9,13},{13,9},{2,6},{6,2},{1... | collective-permute-start | bytes 196616 | tf_op jit(solution)/shard_map/ppermute | solution.py:408
  45.0 2.1 %collective-permute-start.11 = (f32[2,64,128]{2,1,0:T(8,128)S(1)}, f32[2,64,128]{2,1,0:T(8,128)S(1)}, u32[]{:S(2)}, u32[]{:S(2)}) collective-permute-start(f32[2,64,128]{2,1,0:T(8,128)S(1)} %get-tuple-element.53), channel_id=1, source_target_pairs={{0,12},{4,8},{8,4},{12,0},{1,13},{5,9},{9,5},{13,1},{2,14},{6,10},... | collective-permute-start | bytes 196616 | tf_op jit(solution)/shard_map/ppermute | solution.py:408
  47.1 5.8 %shard_map.51.refs_0_ = f32[2,5,3,10,8,128]{5,4,3,2,1,0:T(8,128)S(1)} custom-call(f32[2,5,3,10,8,128]{5,4,3,2,1,0:T(8,128)S(1)} %get-tuple-element.49.refs_0_.refs_1_, f32[2,5,3,10,8,128]{5,4,3,2,1,0:T(8,128)S(1)} %get-tuple-element.43.refs_0_.refs_1_, f32[5,3,10,8,128]{4,3,2,1,0:T(8,128)S(1)} %get-tuple-element.44.refs_2_, f32[1,1]{1,0:T(1,128)} %bitcast.6.refs_3_, ...), custom_call_target="tpu_custom_call" | custom-call | flops 4000000 | bytes 4000000 | tf_op jit(solution)/shard_map/pallas_call | solution.py:444
  53.9 7.6 %collective-permute-start.13 = (f32[2,4,25,8,128]{4,3,2,1,0:T(8,128)S(1)}, f32[2,4,25,8,128]{4,3,2,1,0:T(8,128)S(1)}, u32[]{:S(2)}, u32[]{:S(2)}) collective-permute-start(f32[2,4,25,8,128]{4,3,2,1,0:T(8,128)S(1)} %get-tuple-element.56), channel_id=1, source_target_pairs={{0,16},{16,0},{32,48},{48,32},{64,80},{80,64},{96,112},{112,96},{1... | collective-permute-start | bytes 2457608 | tf_op jit(solution)/shard_map/ppermute | solution.py:408
  64.0 5.8 %shard_map.53.refs_0_ = f32[2,5,3,10,8,128]{5,4,3,2,1,0:T(8,128)S(1)} custom-call(f32[2,5,3,10,8,128]{5,4,3,2,1,0:T(8,128)S(1)} %get-tuple-element.54.refs_0_, f32[2,5,3,10,8,128]{5,4,3,2,1,0:T(8,128)S(1)} %get-tuple-element.49.refs_0_.refs_1_, f32[5,3,10,8,128]{4,3,2,1,0:T(8,128)S(1)} %get-tuple-element.44.refs_2_, f32[1,1]{1,0:T(1,128)} %bitcast.8.refs_3_, ...), custom_call_target="tpu_custom_call" | custom-call | flops 4000000 | bytes 4000000 | tf_op jit(solution)/shard_map/pallas_call | solution.py:444
  72.1 2.6 %collective-permute-start.17 = (f32[2,32,8,128]{3,2,1,0:T(8,128)S(1)}, f32[2,32,8,128]{3,2,1,0:T(8,128)S(1)}, u32[]{:S(2)}, u32[]{:S(2)}) collective-permute-start(f32[2,32,8,128]{3,2,1,0:T(8,128)S(1)} %get-tuple-element.61), channel_id=1, source_target_pairs={{0,2},{1,3},{2,0},{3,1},{4,6},{5,7},{6,4},{7,5},{8,10},{9,11},{10,... | collective-permute-start | bytes 786440 | tf_op jit(solution)/shard_map/ppermute | solution.py:408
  74.8 1.6 %collective-permute-done.16.refs_1_ = f32[2,32,8,128]{3,2,1,0:T(8,128)S(1)} collective-permute-done((f32[2,32,8,128]{3,2,1,0:T(8,128)S(1)}, f32[2,32,8,128]{3,2,1,0:T(8,128)S(1)}, u32[]{:S(2)}, u32[]{:S(2)}) %collective-permute-start.16) | collective-permute-done | bytes 262176 | tf_op jit(solution)/shard_map/ppermute | solution.py:408
  76.4 5.1 %collective-permute-done.17.refs_2_ = f32[2,32,8,128]{3,2,1,0:T(8,128)S(1)} collective-permute-done((f32[2,32,8,128]{3,2,1,0:T(8,128)S(1)}, f32[2,32,8,128]{3,2,1,0:T(8,128)S(1)}, u32[]{:S(2)}, u32[]{:S(2)}) %collective-permute-start.17) | collective-permute-done | bytes 262176 | tf_op jit(solution)/shard_map/ppermute | solution.py:408
  81.4 2.6 %collective-permute-done.18.refs_3_ = f32[2,32,8,128]{3,2,1,0:T(8,128)S(1)} collective-permute-done((f32[2,32,8,128]{3,2,1,0:T(8,128)S(1)}, f32[2,32,8,128]{3,2,1,0:T(8,128)S(1)}, u32[]{:S(2)}, u32[]{:S(2)}) %collective-permute-start.18) | collective-permute-done | bytes 262176 | tf_op jit(solution)/shard_map/ppermute | solution.py:408
  85.0 28.1 %all_to_all.5.sums_ref = f32[256,1,128]{2,1,0:T(1,128)S(1)} all-to-all(f32[256,1,128]{2,1,0:T(1,128)S(1)} %get-tuple-element.64), channel_id=1, replica_groups=mesh['dx'=16,'dy'=4,'band'=4] {'dx','dy','band'}, dimensions={0} | all-to-all | bytes 262144 | tf_op jit(solution)/shard_map/all_to_all | solution.py:464
  114.5 1.9 %collective-permute-start.20 = (f32[2,32,8,128]{3,2,1,0:T(8,128)S(1)}, f32[2,32,8,128]{3,2,1,0:T(8,128)S(1)}, u32[]{:S(2)}, u32[]{:S(2)}) collective-permute-start(f32[2,32,8,128]{3,2,1,0:T(8,128)S(1)} %get-tuple-element.67), channel_id=1, source_target_pairs={{0,2},{1,3},{2,0},{3,1},{4,6},{5,7},{6,4},{7,5},{8,10},{9,11},{10,... | collective-permute-start | bytes 786440 | tf_op jit(solution)/shard_map/ppermute | solution.py:408
  116.3 1.6 %collective-permute-start.21 = (f32[2,32,8,128]{3,2,1,0:T(8,128)S(1)}, f32[2,32,8,128]{3,2,1,0:T(8,128)S(1)}, u32[]{:S(2)}, u32[]{:S(2)}) collective-permute-start(f32[2,32,8,128]{3,2,1,0:T(8,128)S(1)} %get-tuple-element.68), channel_id=1, source_target_pairs={{0,3},{1,2},{2,1},{3,0},{4,7},{5,6},{6,5},{7,4},{8,11},{9,10},{10,... | collective-permute-start | bytes 786440 | tf_op jit(solution)/shard_map/ppermute | solution.py:408
  117.9 3.7 %collective-permute-done.19.refs_1_ = f32[2,32,8,128]{3,2,1,0:T(8,128)S(1)} collective-permute-done((f32[2,32,8,128]{3,2,1,0:T(8,128)S(1)}, f32[2,32,8,128]{3,2,1,0:T(8,128)S(1)}, u32[]{:S(2)}, u32[]{:S(2)}) %collective-permute-start.19) | collective-permute-done | bytes 262176 | tf_op jit(solution)/shard_map/ppermute | solution.py:408
  121.6 6.2 %collective-permute-done.20.refs_2_ = f32[2,32,8,128]{3,2,1,0:T(8,128)S(1)} collective-permute-done((f32[2,32,8,128]{3,2,1,0:T(8,128)S(1)}, f32[2,32,8,128]{3,2,1,0:T(8,128)S(1)}, u32[]{:S(2)}, u32[]{:S(2)}) %collective-permute-start.20) | collective-permute-done | bytes 262176 | tf_op jit(solution)/shard_map/ppermute | solution.py:408
  127.8 2.0 %collective-permute-done.21.refs_3_ = f32[2,32,8,128]{3,2,1,0:T(8,128)S(1)} collective-permute-done((f32[2,32,8,128]{3,2,1,0:T(8,128)S(1)}, f32[2,32,8,128]{3,2,1,0:T(8,128)S(1)}, u32[]{:S(2)}, u32[]{:S(2)}) %collective-permute-start.21) | collective-permute-done | bytes 262176 | tf_op jit(solution)/shard_map/ppermute | solution.py:408
  (37 shorter events, 14.9 us)
Async XLA Ops:
  0.0 1.3 copy-start
  1.3 13.2 %copy-start.1 = (f32[5,80,320]{2,1,0:T(8,128)S(1)}, f32[5,80,320]{2,1,0:T(8,128)}, u32[]{:S(2)}) copy-start(f32[5,80,320]{2,1,0:T(8,128)} %refs_1_.1) | copy-start | bytes 1536004
  1.7 18.6 %collective-permute-start = (f32[2,4,25,8,128]{4,3,2,1,0:T(8,128)S(1)}, f32[2,4,25,8,128]{4,3,2,1,0:T(8,128)S(1)}, u32[]{:S(2)}, u32[]{:S(2)}) collective-permute-start(f32[2,4,25,8,128]{4,3,2,1,0:T(8,128)S(1)} %get-tuple-element.39), channel_id=1, source_target_pairs={{0,240},{16,32},{32,16},{48,64},{64,48},{80,96},{96,80},{112,128},... | collective-permute-start | bytes 2457608 | tf_op jit(solution)/shard_map/ppermute | solution.py:408
  4.4 15.9 %collective-permute-start.1 = (f32[2,4,25,8,128]{4,3,2,1,0:T(8,128)S(1)}, f32[2,4,25,8,128]{4,3,2,1,0:T(8,128)S(1)}, u32[]{:S(2)}, u32[]{:S(2)}) collective-permute-start(f32[2,4,25,8,128]{4,3,2,1,0:T(8,128)S(1)} %get-tuple-element.40), channel_id=1, source_target_pairs={{0,16},{16,0},{32,48},{48,32},{64,80},{80,64},{96,112},{112,96},{1... | collective-permute-start | bytes 2457608 | tf_op jit(solution)/shard_map/ppermute | solution.py:408
  6.8 13.4 %collective-permute-start.2 = (f32[2,64,128]{2,1,0:T(8,128)S(1)}, f32[2,64,128]{2,1,0:T(8,128)S(1)}, u32[]{:S(2)}, u32[]{:S(2)}) collective-permute-start(f32[2,64,128]{2,1,0:T(8,128)S(1)} %get-tuple-element.41), channel_id=1, source_target_pairs={{0,4},{4,0},{8,12},{12,8},{1,5},{5,1},{9,13},{13,9},{2,6},{6,2},{1... | collective-permute-start | bytes 196616 | tf_op jit(solution)/shard_map/ppermute | solution.py:408
  9.8 10.5 %collective-permute-start.3 = (f32[2,64,128]{2,1,0:T(8,128)S(1)}, f32[2,64,128]{2,1,0:T(8,128)S(1)}, u32[]{:S(2)}, u32[]{:S(2)}) collective-permute-start(f32[2,64,128]{2,1,0:T(8,128)S(1)} %get-tuple-element.42), channel_id=1, source_target_pairs={{0,12},{4,8},{8,4},{12,0},{1,13},{5,9},{9,5},{13,1},{2,14},{6,10},... | collective-permute-start | bytes 196616 | tf_op jit(solution)/shard_map/ppermute | solution.py:408
  21.2 14.7 %collective-permute-start.4 = (f32[2,4,25,8,128]{4,3,2,1,0:T(8,128)S(1)}, f32[2,4,25,8,128]{4,3,2,1,0:T(8,128)S(1)}, u32[]{:S(2)}, u32[]{:S(2)}) collective-permute-start(f32[2,4,25,8,128]{4,3,2,1,0:T(8,128)S(1)} %get-tuple-element.45), channel_id=1, source_target_pairs={{0,240},{16,32},{32,16},{48,64},{64,48},{80,96},{96,80},{112,128},... | collective-permute-start | bytes 2457608 | tf_op jit(solution)/shard_map/ppermute | solution.py:408
  21.9 14.1 %collective-permute-start.5 = (f32[2,4,25,8,128]{4,3,2,1,0:T(8,128)S(1)}, f32[2,4,25,8,128]{4,3,2,1,0:T(8,128)S(1)}, u32[]{:S(2)}, u32[]{:S(2)}) collective-permute-start(f32[2,4,25,8,128]{4,3,2,1,0:T(8,128)S(1)} %get-tuple-element.46), channel_id=1, source_target_pairs={{0,16},{16,0},{32,48},{48,32},{64,80},{80,64},{96,112},{112,96},{1... | collective-permute-start | bytes 2457608 | tf_op jit(solution)/shard_map/ppermute | solution.py:408
  26.4 9.5 %collective-permute-start.6 = (f32[2,64,128]{2,1,0:T(8,128)S(1)}, f32[2,64,128]{2,1,0:T(8,128)S(1)}, u32[]{:S(2)}, u32[]{:S(2)}) collective-permute-start(f32[2,64,128]{2,1,0:T(8,128)S(1)} %get-tuple-element.47), channel_id=1, source_target_pairs={{0,4},{4,0},{8,12},{12,8},{1,5},{5,1},{9,13},{13,9},{2,6},{6,2},{1... | collective-permute-start | bytes 196616 | tf_op jit(solution)/shard_map/ppermute | solution.py:408
  27.8 8.1 %collective-permute-start.7 = (f32[2,64,128]{2,1,0:T(8,128)S(1)}, f32[2,64,128]{2,1,0:T(8,128)S(1)}, u32[]{:S(2)}, u32[]{:S(2)}) collective-permute-start(f32[2,64,128]{2,1,0:T(8,128)S(1)} %get-tuple-element.48), channel_id=1, source_target_pairs={{0,12},{4,8},{8,4},{12,0},{1,13},{5,9},{9,5},{13,1},{2,14},{6,10},... | collective-permute-start | bytes 196616 | tf_op jit(solution)/shard_map/ppermute | solution.py:408
  36.7 16.3 %collective-permute-start.8 = (f32[2,4,25,8,128]{4,3,2,1,0:T(8,128)S(1)}, f32[2,4,25,8,128]{4,3,2,1,0:T(8,128)S(1)}, u32[]{:S(2)}, u32[]{:S(2)}) collective-permute-start(f32[2,4,25,8,128]{4,3,2,1,0:T(8,128)S(1)} %get-tuple-element.50), channel_id=1, source_target_pairs={{0,240},{16,32},{32,16},{48,64},{64,48},{80,96},{96,80},{112,128},... | collective-permute-start | bytes 2457608 | tf_op jit(solution)/shard_map/ppermute | solution.py:408
  36.8 16.2 %collective-permute-start.9 = (f32[2,4,25,8,128]{4,3,2,1,0:T(8,128)S(1)}, f32[2,4,25,8,128]{4,3,2,1,0:T(8,128)S(1)}, u32[]{:S(2)}, u32[]{:S(2)}) collective-permute-start(f32[2,4,25,8,128]{4,3,2,1,0:T(8,128)S(1)} %get-tuple-element.51), channel_id=1, source_target_pairs={{0,16},{16,0},{32,48},{48,32},{64,80},{80,64},{96,112},{112,96},{1... | collective-permute-start | bytes 2457608 | tf_op jit(solution)/shard_map/ppermute | solution.py:408
  43.2 9.7 %collective-permute-start.10 = (f32[2,64,128]{2,1,0:T(8,128)S(1)}, f32[2,64,128]{2,1,0:T(8,128)S(1)}, u32[]{:S(2)}, u32[]{:S(2)}) collective-permute-start(f32[2,64,128]{2,1,0:T(8,128)S(1)} %get-tuple-element.52), channel_id=1, source_target_pairs={{0,4},{4,0},{8,12},{12,8},{1,5},{5,1},{9,13},{13,9},{2,6},{6,2},{1... | collective-permute-start | bytes 196616 | tf_op jit(solution)/shard_map/ppermute | solution.py:408
  45.0 8.0 %collective-permute-start.11 = (f32[2,64,128]{2,1,0:T(8,128)S(1)}, f32[2,64,128]{2,1,0:T(8,128)S(1)}, u32[]{:S(2)}, u32[]{:S(2)}) collective-permute-start(f32[2,64,128]{2,1,0:T(8,128)S(1)} %get-tuple-element.53), channel_id=1, source_target_pairs={{0,12},{4,8},{8,4},{12,0},{1,13},{5,9},{9,5},{13,1},{2,14},{6,10},... | collective-permute-start | bytes 196616 | tf_op jit(solution)/shard_map/ppermute | solution.py:408
  53.8 16.0 %collective-permute-start.12 = (f32[2,4,25,8,128]{4,3,2,1,0:T(8,128)S(1)}, f32[2,4,25,8,128]{4,3,2,1,0:T(8,128)S(1)}, u32[]{:S(2)}, u32[]{:S(2)}) collective-permute-start(f32[2,4,25,8,128]{4,3,2,1,0:T(8,128)S(1)} %get-tuple-element.55), channel_id=1, source_target_pairs={{0,240},{16,32},{32,16},{48,64},{64,48},{80,96},{96,80},{112,128},... | collective-permute-start | bytes 2457608 | tf_op jit(solution)/shard_map/ppermute | solution.py:408
  53.9 16.0 %collective-permute-start.13 = (f32[2,4,25,8,128]{4,3,2,1,0:T(8,128)S(1)}, f32[2,4,25,8,128]{4,3,2,1,0:T(8,128)S(1)}, u32[]{:S(2)}, u32[]{:S(2)}) collective-permute-start(f32[2,4,25,8,128]{4,3,2,1,0:T(8,128)S(1)} %get-tuple-element.56), channel_id=1, source_target_pairs={{0,16},{16,0},{32,48},{48,32},{64,80},{80,64},{96,112},{112,96},{1... | collective-permute-start | bytes 2457608 | tf_op jit(solution)/shard_map/ppermute | solution.py:408
  61.5 8.3 %collective-permute-start.14 = (f32[2,64,128]{2,1,0:T(8,128)S(1)}, f32[2,64,128]{2,1,0:T(8,128)S(1)}, u32[]{:S(2)}, u32[]{:S(2)}) collective-permute-start(f32[2,64,128]{2,1,0:T(8,128)S(1)} %get-tuple-element.57), channel_id=1, source_target_pairs={{0,4},{4,0},{8,12},{12,8},{1,5},{5,1},{9,13},{13,9},{2,6},{6,2},{1... | collective-permute-start | bytes 196616 | tf_op jit(solution)/shard_map/ppermute | solution.py:408
  62.9 6.9 %collective-permute-start.15 = (f32[2,64,128]{2,1,0:T(8,128)S(1)}, f32[2,64,128]{2,1,0:T(8,128)S(1)}, u32[]{:S(2)}, u32[]{:S(2)}) collective-permute-start(f32[2,64,128]{2,1,0:T(8,128)S(1)} %get-tuple-element.58), channel_id=1, source_target_pairs={{0,12},{4,8},{8,4},{12,0},{1,13},{5,9},{9,5},{13,1},{2,14},{6,10},... | collective-permute-start | bytes 196616 | tf_op jit(solution)/shard_map/ppermute | solution.py:408
  70.8 5.6 %collective-permute-start.16 = (f32[2,32,8,128]{3,2,1,0:T(8,128)S(1)}, f32[2,32,8,128]{3,2,1,0:T(8,128)S(1)}, u32[]{:S(2)}, u32[]{:S(2)}) collective-permute-start(f32[2,32,8,128]{3,2,1,0:T(8,128)S(1)} %get-tuple-element.60), channel_id=1, source_target_pairs={{0,1},{1,0},{2,3},{3,2},{4,5},{5,4},{6,7},{7,6},{8,9},{9,8},{10,11... | collective-permute-start | bytes 786440 | tf_op jit(solution)/shard_map/ppermute | solution.py:408
  72.1 9.3 %collective-permute-start.17 = (f32[2,32,8,128]{3,2,1,0:T(8,128)S(1)}, f32[2,32,8,128]{3,2,1,0:T(8,128)S(1)}, u32[]{:S(2)}, u32[]{:S(2)}) collective-permute-start(f32[2,32,8,128]{3,2,1,0:T(8,128)S(1)} %get-tuple-element.61), channel_id=1, source_target_pairs={{0,2},{1,3},{2,0},{3,1},{4,6},{5,7},{6,4},{7,5},{8,10},{9,11},{10,... | collective-permute-start | bytes 786440 | tf_op jit(solution)/shard_map/ppermute | solution.py:408
  74.8 9.2 %collective-permute-start.18 = (f32[2,32,8,128]{3,2,1,0:T(8,128)S(1)}, f32[2,32,8,128]{3,2,1,0:T(8,128)S(1)}, u32[]{:S(2)}, u32[]{:S(2)}) collective-permute-start(f32[2,32,8,128]{3,2,1,0:T(8,128)S(1)} %get-tuple-element.62), channel_id=1, source_target_pairs={{0,3},{1,2},{2,1},{3,0},{4,7},{5,6},{6,5},{7,4},{8,11},{9,10},{10,... | collective-permute-start | bytes 786440 | tf_op jit(solution)/shard_map/ppermute | solution.py:408
  114.0 7.6 %collective-permute-start.19 = (f32[2,32,8,128]{3,2,1,0:T(8,128)S(1)}, f32[2,32,8,128]{3,2,1,0:T(8,128)S(1)}, u32[]{:S(2)}, u32[]{:S(2)}) collective-permute-start(f32[2,32,8,128]{3,2,1,0:T(8,128)S(1)} %get-tuple-element.66), channel_id=1, source_target_pairs={{0,1},{1,0},{2,3},{3,2},{4,5},{5,4},{6,7},{7,6},{8,9},{9,8},{10,11... | collective-permute-start | bytes 786440 | tf_op jit(solution)/shard_map/ppermute | solution.py:408
  114.5 13.4 %collective-permute-start.20 = (f32[2,32,8,128]{3,2,1,0:T(8,128)S(1)}, f32[2,32,8,128]{3,2,1,0:T(8,128)S(1)}, u32[]{:S(2)}, u32[]{:S(2)}) collective-permute-start(f32[2,32,8,128]{3,2,1,0:T(8,128)S(1)} %get-tuple-element.67), channel_id=1, source_target_pairs={{0,2},{1,3},{2,0},{3,1},{4,6},{5,7},{6,4},{7,5},{8,10},{9,11},{10,... | collective-permute-start | bytes 786440 | tf_op jit(solution)/shard_map/ppermute | solution.py:408
  116.3 13.5 %collective-permute-start.21 = (f32[2,32,8,128]{3,2,1,0:T(8,128)S(1)}, f32[2,32,8,128]{3,2,1,0:T(8,128)S(1)}, u32[]{:S(2)}, u32[]{:S(2)}) collective-permute-start(f32[2,32,8,128]{3,2,1,0:T(8,128)S(1)} %get-tuple-element.68), channel_id=1, source_target_pairs={{0,3},{1,2},{2,1},{3,0},{4,7},{5,6},{6,5},{7,4},{8,11},{9,10},{10,... | collective-permute-start | bytes 786440 | tf_op jit(solution)/shard_map/ppermute | solution.py:408
where the time goes:
time: 131 us
  starting transfers between devices  48.8 us (37%)
  Pallas kernels  30.3 us (23%)
  blocking collectives  28.1 us (21%)
  waiting for transfers between devices  21.2 us (16%)
  between operations  1.55 us (1%)
    ppermute x22, starting transfers between devices, swapped(): lax.ppermute(array, axis, [(i, partner(i)) for i in range(lax.axis_size(a...  48.8 us
    all_to_all x1, blocking collectives, local(): sums = lax.all_to_all(sums, ('dx', 'dy', 'band'), 0, 0)  28.1 us
    ppermute x22, waiting for transfers between devices, swapped(): lax.ppermute(array, axis, [(i, partner(i)) for i in range(lax.axis_size(a...  21.2 us
    pallas_call x3, Pallas kernels, local(): call(functools.partial(inner_kernel, False), (STATE,), scratch=(wide,))  17.5 us
    pallas_call x1, Pallas kernels, local(): call(functools.partial(inner_kernel, True), (STATE, STATE[1:]), scratch=(...  5.83 us
  transfers between devices with their start and end apart: 22, of which 6 were waited for; matrix products, arithmetic and copies ran while one was open for 0% of the time, Pallas kernels for 18%

commit v1 on v0

--- a/solution.py
+++ b/solution.py
@@ -21,14 +21,16 @@
 PIECE = (BANDS, 32, 8, 128)
 
 
-def call(kernel, outs, scratch=(), in_specs=None, cost=4_000_000):
-    kwargs = {} if in_specs is None else {"in_specs": in_specs}
+def call(kernel, outs, scratch=(), semaphores=0, **kwargs):
+    scratch = [pltpu.VMEM(shape, F32) for shape in scratch]
+    if semaphores:
+        scratch.append(pltpu.SemaphoreType.DMA((semaphores,)))
     return pl.pallas_call(
         kernel,
         out_shape=tuple(jax.ShapeDtypeStruct(shape, F32) for shape in outs),
-        scratch_shapes=[pltpu.VMEM(shape, F32) for shape in scratch],
+        scratch_shapes=scratch,
         compiler_params=pltpu.CompilerParams(vmem_limit_bytes=16 * 1024 * 1024),
-        cost_estimate=pl.CostEstimate(flops=cost, bytes_accessed=4_000_000, transcendentals=0),
+        cost_estimate=pl.CostEstimate(flops=4_000_000, bytes_accessed=4_000_000, transcendentals=0),
         **kwargs,
     )
 
@@ -145,69 +147,66 @@
     lane = lanes()
     row = sublanes()
 
-    def one_band(band, carry):
-        def widen(j, carry):
+    def plane(at, carry):
+        band, layer = at // LAYERS, lax.rem(at, LAYERS)
+        for j in range(10):
+            tiles = [state_ref[band, layer, tile, j] for tile in range(3)]
+            tiles[2] = jnp.where(
+                lane < 64, tiles[2], jnp.where(lane < 96, pltpu.roll(tiles[0], 64, 1), pltpu.roll(tiles[2], 64, 1))
+            )
+            for tile in range(3):
+                wide_ref[tile, j] = tiles[tile]
+        for tile in range(3):
+            ext = [wide_ref[tile, j] for j in range(10)]
+            below = [jnp.where(row > 0, pltpu.roll(cells, 1, 0), 0.0) for cells in ext[6:]]
+            above = [jnp.where(row < 7, pltpu.roll(cells, 7, 0), 0.0) for cells in ext[:4]]
+            ext = below + ext + above
+            for j in range(10):
+                total = None
+                for k in range(1, 5):
+                    part = weights[k] * (ext[j + 4 + k] + ext[j + 4 - k])
+                    total = part if total is None else total + part
+                out_ref[band, layer, tile, j] = total
+        for j in range(10):
+            mid = [wide_ref[tile, j] for tile in range(3)]
+            lefts = [pltpu.roll(cells, 1, 1) for cells in mid]
+            lefts = [jnp.where(lane < 1, lefts[(tile + 2) % 3], lefts[tile]) for tile in range(3)]
+            rights = [pltpu.roll(cells, 127, 1) for cells in mid]
+            rights = [jnp.where(lane < 127, rights[tile], rights[(tile + 1) % 3]) for tile in range(3)]
+            ups, downs = [], []
+            for tile in range(3):
+                centre = weights[3] * mid[tile]
+                ups.append(centre + weights[2] * lefts[tile] + weights[4] * rights[tile])
+                downs.append(centre + weights[4] * lefts[tile] + weights[2] * rights[tile])
+            ups = [pltpu.roll(up, 125, 1) for up in ups]
+            downs = [pltpu.roll(down, 3, 1) for down in downs]
+            for tile in range(3):
+                up = ups[2] if tile == 2 else jnp.where(lane < 125, ups[tile], ups[tile + 1])
+                total = up + jnp.where(lane < 3, downs[(tile + 2) % 3], downs[tile])
+                total += weights[1] * (lefts[tile] + rights[tile])
+                out_ref[band, layer, tile, j] += total
+        return carry
+
+    lax.fori_loop(0, BANDS * LAYERS, plane, 0)
+
+    def column(at, carry):
+        band, j = at // 10, lax.rem(at, 10)
+        for tile in range(3):
+            mids = [state_ref[band, layer, tile, j] for layer in range(LAYERS)]
             for layer in range(LAYERS):
-                tiles = [state_ref[band, layer, tile, j] for tile in range(3)]
-                tiles[2] = jnp.where(
-                    lane < 64,
-                    tiles[2],
-                    jnp.where(lane < 96, pltpu.roll(tiles[0], 64, 1), pltpu.roll(tiles[2], 64, 1)),
-                )
-                for tile in range(3):
-                    wide_ref[layer, tile, j + 4] = tiles[tile]
-            return carry
-
-        lax.fori_loop(0, 10, widen, 0)
-
-        def wrap(j, carry):
-            for layer in range(LAYERS):
-                for tile in range(3):
-                    above = wide_ref[layer, tile, j + 4]
-                    wide_ref[layer, tile, j + 14] = jnp.where(row < 7, pltpu.roll(above, 7, 0), 0.0)
-                    below = wide_ref[layer, tile, j + 10]
-                    wide_ref[layer, tile, j] = jnp.where(row > 0, pltpu.roll(below, 1, 0), 0.0)
-            return carry
-
-        lax.fori_loop(0, 4, wrap, 0)
-
-        def rows(j, carry):
-            mids = [[wide_ref[layer, tile, j + 4] for tile in range(3)] for layer in range(LAYERS)]
-            for layer in range(LAYERS):
-                mid = mids[layer]
-                lefts = [pltpu.roll(mid[tile], 1, 1) for tile in range(3)]
-                lefts = [jnp.where(lane < 1, lefts[(tile + 2) % 3], lefts[tile]) for tile in range(3)]
-                rights = [pltpu.roll(mid[tile], 127, 1) for tile in range(3)]
-                rights = [jnp.where(lane < 127, rights[tile], rights[(tile + 1) % 3]) for tile in range(3)]
-                ups, downs = [], []
-                for tile in range(3):
-                    centre = weights[3] * mid[tile]
-                    ups.append(centre + weights[2] * lefts[tile] + weights[4] * rights[tile])
-                    downs.append(centre + weights[4] * lefts[tile] + weights[2] * rights[tile])
-                ups = [pltpu.roll(up, 125, 1) for up in ups]
-                downs = [pltpu.roll(down, 3, 1) for down in downs]
-                for tile in range(3):
-                    up = ups[2] if tile == 2 else jnp.where(lane < 125, ups[tile], ups[tile + 1])
-                    total = up + jnp.where(lane < 3, downs[(tile + 2) % 3], downs[tile])
-                    for k in range(1, 5):
-                        part = wide_ref[layer, tile, j + 4 + k] + wide_ref[layer, tile, j + 4 - k]
-                        if k == 1:
-                            part += lefts[tile] + rights[tile]
-                        if layer + k < LAYERS:
-                            part += mids[layer + k][tile]
-                        if layer - k >= 0:
-                            part += mids[layer - k][tile]
-                        total += weights[k] * part
-                    diagonal = diagonal_ref[layer, tile, j] * mid[tile]
-                    if first:
-                        out_ref[band, layer, tile, j] = total + 0.5 * diagonal
-                    else:
-                        out_ref[band, layer, tile, j] = total + (diagonal - previous_ref[band, layer, tile, j])
-            return carry
-
-        return lax.fori_loop(0, 10, rows, carry)
-
-    lax.fori_loop(0, BANDS, one_band, 0)
+                total = out_ref[band, layer, tile, j]
+                for k in range(1, 5):
+                    near = [mids[at] for at in (layer - k, layer + k) if 0 <= at < LAYERS]
+                    if near:
+                        total += weights[k] * sum(near[1:], near[0])
+                diagonal = diagonal_ref[layer, tile, j] * mids[layer]
+                if first:
+                    out_ref[band, layer, tile, j] = total + 0.5 * diagonal
+                else:
+                    out_ref[band, layer, tile, j] = total + (diagonal - previous_ref[band, layer, tile, j])
+        return carry
+
+    lax.fori_loop(0, BANDS * 10, column, 0)
 
 
 def outer_kernel(first, last, *refs):
@@ -383,25 +382,28 @@
 
 
 def merge_kernel(*refs):
-    *piece_refs, out_ref, whole_ref, stage_ref = refs
+    *piece_refs, out_ref, whole_ref, stage_ref, plane_ref, sems = refs
     collect(piece_refs, whole_ref)
 
-    def one_band(band, carry):
-        for layer in range(LAYERS):
-            for v in range(25):
-                place = layer * 25 + v
-                cell = whole_ref[place // 32, band, place % 32]
-                if v < 20:
-                    stage_ref[v // 10, pl.ds(v % 10, 8, stride=10), :] = cell
-                else:
-                    stage_ref[2, pl.ds(v - 20, 8, stride=10), :] = cell
-                    stage_ref[2, pl.ds(v - 15, 8, stride=10), :] = pltpu.roll(cell, 64, 1)
-            for tile in range(2):
-                out_ref[band, layer, :, tile * 128 : tile * 128 + 128] = stage_ref[tile]
-            out_ref[band, layer, :, 256:320] = stage_ref[2, :, 0:64]
-        return carry
-
-    lax.fori_loop(0, BANDS, one_band, 0)
+    def copy_out(at):
+        return pltpu.make_async_copy(plane_ref.at[at], out_ref.at[at // LAYERS, at % LAYERS], sems.at[at])
+
+    for at in range(BANDS * LAYERS):
+        band, layer = at // LAYERS, at % LAYERS
+        for v in range(25):
+            place = layer * 25 + v
+            cell = whole_ref[place // 32, band, place % 32]
+            if v < 20:
+                stage_ref[v // 10, pl.ds(v % 10, 8, stride=10), :] = cell
+            else:
+                stage_ref[2, pl.ds(v - 20, 8, stride=10), :] = cell
+                stage_ref[2, pl.ds(v - 15, 8, stride=10), :] = pltpu.roll(cell, 64, 1)
+        for tile in range(2):
+            plane_ref[at, :, tile * 128 : tile * 128 + 128] = stage_ref[tile]
+        plane_ref[at, :, 256:320] = stage_ref[2, :, 0:64]
+        copy_out(at).start()
+    for at in range(BANDS * LAYERS):
+        copy_out(at).wait()
 
 
 def swapped(array, axis, partner):
@@ -435,7 +437,7 @@
         near = beside(near, "dx", 1)
         inner = beside(inner, "dy", 1)
         outer = beside(outer, "dy", -1)
-        wide = (LAYERS, 3, 18, 8, 128)
+        wide = (3, 10, 8, 128)
         if first:
             part, diagonal = call(
                 functools.partial(inner_kernel, True), (STATE, STATE[1:]), scratch=(wide, stage)
@@ -466,8 +468,13 @@
         functools.partial(rotate_kernel, cell_count), (PIECE,) * 4, scratch=((GROUPS,) + PIECE,)
     )(whole, sums)
     pieces = exchange(pieces)
+    planes = BANDS * LAYERS
     (rotated,) = call(
-        merge_kernel, ((BANDS, LAYERS, 80, 320),), scratch=((GROUPS,) + PIECE, stage)
+        merge_kernel,
+        ((BANDS, LAYERS, 80, 320),),
+        scratch=((GROUPS,) + PIECE, stage, (planes, 80, 320)),
+        semaphores=planes,
+        out_specs=(pl.BlockSpec(memory_space=pl.ANY),),
     )(*pieces)
     return rotated
 

time: 131 us -> 130 us (level)
  Pallas kernels: 30.3 us -> 22.9 us
  starting transfers between devices: 48.8 us -> 53 us
  waiting for transfers between devices: 21.2 us -> 23.7 us
    pallas_call x3, Pallas kernels: 17.5 us -> 12 us  [local(): call(functools.partial(inner_kernel, False), (STATE,), scratch=(wide,))]
    ppermute x22, starting transfers between devices: 48.8 us -> 53 us  [swapped(): lax.ppermute(array, axis, [(i, partner(i)) for i in range(lax.axis_size(a...]
    ppermute x22, waiting for transfers between devices: 21.2 us -> 23.7 us  [swapped(): lax.ppermute(array, axis, [(i, partner(i)) for i in range(lax.axis_size(a...]
    pallas_call x1, Pallas kernels: 5.83 us -> 4.02 us  [local(): call(functools.partial(inner_kernel, True), (STATE, STATE[1:]), scratch=(...]
  transfers between devices with their start and end apart: 22 -> 22, of which waited for: 6 -> 9; matrix products, arithmetic and copies ran while one was open for 0% -> 0% of each run, Pallas kernels for 18% -> 12%
where the time goes in v1:
time: 130 us
  starting transfers between devices  53 us (41%)
  blocking collectives  27.3 us (21%)
  waiting for transfers between devices  23.7 us (18%)
  Pallas kernels  22.9 us (18%)
  between operations  1.63 us (1%)
    ppermute x22, starting transfers between devices, swapped(): lax.ppermute(array, axis, [(i, partner(i)) for i in range(lax.axis_size(a...  53 us
    all_to_all x1, blocking collectives, local(): sums = lax.all_to_all(sums, ('dx', 'dy', 'band'), 0, 0)  27.3 us
    ppermute x22, waiting for transfers between devices, swapped(): lax.ppermute(array, axis, [(i, partner(i)) for i in range(lax.axis_size(a...  23.7 us
    pallas_call x3, Pallas kernels, local(): call(functools.partial(inner_kernel, False), (STATE,), scratch=(wide,))  12 us
    pallas_call x1, Pallas kernels, local(): call(functools.partial(inner_kernel, True), (STATE, STATE[1:]), scratch=(...  4.02 us
  transfers between devices with their start and end apart: 22, of which 9 were waited for; matrix products, arithmetic and copies ran while one was open for 0% of the time, Pallas kernels for 12%

profile of v1, /device:TPU:1, one launch (start us, length us, event | category | flops | bytes accessed | tf_op | source)
XLA Modules:
  0.0 129.8 jit_solution(9641011797089966767)
XLA Ops:
  1.7 2.7 %collective-permute-start = (f32[2,4,25,8,128]{4,3,2,1,0:T(8,128)S(1)}, f32[2,4,25,8,128]{4,3,2,1,0:T(8,128)S(1)}, u32[]{:S(2)}, u32[]{:S(2)}) collective-permute-start(f32[2,4,25,8,128]{4,3,2,1,0:T(8,128)S(1)} %get-tuple-element.39), channel_id=1, source_target_pairs={{0,240},{16,32},{32,16},{48,64},{64,48},{80,96},{96,80},{112,128},... | collective-permute-start | bytes 2457608 | tf_op jit(solution)/shard_map/ppermute | solution.py:410
  4.4 2.5 %collective-permute-start.1 = (f32[2,4,25,8,128]{4,3,2,1,0:T(8,128)S(1)}, f32[2,4,25,8,128]{4,3,2,1,0:T(8,128)S(1)}, u32[]{:S(2)}, u32[]{:S(2)}) collective-permute-start(f32[2,4,25,8,128]{4,3,2,1,0:T(8,128)S(1)} %get-tuple-element.40), channel_id=1, source_target_pairs={{0,16},{16,0},{32,48},{48,32},{64,80},{80,64},{96,112},{112,96},{1... | collective-permute-start | bytes 2457608 | tf_op jit(solution)/shard_map/ppermute | solution.py:410
  6.8 3.0 %collective-permute-start.2 = (f32[2,64,128]{2,1,0:T(8,128)S(1)}, f32[2,64,128]{2,1,0:T(8,128)S(1)}, u32[]{:S(2)}, u32[]{:S(2)}) collective-permute-start(f32[2,64,128]{2,1,0:T(8,128)S(1)} %get-tuple-element.41), channel_id=1, source_target_pairs={{0,4},{4,0},{8,12},{12,8},{1,5},{5,1},{9,13},{13,9},{2,6},{6,2},{1... | collective-permute-start | bytes 196616 | tf_op jit(solution)/shard_map/ppermute | solution.py:410
  9.8 3.3 %collective-permute-start.3 = (f32[2,64,128]{2,1,0:T(8,128)S(1)}, f32[2,64,128]{2,1,0:T(8,128)S(1)}, u32[]{:S(2)}, u32[]{:S(2)}) collective-permute-start(f32[2,64,128]{2,1,0:T(8,128)S(1)} %get-tuple-element.42), channel_id=1, source_target_pairs={{0,12},{4,8},{8,4},{12,0},{1,13},{5,9},{9,5},{13,1},{2,14},{6,10},... | collective-permute-start | bytes 196616 | tf_op jit(solution)/shard_map/ppermute | solution.py:410
  14.5 4.0 %shard_map.47 = (f32[2,5,3,10,8,128]{5,4,3,2,1,0:T(8,128)S(1)}, f32[5,3,10,8,128]{4,3,2,1,0:T(8,128)S(1)}) custom-call(f32[2,5,3,10,8,128]{5,4,3,2,1,0:T(8,128)S(1)} %get-tuple-element.37.refs_0_.refs_1_, f32[5,80,320]{2,1,0:T(8,128)S(1)} %copy-done.1, f32[1,1]{1,0:T(1,128)} %bitcast.2.refs_2_, f32[1,1]{1,0:T(1,128)} %bitcast.10.refs_3_), custom_call_target="tpu_custom_call" | custom-call | flops 4000000 | bytes 4000000 | tf_op jit(solution)/shard_map/pallas_call | solution.py:442
  20.0 6.3 %collective-permute-start.5 = (f32[2,4,25,8,128]{4,3,2,1,0:T(8,128)S(1)}, f32[2,4,25,8,128]{4,3,2,1,0:T(8,128)S(1)}, u32[]{:S(2)}, u32[]{:S(2)}) collective-permute-start(f32[2,4,25,8,128]{4,3,2,1,0:T(8,128)S(1)} %get-tuple-element.46), channel_id=1, source_target_pairs={{0,16},{16,0},{32,48},{48,32},{64,80},{80,64},{96,112},{112,96},{1... | collective-permute-start | bytes 2457608 | tf_op jit(solution)/shard_map/ppermute | solution.py:410
  27.8 2.2 %collective-permute-start.7 = (f32[2,64,128]{2,1,0:T(8,128)S(1)}, f32[2,64,128]{2,1,0:T(8,128)S(1)}, u32[]{:S(2)}, u32[]{:S(2)}) collective-permute-start(f32[2,64,128]{2,1,0:T(8,128)S(1)} %get-tuple-element.48), channel_id=1, source_target_pairs={{0,12},{4,8},{8,4},{12,0},{1,13},{5,9},{9,5},{13,1},{2,14},{6,10},... | collective-permute-start | bytes 196616 | tf_op jit(solution)/shard_map/ppermute | solution.py:410
  30.0 4.0 %shard_map.49.refs_0_ = f32[2,5,3,10,8,128]{5,4,3,2,1,0:T(8,128)S(1)} custom-call(f32[2,5,3,10,8,128]{5,4,3,2,1,0:T(8,128)S(1)} %get-tuple-element.43.refs_0_.refs_1_, f32[2,5,3,10,8,128]{5,4,3,2,1,0:T(8,128)S(1)} %get-tuple-element.37.refs_0_.refs_1_, f32[5,3,10,8,128]{4,3,2,1,0:T(8,128)S(1)} %get-tuple-element.44.refs_2_, f32[1,1]{1,0:T(1,128)} %bitcast.4.refs_3_, ...), custom_call_target="tpu_custom_call" | custom-call | flops 4000000 | bytes 4000000 | tf_op jit(solution)/shard_map/pallas_call | solution.py:446
  35.7 7.5 %collective-permute-start.9 = (f32[2,4,25,8,128]{4,3,2,1,0:T(8,128)S(1)}, f32[2,4,25,8,128]{4,3,2,1,0:T(8,128)S(1)}, u32[]{:S(2)}, u32[]{:S(2)}) collective-permute-start(f32[2,4,25,8,128]{4,3,2,1,0:T(8,128)S(1)} %get-tuple-element.51), channel_id=1, source_target_pairs={{0,16},{16,0},{32,48},{48,32},{64,80},{80,64},{96,112},{112,96},{1... | collective-permute-start | bytes 2457608 | tf_op jit(solution)/shard_map/ppermute | solution.py:410
  43.2 1.8 %collective-permute-start.10 = (f32[2,64,128]{2,1,0:T(8,128)S(1)}, f32[2,64,128]{2,1,0:T(8,128)S(1)}, u32[]{:S(2)}, u32[]{:S(2)}) collective-permute-start(f32[2,64,128]{2,1,0:T(8,128)S(1)} %get-tuple-element.52), channel_id=1, source_target_pairs={{0,4},{4,0},{8,12},{12,8},{1,5},{5,1},{9,13},{13,9},{2,6},{6,2},{1... | collective-permute-start | bytes 196616 | tf_op jit(solution)/shard_map/ppermute | solution.py:410
  45.0 2.1 %collective-permute-start.11 = (f32[2,64,128]{2,1,0:T(8,128)S(1)}, f32[2,64,128]{2,1,0:T(8,128)S(1)}, u32[]{:S(2)}, u32[]{:S(2)}) collective-permute-start(f32[2,64,128]{2,1,0:T(8,128)S(1)} %get-tuple-element.53), channel_id=1, source_target_pairs={{0,12},{4,8},{8,4},{12,0},{1,13},{5,9},{9,5},{13,1},{2,14},{6,10},... | collective-permute-start | bytes 196616 | tf_op jit(solution)/shard_map/ppermute | solution.py:410
  47.1 4.0 %shard_map.51.refs_0_ = f32[2,5,3,10,8,128]{5,4,3,2,1,0:T(8,128)S(1)} custom-call(f32[2,5,3,10,8,128]{5,4,3,2,1,0:T(8,128)S(1)} %get-tuple-element.49.refs_0_.refs_1_, f32[2,5,3,10,8,128]{5,4,3,2,1,0:T(8,128)S(1)} %get-tuple-element.43.refs_0_.refs_1_, f32[5,3,10,8,128]{4,3,2,1,0:T(8,128)S(1)} %get-tuple-element.44.refs_2_, f32[1,1]{1,0:T(1,128)} %bitcast.6.refs_3_, ...), custom_call_target="tpu_custom_call" | custom-call | flops 4000000 | bytes 4000000 | tf_op jit(solution)/shard_map/pallas_call | solution.py:446
  52.7 8.9 %collective-permute-start.13 = (f32[2,4,25,8,128]{4,3,2,1,0:T(8,128)S(1)}, f32[2,4,25,8,128]{4,3,2,1,0:T(8,128)S(1)}, u32[]{:S(2)}, u32[]{:S(2)}) collective-permute-start(f32[2,4,25,8,128]{4,3,2,1,0:T(8,128)S(1)} %get-tuple-element.56), channel_id=1, source_target_pairs={{0,16},{16,0},{32,48},{48,32},{64,80},{80,64},{96,112},{112,96},{1... | collective-permute-start | bytes 2457608 | tf_op jit(solution)/shard_map/ppermute | solution.py:410
  64.0 4.0 %shard_map.53.refs_0_ = f32[2,5,3,10,8,128]{5,4,3,2,1,0:T(8,128)S(1)} custom-call(f32[2,5,3,10,8,128]{5,4,3,2,1,0:T(8,128)S(1)} %get-tuple-element.54.refs_0_, f32[2,5,3,10,8,128]{5,4,3,2,1,0:T(8,128)S(1)} %get-tuple-element.49.refs_0_.refs_1_, f32[5,3,10,8,128]{4,3,2,1,0:T(8,128)S(1)} %get-tuple-element.44.refs_2_, f32[1,1]{1,0:T(1,128)} %bitcast.8.refs_3_, ...), custom_call_target="tpu_custom_call" | custom-call | flops 4000000 | bytes 4000000 | tf_op jit(solution)/shard_map/pallas_call | solution.py:446
  71.5 2.6 %collective-permute-start.17 = (f32[2,32,8,128]{3,2,1,0:T(8,128)S(1)}, f32[2,32,8,128]{3,2,1,0:T(8,128)S(1)}, u32[]{:S(2)}, u32[]{:S(2)}) collective-permute-start(f32[2,32,8,128]{3,2,1,0:T(8,128)S(1)} %get-tuple-element.61), channel_id=1, source_target_pairs={{0,2},{1,3},{2,0},{3,1},{4,6},{5,7},{6,4},{7,5},{8,10},{9,11},{10,... | collective-permute-start | bytes 786440 | tf_op jit(solution)/shard_map/ppermute | solution.py:410
  74.1 1.6 %collective-permute-done.16.refs_1_ = f32[2,32,8,128]{3,2,1,0:T(8,128)S(1)} collective-permute-done((f32[2,32,8,128]{3,2,1,0:T(8,128)S(1)}, f32[2,32,8,128]{3,2,1,0:T(8,128)S(1)}, u32[]{:S(2)}, u32[]{:S(2)}) %collective-permute-start.16) | collective-permute-done | bytes 262176 | tf_op jit(solution)/shard_map/ppermute | solution.py:410
  75.7 5.1 %collective-permute-done.17.refs_2_ = f32[2,32,8,128]{3,2,1,0:T(8,128)S(1)} collective-permute-done((f32[2,32,8,128]{3,2,1,0:T(8,128)S(1)}, f32[2,32,8,128]{3,2,1,0:T(8,128)S(1)}, u32[]{:S(2)}, u32[]{:S(2)}) %collective-permute-start.17) | collective-permute-done | bytes 262176 | tf_op jit(solution)/shard_map/ppermute | solution.py:410
  80.8 2.6 %collective-permute-done.18.refs_3_ = f32[2,32,8,128]{3,2,1,0:T(8,128)S(1)} collective-permute-done((f32[2,32,8,128]{3,2,1,0:T(8,128)S(1)}, f32[2,32,8,128]{3,2,1,0:T(8,128)S(1)}, u32[]{:S(2)}, u32[]{:S(2)}) %collective-permute-start.18) | collective-permute-done | bytes 262176 | tf_op jit(solution)/shard_map/ppermute | solution.py:410
  84.4 27.3 %all_to_all.5.sums_ref = f32[256,1,128]{2,1,0:T(1,128)S(1)} all-to-all(f32[256,1,128]{2,1,0:T(1,128)S(1)} %get-tuple-element.64), channel_id=1, replica_groups=mesh['dx'=16,'dy'=4,'band'=4] {'dx','dy','band'}, dimensions={0} | all-to-all | bytes 262144 | tf_op jit(solution)/shard_map/all_to_all | solution.py:466
  113.0 1.9 %collective-permute-start.20 = (f32[2,32,8,128]{3,2,1,0:T(8,128)S(1)}, f32[2,32,8,128]{3,2,1,0:T(8,128)S(1)}, u32[]{:S(2)}, u32[]{:S(2)}) collective-permute-start(f32[2,32,8,128]{3,2,1,0:T(8,128)S(1)} %get-tuple-element.67), channel_id=1, source_target_pairs={{0,2},{1,3},{2,0},{3,1},{4,6},{5,7},{6,4},{7,5},{8,10},{9,11},{10,... | collective-permute-start | bytes 786440 | tf_op jit(solution)/shard_map/ppermute | solution.py:410
  114.8 1.6 %collective-permute-start.21 = (f32[2,32,8,128]{3,2,1,0:T(8,128)S(1)}, f32[2,32,8,128]{3,2,1,0:T(8,128)S(1)}, u32[]{:S(2)}, u32[]{:S(2)}) collective-permute-start(f32[2,32,8,128]{3,2,1,0:T(8,128)S(1)} %get-tuple-element.68), channel_id=1, source_target_pairs={{0,3},{1,2},{2,1},{3,0},{4,7},{5,6},{6,5},{7,4},{8,11},{9,10},{10,... | collective-permute-start | bytes 786440 | tf_op jit(solution)/shard_map/ppermute | solution.py:410
  116.5 3.7 %collective-permute-done.19.refs_1_ = f32[2,32,8,128]{3,2,1,0:T(8,128)S(1)} collective-permute-done((f32[2,32,8,128]{3,2,1,0:T(8,128)S(1)}, f32[2,32,8,128]{3,2,1,0:T(8,128)S(1)}, u32[]{:S(2)}, u32[]{:S(2)}) %collective-permute-start.19) | collective-permute-done | bytes 262176 | tf_op jit(solution)/shard_map/ppermute | solution.py:410
  120.1 6.2 %collective-permute-done.20.refs_2_ = f32[2,32,8,128]{3,2,1,0:T(8,128)S(1)} collective-permute-done((f32[2,32,8,128]{3,2,1,0:T(8,128)S(1)}, f32[2,32,8,128]{3,2,1,0:T(8,128)S(1)}, u32[]{:S(2)}, u32[]{:S(2)}) %collective-permute-start.20) | collective-permute-done | bytes 262176 | tf_op jit(solution)/shard_map/ppermute | solution.py:410
  126.3 2.0 %collective-permute-done.21.refs_3_ = f32[2,32,8,128]{3,2,1,0:T(8,128)S(1)} collective-permute-done((f32[2,32,8,128]{3,2,1,0:T(8,128)S(1)}, f32[2,32,8,128]{3,2,1,0:T(8,128)S(1)}, u32[]{:S(2)}, u32[]{:S(2)}) %collective-permute-start.21) | collective-permute-done | bytes 262176 | tf_op jit(solution)/shard_map/ppermute | solution.py:410
  (37 shorter events, 17.3 us)
Async XLA Ops:
  0.0 1.3 copy-start
  1.3 13.2 %copy-start.1 = (f32[5,80,320]{2,1,0:T(8,128)S(1)}, f32[5,80,320]{2,1,0:T(8,128)}, u32[]{:S(2)}) copy-start(f32[5,80,320]{2,1,0:T(8,128)} %refs_1_.1) | copy-start | bytes 1536004
  1.7 16.8 %collective-permute-start = (f32[2,4,25,8,128]{4,3,2,1,0:T(8,128)S(1)}, f32[2,4,25,8,128]{4,3,2,1,0:T(8,128)S(1)}, u32[]{:S(2)}, u32[]{:S(2)}) collective-permute-start(f32[2,4,25,8,128]{4,3,2,1,0:T(8,128)S(1)} %get-tuple-element.39), channel_id=1, source_target_pairs={{0,240},{16,32},{32,16},{48,64},{64,48},{80,96},{96,80},{112,128},... | collective-permute-start | bytes 2457608 | tf_op jit(solution)/shard_map/ppermute | solution.py:410
  4.4 14.1 %collective-permute-start.1 = (f32[2,4,25,8,128]{4,3,2,1,0:T(8,128)S(1)}, f32[2,4,25,8,128]{4,3,2,1,0:T(8,128)S(1)}, u32[]{:S(2)}, u32[]{:S(2)}) collective-permute-start(f32[2,4,25,8,128]{4,3,2,1,0:T(8,128)S(1)} %get-tuple-element.40), channel_id=1, source_target_pairs={{0,16},{16,0},{32,48},{48,32},{64,80},{80,64},{96,112},{112,96},{1... | collective-permute-start | bytes 2457608 | tf_op jit(solution)/shard_map/ppermute | solution.py:410
  6.8 11.6 %collective-permute-start.2 = (f32[2,64,128]{2,1,0:T(8,128)S(1)}, f32[2,64,128]{2,1,0:T(8,128)S(1)}, u32[]{:S(2)}, u32[]{:S(2)}) collective-permute-start(f32[2,64,128]{2,1,0:T(8,128)S(1)} %get-tuple-element.41), channel_id=1, source_target_pairs={{0,4},{4,0},{8,12},{12,8},{1,5},{5,1},{9,13},{13,9},{2,6},{6,2},{1... | collective-permute-start | bytes 196616 | tf_op jit(solution)/shard_map/ppermute | solution.py:410
  9.8 8.6 %collective-permute-start.3 = (f32[2,64,128]{2,1,0:T(8,128)S(1)}, f32[2,64,128]{2,1,0:T(8,128)S(1)}, u32[]{:S(2)}, u32[]{:S(2)}) collective-permute-start(f32[2,64,128]{2,1,0:T(8,128)S(1)} %get-tuple-element.42), channel_id=1, source_target_pairs={{0,12},{4,8},{8,4},{12,0},{1,13},{5,9},{9,5},{13,1},{2,14},{6,10},... | collective-permute-start | bytes 196616 | tf_op jit(solution)/shard_map/ppermute | solution.py:410
  19.3 15.5 %collective-permute-start.4 = (f32[2,4,25,8,128]{4,3,2,1,0:T(8,128)S(1)}, f32[2,4,25,8,128]{4,3,2,1,0:T(8,128)S(1)}, u32[]{:S(2)}, u32[]{:S(2)}) collective-permute-start(f32[2,4,25,8,128]{4,3,2,1,0:T(8,128)S(1)} %get-tuple-element.45), channel_id=1, source_target_pairs={{0,240},{16,32},{32,16},{48,64},{64,48},{80,96},{96,80},{112,128},... | collective-permute-start | bytes 2457608 | tf_op jit(solution)/shard_map/ppermute | solution.py:410
  20.0 14.8 %collective-permute-start.5 = (f32[2,4,25,8,128]{4,3,2,1,0:T(8,128)S(1)}, f32[2,4,25,8,128]{4,3,2,1,0:T(8,128)S(1)}, u32[]{:S(2)}, u32[]{:S(2)}) collective-permute-start(f32[2,4,25,8,128]{4,3,2,1,0:T(8,128)S(1)} %get-tuple-element.46), channel_id=1, source_target_pairs={{0,16},{16,0},{32,48},{48,32},{64,80},{80,64},{96,112},{112,96},{1... | collective-permute-start | bytes 2457608 | tf_op jit(solution)/shard_map/ppermute | solution.py:410
  26.4 7.7 %collective-permute-start.6 = (f32[2,64,128]{2,1,0:T(8,128)S(1)}, f32[2,64,128]{2,1,0:T(8,128)S(1)}, u32[]{:S(2)}, u32[]{:S(2)}) collective-permute-start(f32[2,64,128]{2,1,0:T(8,128)S(1)} %get-tuple-element.47), channel_id=1, source_target_pairs={{0,4},{4,0},{8,12},{12,8},{1,5},{5,1},{9,13},{13,9},{2,6},{6,2},{1... | collective-permute-start | bytes 196616 | tf_op jit(solution)/shard_map/ppermute | solution.py:410
  27.8 7.0 %collective-permute-start.7 = (f32[2,64,128]{2,1,0:T(8,128)S(1)}, f32[2,64,128]{2,1,0:T(8,128)S(1)}, u32[]{:S(2)}, u32[]{:S(2)}) collective-permute-start(f32[2,64,128]{2,1,0:T(8,128)S(1)} %get-tuple-element.48), channel_id=1, source_target_pairs={{0,12},{4,8},{8,4},{12,0},{1,13},{5,9},{9,5},{13,1},{2,14},{6,10},... | collective-permute-start | bytes 196616 | tf_op jit(solution)/shard_map/ppermute | solution.py:410
  35.6 16.1 %collective-permute-start.8 = (f32[2,4,25,8,128]{4,3,2,1,0:T(8,128)S(1)}, f32[2,4,25,8,128]{4,3,2,1,0:T(8,128)S(1)}, u32[]{:S(2)}, u32[]{:S(2)}) collective-permute-start(f32[2,4,25,8,128]{4,3,2,1,0:T(8,128)S(1)} %get-tuple-element.50), channel_id=1, source_target_pairs={{0,240},{16,32},{32,16},{48,64},{64,48},{80,96},{96,80},{112,128},... | collective-permute-start | bytes 2457608 | tf_op jit(solution)/shard_map/ppermute | solution.py:410
  35.7 16.0 %collective-permute-start.9 = (f32[2,4,25,8,128]{4,3,2,1,0:T(8,128)S(1)}, f32[2,4,25,8,128]{4,3,2,1,0:T(8,128)S(1)}, u32[]{:S(2)}, u32[]{:S(2)}) collective-permute-start(f32[2,4,25,8,128]{4,3,2,1,0:T(8,128)S(1)} %get-tuple-element.51), channel_id=1, source_target_pairs={{0,16},{16,0},{32,48},{48,32},{64,80},{80,64},{96,112},{112,96},{1... | collective-permute-start | bytes 2457608 | tf_op jit(solution)/shard_map/ppermute | solution.py:410
  43.2 7.9 %collective-permute-start.10 = (f32[2,64,128]{2,1,0:T(8,128)S(1)}, f32[2,64,128]{2,1,0:T(8,128)S(1)}, u32[]{:S(2)}, u32[]{:S(2)}) collective-permute-start(f32[2,64,128]{2,1,0:T(8,128)S(1)} %get-tuple-element.52), channel_id=1, source_target_pairs={{0,4},{4,0},{8,12},{12,8},{1,5},{5,1},{9,13},{13,9},{2,6},{6,2},{1... | collective-permute-start | bytes 196616 | tf_op jit(solution)/shard_map/ppermute | solution.py:410
  45.0 6.7 %collective-permute-start.11 = (f32[2,64,128]{2,1,0:T(8,128)S(1)}, f32[2,64,128]{2,1,0:T(8,128)S(1)}, u32[]{:S(2)}, u32[]{:S(2)}) collective-permute-start(f32[2,64,128]{2,1,0:T(8,128)S(1)} %get-tuple-element.53), channel_id=1, source_target_pairs={{0,12},{4,8},{8,4},{12,0},{1,13},{5,9},{9,5},{13,1},{2,14},{6,10},... | collective-permute-start | bytes 196616 | tf_op jit(solution)/shard_map/ppermute | solution.py:410
  52.6 16.7 %collective-permute-start.12 = (f32[2,4,25,8,128]{4,3,2,1,0:T(8,128)S(1)}, f32[2,4,25,8,128]{4,3,2,1,0:T(8,128)S(1)}, u32[]{:S(2)}, u32[]{:S(2)}) collective-permute-start(f32[2,4,25,8,128]{4,3,2,1,0:T(8,128)S(1)} %get-tuple-element.55), channel_id=1, source_target_pairs={{0,240},{16,32},{32,16},{48,64},{64,48},{80,96},{96,80},{112,128},... | collective-permute-start | bytes 2457608 | tf_op jit(solution)/shard_map/ppermute | solution.py:410
  52.7 16.6 %collective-permute-start.13 = (f32[2,4,25,8,128]{4,3,2,1,0:T(8,128)S(1)}, f32[2,4,25,8,128]{4,3,2,1,0:T(8,128)S(1)}, u32[]{:S(2)}, u32[]{:S(2)}) collective-permute-start(f32[2,4,25,8,128]{4,3,2,1,0:T(8,128)S(1)} %get-tuple-element.56), channel_id=1, source_target_pairs={{0,16},{16,0},{32,48},{48,32},{64,80},{80,64},{96,112},{112,96},{1... | collective-permute-start | bytes 2457608 | tf_op jit(solution)/shard_map/ppermute | solution.py:410
  61.5 6.5 %collective-permute-start.14 = (f32[2,64,128]{2,1,0:T(8,128)S(1)}, f32[2,64,128]{2,1,0:T(8,128)S(1)}, u32[]{:S(2)}, u32[]{:S(2)}) collective-permute-start(f32[2,64,128]{2,1,0:T(8,128)S(1)} %get-tuple-element.57), channel_id=1, source_target_pairs={{0,4},{4,0},{8,12},{12,8},{1,5},{5,1},{9,13},{13,9},{2,6},{6,2},{1... | collective-permute-start | bytes 196616 | tf_op jit(solution)/shard_map/ppermute | solution.py:410
  62.9 6.3 %collective-permute-start.15 = (f32[2,64,128]{2,1,0:T(8,128)S(1)}, f32[2,64,128]{2,1,0:T(8,128)S(1)}, u32[]{:S(2)}, u32[]{:S(2)}) collective-permute-start(f32[2,64,128]{2,1,0:T(8,128)S(1)} %get-tuple-element.58), channel_id=1, source_target_pairs={{0,12},{4,8},{8,4},{12,0},{1,13},{5,9},{9,5},{13,1},{2,14},{6,10},... | collective-permute-start | bytes 196616 | tf_op jit(solution)/shard_map/ppermute | solution.py:410
  70.1 5.6 %collective-permute-start.16 = (f32[2,32,8,128]{3,2,1,0:T(8,128)S(1)}, f32[2,32,8,128]{3,2,1,0:T(8,128)S(1)}, u32[]{:S(2)}, u32[]{:S(2)}) collective-permute-start(f32[2,32,8,128]{3,2,1,0:T(8,128)S(1)} %get-tuple-element.60), channel_id=1, source_target_pairs={{0,1},{1,0},{2,3},{3,2},{4,5},{5,4},{6,7},{7,6},{8,9},{9,8},{10,11... | collective-permute-start | bytes 786440 | tf_op jit(solution)/shard_map/ppermute | solution.py:410
  71.5 9.3 %collective-permute-start.17 = (f32[2,32,8,128]{3,2,1,0:T(8,128)S(1)}, f32[2,32,8,128]{3,2,1,0:T(8,128)S(1)}, u32[]{:S(2)}, u32[]{:S(2)}) collective-permute-start(f32[2,32,8,128]{3,2,1,0:T(8,128)S(1)} %get-tuple-element.61), channel_id=1, source_target_pairs={{0,2},{1,3},{2,0},{3,1},{4,6},{5,7},{6,4},{7,5},{8,10},{9,11},{10,... | collective-permute-start | bytes 786440 | tf_op jit(solution)/shard_map/ppermute | solution.py:410
  74.1 9.2 %collective-permute-start.18 = (f32[2,32,8,128]{3,2,1,0:T(8,128)S(1)}, f32[2,32,8,128]{3,2,1,0:T(8,128)S(1)}, u32[]{:S(2)}, u32[]{:S(2)}) collective-permute-start(f32[2,32,8,128]{3,2,1,0:T(8,128)S(1)} %get-tuple-element.62), channel_id=1, source_target_pairs={{0,3},{1,2},{2,1},{3,0},{4,7},{5,6},{6,5},{7,4},{8,11},{9,10},{10,... | collective-permute-start | bytes 786440 | tf_op jit(solution)/shard_map/ppermute | solution.py:410
  112.5 7.6 %collective-permute-start.19 = (f32[2,32,8,128]{3,2,1,0:T(8,128)S(1)}, f32[2,32,8,128]{3,2,1,0:T(8,128)S(1)}, u32[]{:S(2)}, u32[]{:S(2)}) collective-permute-start(f32[2,32,8,128]{3,2,1,0:T(8,128)S(1)} %get-tuple-element.66), channel_id=1, source_target_pairs={{0,1},{1,0},{2,3},{3,2},{4,5},{5,4},{6,7},{7,6},{8,9},{9,8},{10,11... | collective-permute-start | bytes 786440 | tf_op jit(solution)/shard_map/ppermute | solution.py:410
  113.0 13.4 %collective-permute-start.20 = (f32[2,32,8,128]{3,2,1,0:T(8,128)S(1)}, f32[2,32,8,128]{3,2,1,0:T(8,128)S(1)}, u32[]{:S(2)}, u32[]{:S(2)}) collective-permute-start(f32[2,32,8,128]{3,2,1,0:T(8,128)S(1)} %get-tuple-element.67), channel_id=1, source_target_pairs={{0,2},{1,3},{2,0},{3,1},{4,6},{5,7},{6,4},{7,5},{8,10},{9,11},{10,... | collective-permute-start | bytes 786440 | tf_op jit(solution)/shard_map/ppermute | solution.py:410
  114.8 13.5 %collective-permute-start.21 = (f32[2,32,8,128]{3,2,1,0:T(8,128)S(1)}, f32[2,32,8,128]{3,2,1,0:T(8,128)S(1)}, u32[]{:S(2)}, u32[]{:S(2)}) collective-permute-start(f32[2,32,8,128]{3,2,1,0:T(8,128)S(1)} %get-tuple-element.68), channel_id=1, source_target_pairs={{0,3},{1,2},{2,1},{3,0},{4,7},{5,6},{6,5},{7,4},{8,11},{9,10},{10,... | collective-permute-start | bytes 786440 | tf_op jit(solution)/shard_map/ppermute | solution.py:410

commit v2 on v1

--- a/solution.py
+++ b/solution.py
@@ -17,8 +17,9 @@
 
 STATE = (BANDS, LAYERS, 3, 10, 8, 128)
 SIDE = (BANDS, WIDTH, 25, 8, 128)
-EDGE = (BANDS, 64, 128)
-PIECE = (BANDS, 32, 8, 128)
+EDGE = (104, 128)
+EDGE_ROWS = 50
+WHOLE = (GROUPS, BANDS, 32, 8, 128)
 
 
 def call(kernel, outs, scratch=(), semaphores=0, **kwargs):
@@ -68,18 +69,16 @@
             high_ref[band, layer - 1, 20 + j] = both
 
 
-def send_edges(tiles, band, layer, low_ref, high_ref):
-    for tile in range(3):
+def send_edges(tiles, band, layer, edge_ref):
+    for side, (start, sublane) in enumerate(((0, 0), (6, 7))):
         for j in range(4):
-            row = j * 16 + layer * 3 + tile
-            low_ref[band, row : row + 1, :] = tiles[tile][j][0:1]
-            high_ref[band, row : row + 1, :] = tiles[tile][6 + j][7:8]
-
-
-def clear_edges(band, *refs):
-    for ref in refs:
-        for j in range(4):
-            ref[band, j * 16 + 15 : j * 16 + 16, :] = jnp.zeros((1, 128), F32)
+            for tile in range(2):
+                at = j * 10 + layer * 2 + tile
+                edge_ref[side, band, at : at + 1, :] = tiles[tile][start + j][sublane : sublane + 1]
+        for j in range(2):
+            both = pair(tiles[2][start + j], tiles[2][start + j + 2])
+            at = 40 + j * 5 + layer
+            edge_ref[side, band, at : at + 1, :] = both[sublane : sublane + 1]
 
 
 def parity(axis):
@@ -98,8 +97,10 @@
 
 def hand_edges(edge_ref, inner_ref, outer_ref):
     def copy(low_ref, high_ref):
-        low_ref[...] = edge_ref[0]
-        high_ref[...] = edge_ref[1]
+        for side, ref in enumerate((low_ref, high_ref)):
+            for band in range(BANDS):
+                ref[band * EDGE_ROWS : (band + 1) * EDGE_ROWS, :] = edge_ref[side, band, 0:EDGE_ROWS, :]
+            ref[BANDS * EDGE_ROWS : EDGE[0], :] = jnp.zeros((EDGE[0] - BANDS * EDGE_ROWS, 128), F32)
 
     by_parity("dy", copy, outer_ref, inner_ref)
 
@@ -116,8 +117,7 @@
                     for j in range(10):
                         state_ref[band, layer, tile, j] = tiles[tile][j]
                 send_sides(tiles, band, layer, side_low_ref, side_high_ref)
-                send_edges(tiles, band, layer, edge_ref.at[0], edge_ref.at[1])
-            clear_edges(band, edge_ref.at[0], edge_ref.at[1])
+                send_edges(tiles, band, layer, edge_ref)
             return carry
 
         lax.fori_loop(0, BANDS, one_band, 0)
@@ -212,7 +212,7 @@
 def outer_kernel(first, last, *refs):
     part_ref, far_in_ref, near_in_ref, inner_in_ref, outer_in_ref, cutoff_ref, upper_ref, *refs = refs
     if last:
-        *piece_refs, rim_ref, whole_ref = refs
+        whole_ref, rim_ref = refs
         state_ref, far_ref, near_ref, edge_ref = None, None, None, None
     else:
         state_ref, far_ref, near_ref, inner_ref, outer_ref, rim_ref, edge_ref = refs
@@ -221,21 +221,21 @@
     factor = 1.0 if first else 2.0
     weights = [None] + [(-0.5 * factor * stencil_weights[k]) * per_half_width for k in range(1, 5)]
 
+    def halos(ref, band):
+        start = band * EDGE_ROWS
+        whole = [ref[start + j * 10 : start + j * 10 + 10, :] for j in range(4)]
+        half = [ref[start + 40 + j * 5 : start + 48 + j * 5, :] for j in range(2)]
+        return whole, half + [pltpu.roll(rows, 64, 1) for rows in half]
+
     def rims(below_ref, above_ref):
-        def one_band(band, carry):
-            for half in range(2):
-                below = [below_ref[band, 16 * j + 8 * half : 16 * j + 8 * half + 8, :] for j in range(4)]
-                above = [above_ref[band, 16 * j + 8 * half : 16 * j + 8 * half + 8, :] for j in range(4)]
+        for band in range(BANDS):
+            for below, above, rows in zip(halos(below_ref, band), halos(above_ref, band), (slice(0, 10), slice(10, 18))):
                 for j in range(4):
-                    rim_ref[band, 0, j, 8 * half : 8 * half + 8, :] = sum(
-                        weights[k] * below[4 + j - k] for k in range(j + 1, 5)
-                    )
-                    rim_ref[band, 1, j, 8 * half : 8 * half + 8, :] = sum(
-                        weights[k] * above[j + 6 + k - 10] for k in range(4 - j, 5)
-                    )
-            return carry
-
-        lax.fori_loop(0, BANDS, one_band, 0)
+                    rim_ref[band, 0, j, rows, :] = sum(weights_of(below[4 + j - k], k) for k in range(j + 1, 5))
+                    rim_ref[band, 1, j, rows, :] = sum(weights_of(above[j + k - 4], k) for k in range(4 - j, 5))
+
+    def weights_of(rows, k):
+        return (-0.5 * factor * stencil_weights[k]) * rows * per_half_width[0:1]
 
     by_parity("dy", rims, outer_in_ref, inner_in_ref)
 
@@ -243,9 +243,7 @@
         add_outside(weights, part_ref, rim_ref, low, high, state_ref, edge_ref, whole_ref)
 
     by_parity("dx", body, (far_in_ref, far_ref), (near_in_ref, near_ref))
-    if last:
-        deal(whole_ref, piece_refs)
-    else:
+    if not last:
         hand_edges(edge_ref, inner_ref, outer_ref)
 
 
@@ -273,7 +271,7 @@
                     else:
                         extra = pltpu.roll(outside[15 + j], 64, 1)
                     cell = part_ref[band, layer, tile, j] + extra
-                    at = layer * 3 + tile
+                    at = layer * 2 + tile if tile < 2 else 10 + layer
                     if j < 4:
                         cell += jnp.where(row == 0, rim_ref[band, 0, j, at : at + 1, :], 0.0)
                     if j >= 6:
@@ -290,34 +288,19 @@
                     for j in range(10):
                         state_ref[band, layer, tile, j] = tiles[tile][j]
                 send_sides(tiles, band, layer, side_low_ref, side_high_ref)
-                send_edges(tiles, band, layer, edge_ref.at[0], edge_ref.at[1])
+                send_edges(tiles, band, layer, edge_ref)
         if last:
             for place in range(125, 128):
                 whole_ref[place // 32, band, place % 32] = jnp.zeros((8, 128), F32)
-        else:
-            clear_edges(band, edge_ref.at[0], edge_ref.at[1])
         return carry
 
     lax.fori_loop(0, BANDS, one_band, 0)
 
 
-def deal(whole_ref, piece_refs):
-    for step, piece_ref in enumerate(piece_refs):
-        piece_ref[...] = whole_ref[lax.axis_index("band") ^ step]
-
-
-def collect(piece_refs, whole_ref):
-    for step, piece_ref in enumerate(piece_refs):
-        whole_ref[lax.axis_index("band") ^ step] = piece_ref[...]
-
-
 PAIRS = [(a, b) for a in range(GROUPS * BANDS) for b in range(a + 1)]
 
 
-def overlap_kernel(*refs):
-    *piece_refs, whole_ref, sums_ref, row_ref = refs
-    collect(piece_refs, whole_ref)
-
+def overlap_kernel(whole_ref, sums_ref, row_ref):
     def accumulate(at, totals):
         cells = [whole_ref[a // BANDS, a % BANDS, at] for a in range(GROUPS * BANDS)]
         return tuple(total + cells[a] * cells[b] for total, (a, b) in zip(totals, PAIRS))
@@ -336,8 +319,7 @@
     sums_ref[...] = jnp.broadcast_to(sums[0:1].reshape(1, 1, 128), sums_ref.shape)
 
 
-def rotate_kernel(cell_count, whole_ref, sums_ref, *refs):
-    *piece_refs, turned_ref = refs
+def rotate_kernel(cell_count, whole_ref, sums_ref, turned_ref):
     count = sums_ref.shape[0] // 8
     parts = [jnp.sum(sums_ref[i * count : (i + 1) * count], axis=0) for i in range(8)]
     while len(parts) > 1:
@@ -378,13 +360,9 @@
         return carry
 
     lax.fori_loop(0, 32, turn, 0)
-    deal(turned_ref, piece_refs)
-
-
-def merge_kernel(*refs):
-    *piece_refs, out_ref, whole_ref, stage_ref, plane_ref, sems = refs
-    collect(piece_refs, whole_ref)
-
+
+
+def merge_kernel(whole_ref, out_ref, stage_ref, plane_ref, sems):
     def copy_out(at):
         return pltpu.make_async_copy(plane_ref.at[at], out_ref.at[at // LAYERS, at % LAYERS], sems.at[at])
 
@@ -415,9 +393,9 @@
     return swapped(array, axis, lambda i: (i + (offset if i % 2 == 0 else -offset)) % count)
 
 
-def exchange(pieces):
-    moved = {step: swapped(pieces[step], "band", lambda i: i ^ step) for step in (2, 1, 3)}
-    return [pieces[0], moved[1], moved[2], moved[3]]
+def exchange(whole):
+    flat = whole.reshape(GROUPS, BANDS * 32 * 8, 128)
+    return lax.all_to_all(flat, "band", 0, 0).reshape(whole.shape)
 
 
 def local(band_fields, potential, cutoff, upper_bound):
@@ -426,7 +404,7 @@
     cutoff = cutoff.reshape(1, 1)
     upper_bound = upper_bound.reshape(1, 1)
     stage = (3, 80, 128)
-    edges = (2,) + EDGE
+    edges = (2, BANDS, 56, 128)
     state, far, near, inner, outer = call(
         split_kernel, (STATE, SIDE, SIDE, EDGE, EDGE), scratch=(stage, edges)
     )(band_fields)
@@ -448,34 +426,28 @@
             )
         previous = state
         arguments = (part, far, near, inner, outer, cutoff, upper_bound)
-        rim = (BANDS, 2, 4, 16, 128)
+        rim = (BANDS, 2, 4, 24, 128)
         if last:
-            pieces = call(
-                functools.partial(outer_kernel, first, last),
-                (PIECE,) * 4,
-                scratch=(rim, (GROUPS,) + PIECE),
-            )(*arguments)
+            (whole,) = call(functools.partial(outer_kernel, first, last), (WHOLE,), scratch=(rim,))(*arguments)
         else:
             state, far, near, inner, outer = call(
                 functools.partial(outer_kernel, first, last),
                 (STATE, SIDE, SIDE, EDGE, EDGE),
                 scratch=(rim, edges),
             )(*arguments)
-    pieces = exchange(pieces)
-    whole, sums = call(overlap_kernel, ((GROUPS,) + PIECE, (devices, 1, 128)), scratch=((128, 128),))(*pieces)
-    sums = lax.all_to_all(sums, ("dx", "dy", "band"), 0, 0)
-    pieces = call(
-        functools.partial(rotate_kernel, cell_count), (PIECE,) * 4, scratch=((GROUPS,) + PIECE,)
-    )(whole, sums)
-    pieces = exchange(pieces)
+    whole = exchange(whole)
+    (sums,) = call(overlap_kernel, ((devices, 1, 128),), scratch=((128, 128),))(whole)
+    sums = lax.all_to_all(sums, ("dy", "band", "dx"), 0, 0)
+    (turned,) = call(functools.partial(rotate_kernel, cell_count), (WHOLE,))(whole, sums)
+    turned = exchange(turned)
     planes = BANDS * LAYERS
     (rotated,) = call(
         merge_kernel,
         ((BANDS, LAYERS, 80, 320),),
-        scratch=((GROUPS,) + PIECE, stage, (planes, 80, 320)),
+        scratch=(stage, (planes, 80, 320)),
         semaphores=planes,
         out_specs=(pl.BlockSpec(memory_space=pl.ANY),),
-    )(*pieces)
+    )(turned)
     return rotated
 
 

time: 130 us -> 129 us (level)
  blocking collectives: 27.3 us -> 57.8 us
  waiting for transfers between devices: 23.7 us -> 1.18 us
  starting transfers between devices: 53 us -> 44.7 us
    all_to_all x1 -> x3, blocking collectives: 27.3 us -> 57.8 us  [the longest x2 30.3 us: exchange(): return lax.all_to_all(flat, 'band', 0, 0).reshape(whole.shape)]
    ppermute x22 -> x16, waiting for transfers between devices: 23.7 us -> 1.18 us  [swapped(): lax.ppermute(array, axis, [(i, partner(i)) for i in range(lax.axis_size(a...]
    ppermute x22 -> x16, starting transfers between devices: 53 us -> 44.7 us  [swapped(): lax.ppermute(array, axis, [(i, partner(i)) for i in range(lax.axis_size(a...]
  transfers between devices with their start and end apart: 22 -> 16, of which waited for: 9 -> 3; matrix products, arithmetic and copies ran while one was open for 0% -> 0% of each run, Pallas kernels for 12% -> 12%
where the time goes in v2:
time: 129 us
  blocking collectives  57.8 us (45%)
  starting transfers between devices  44.7 us (35%)
  Pallas kernels  22.6 us (18%)
  between operations  1.63 us (1%)
  local copies, waits for them, and re-layouts  1.29 us (1%)
    ppermute x16, starting transfers between devices, swapped(): lax.ppermute(array, axis, [(i, partner(i)) for i in range(lax.axis_size(a...  44.7 us
    all_to_all x2, blocking collectives, exchange(): return lax.all_to_all(flat, 'band', 0, 0).reshape(whole.shape)  30.3 us
    all_to_all x1, blocking collectives, local(): sums = lax.all_to_all(sums, ('dy', 'band', 'dx'), 0, 0)  27.5 us
    pallas_call x3, Pallas kernels, local(): call(functools.partial(inner_kernel, False), (STATE,), scratch=(wide,))  12 us
    pallas_call x1, Pallas kernels, local(): call(functools.partial(inner_kernel, True), (STATE, STATE[1:]), scratch=(...  4.02 us
  transfers between devices with their start and end apart: 16, of which 3 were waited for; matrix products, arithmetic and copies ran while one was open for 0% of the time, Pallas kernels for 12%

profile of v2, /device:TPU:1, one launch (start us, length us, event | category | flops | bytes accessed | tf_op | source)
XLA Modules:
  0.0 129.3 jit_solution(5981707928059793157)
XLA Ops:
  0.0 1.3 copy-done
  1.7 2.7 %collective-permute-start = (f32[2,4,25,8,128]{4,3,2,1,0:T(8,128)S(1)}, f32[2,4,25,8,128]{4,3,2,1,0:T(8,128)S(1)}, u32[]{:S(2)}, u32[]{:S(2)}) collective-permute-start(f32[2,4,25,8,128]{4,3,2,1,0:T(8,128)S(1)} %get-tuple-element.29), channel_id=1, source_target_pairs={{0,240},{16,32},{32,16},{48,64},{64,48},{80,96},{96,80},{112,128},... | collective-permute-start | bytes 2457608 | tf_op jit(solution)/shard_map/ppermute | solution.py:388
  4.4 2.5 %collective-permute-start.1 = (f32[2,4,25,8,128]{4,3,2,1,0:T(8,128)S(1)}, f32[2,4,25,8,128]{4,3,2,1,0:T(8,128)S(1)}, u32[]{:S(2)}, u32[]{:S(2)}) collective-permute-start(f32[2,4,25,8,128]{4,3,2,1,0:T(8,128)S(1)} %get-tuple-element.30), channel_id=1, source_target_pairs={{0,16},{16,0},{32,48},{48,32},{64,80},{80,64},{96,112},{112,96},{1... | collective-permute-start | bytes 2457608 | tf_op jit(solution)/shard_map/ppermute | solution.py:388
  6.8 3.0 %collective-permute-start.2 = (f32[104,128]{1,0:T(8,128)S(1)}, f32[104,128]{1,0:T(8,128)S(1)}, u32[]{:S(2)}, u32[]{:S(2)}) collective-permute-start(f32[104,128]{1,0:T(8,128)S(1)} %get-tuple-element.31), channel_id=1, source_target_pairs={{0,4},{4,0},{8,12},{12,8},{1,5},{5,1},{9,13},{13,9},{2,6},{6,2},{1... | collective-permute-start | bytes 159752 | tf_op jit(solution)/shard_map/ppermute | solution.py:388
  9.8 3.3 %collective-permute-start.3 = (f32[104,128]{1,0:T(8,128)S(1)}, f32[104,128]{1,0:T(8,128)S(1)}, u32[]{:S(2)}, u32[]{:S(2)}) collective-permute-start(f32[104,128]{1,0:T(8,128)S(1)} %get-tuple-element.32), channel_id=1, source_target_pairs={{0,12},{4,8},{8,4},{12,0},{1,13},{5,9},{9,5},{13,1},{2,14},{6,10},... | collective-permute-start | bytes 159752 | tf_op jit(solution)/shard_map/ppermute | solution.py:388
  14.4 4.0 %shard_map.47 = (f32[2,5,3,10,8,128]{5,4,3,2,1,0:T(8,128)S(1)}, f32[5,3,10,8,128]{4,3,2,1,0:T(8,128)S(1)}) custom-call(f32[2,5,3,10,8,128]{5,4,3,2,1,0:T(8,128)S(1)} %get-tuple-element.27.refs_0_.refs_1_, f32[5,80,320]{2,1,0:T(8,128)S(1)} %copy-done.1, f32[1,1]{1,0:T(1,128)} %bitcast.6.refs_2_, f32[1,1]{1,0:T(1,128)} %bitcast.14.refs_3_), custom_call_target="tpu_custom_call" | custom-call | flops 4000000 | bytes 4000000 | tf_op jit(solution)/shard_map/pallas_call | solution.py:420
  20.0 5.8 %collective-permute-start.5 = (f32[2,4,25,8,128]{4,3,2,1,0:T(8,128)S(1)}, f32[2,4,25,8,128]{4,3,2,1,0:T(8,128)S(1)}, u32[]{:S(2)}, u32[]{:S(2)}) collective-permute-start(f32[2,4,25,8,128]{4,3,2,1,0:T(8,128)S(1)} %get-tuple-element.36), channel_id=1, source_target_pairs={{0,16},{16,0},{32,48},{48,32},{64,80},{80,64},{96,112},{112,96},{1... | collective-permute-start | bytes 2457608 | tf_op jit(solution)/shard_map/ppermute | solution.py:388
  25.9 1.4 %collective-permute-start.6 = (f32[104,128]{1,0:T(8,128)S(1)}, f32[104,128]{1,0:T(8,128)S(1)}, u32[]{:S(2)}, u32[]{:S(2)}) collective-permute-start(f32[104,128]{1,0:T(8,128)S(1)} %get-tuple-element.37), channel_id=1, source_target_pairs={{0,4},{4,0},{8,12},{12,8},{1,5},{5,1},{9,13},{13,9},{2,6},{6,2},{1... | collective-permute-start | bytes 159752 | tf_op jit(solution)/shard_map/ppermute | solution.py:388
  27.3 2.3 %collective-permute-start.7 = (f32[104,128]{1,0:T(8,128)S(1)}, f32[104,128]{1,0:T(8,128)S(1)}, u32[]{:S(2)}, u32[]{:S(2)}) collective-permute-start(f32[104,128]{1,0:T(8,128)S(1)} %get-tuple-element.38), channel_id=1, source_target_pairs={{0,12},{4,8},{8,4},{12,0},{1,13},{5,9},{9,5},{13,1},{2,14},{6,10},... | collective-permute-start | bytes 159752 | tf_op jit(solution)/shard_map/ppermute | solution.py:388
  29.6 4.0 %shard_map.49.refs_0_ = f32[2,5,3,10,8,128]{5,4,3,2,1,0:T(8,128)S(1)} custom-call(f32[2,5,3,10,8,128]{5,4,3,2,1,0:T(8,128)S(1)} %get-tuple-element.33.refs_0_.refs_1_, f32[2,5,3,10,8,128]{5,4,3,2,1,0:T(8,128)S(1)} %get-tuple-element.27.refs_0_.refs_1_, f32[5,3,10,8,128]{4,3,2,1,0:T(8,128)S(1)} %get-tuple-element.34.refs_2_, f32[1,1]{1,0:T(1,128)} %bitcast.8.refs_3_, ...), custom_call_target="tpu_custom_call" | custom-call | flops 4000000 | bytes 4000000 | tf_op jit(solution)/shard_map/pallas_call | solution.py:424
  34.8 7.6 %collective-permute-start.9 = (f32[2,4,25,8,128]{4,3,2,1,0:T(8,128)S(1)}, f32[2,4,25,8,128]{4,3,2,1,0:T(8,128)S(1)}, u32[]{:S(2)}, u32[]{:S(2)}) collective-permute-start(f32[2,4,25,8,128]{4,3,2,1,0:T(8,128)S(1)} %get-tuple-element.41), channel_id=1, source_target_pairs={{0,16},{16,0},{32,48},{48,32},{64,80},{80,64},{96,112},{112,96},{1... | collective-permute-start | bytes 2457608 | tf_op jit(solution)/shard_map/ppermute | solution.py:388
  42.4 1.6 %collective-permute-start.10 = (f32[104,128]{1,0:T(8,128)S(1)}, f32[104,128]{1,0:T(8,128)S(1)}, u32[]{:S(2)}, u32[]{:S(2)}) collective-permute-start(f32[104,128]{1,0:T(8,128)S(1)} %get-tuple-element.42), channel_id=1, source_target_pairs={{0,4},{4,0},{8,12},{12,8},{1,5},{5,1},{9,13},{13,9},{2,6},{6,2},{1... | collective-permute-start | bytes 159752 | tf_op jit(solution)/shard_map/ppermute | solution.py:388
  44.0 2.1 %collective-permute-start.11 = (f32[104,128]{1,0:T(8,128)S(1)}, f32[104,128]{1,0:T(8,128)S(1)}, u32[]{:S(2)}, u32[]{:S(2)}) collective-permute-start(f32[104,128]{1,0:T(8,128)S(1)} %get-tuple-element.43), channel_id=1, source_target_pairs={{0,12},{4,8},{8,4},{12,0},{1,13},{5,9},{9,5},{13,1},{2,14},{6,10},... | collective-permute-start | bytes 159752 | tf_op jit(solution)/shard_map/ppermute | solution.py:388
  46.1 4.0 %shard_map.51.refs_0_ = f32[2,5,3,10,8,128]{5,4,3,2,1,0:T(8,128)S(1)} custom-call(f32[2,5,3,10,8,128]{5,4,3,2,1,0:T(8,128)S(1)} %get-tuple-element.39.refs_0_.refs_1_, f32[2,5,3,10,8,128]{5,4,3,2,1,0:T(8,128)S(1)} %get-tuple-element.33.refs_0_.refs_1_, f32[5,3,10,8,128]{4,3,2,1,0:T(8,128)S(1)} %get-tuple-element.34.refs_2_, f32[1,1]{1,0:T(1,128)} %bitcast.10.refs_3_, ...), custom_call_target="tpu_custom_call" | custom-call | flops 4000000 | bytes 4000000 | tf_op jit(solution)/shard_map/pallas_call | solution.py:424
  50.3 0.8 shard_map.52
  51.2 8.8 %collective-permute-start.13 = (f32[2,4,25,8,128]{4,3,2,1,0:T(8,128)S(1)}, f32[2,4,25,8,128]{4,3,2,1,0:T(8,128)S(1)}, u32[]{:S(2)}, u32[]{:S(2)}) collective-permute-start(f32[2,4,25,8,128]{4,3,2,1,0:T(8,128)S(1)} %get-tuple-element.46), channel_id=1, source_target_pairs={{0,16},{16,0},{32,48},{48,32},{64,80},{80,64},{96,112},{112,96},{1... | collective-permute-start | bytes 2457608 | tf_op jit(solution)/shard_map/ppermute | solution.py:388
  60.0 1.4 %collective-permute-start.14 = (f32[104,128]{1,0:T(8,128)S(1)}, f32[104,128]{1,0:T(8,128)S(1)}, u32[]{:S(2)}, u32[]{:S(2)}) collective-permute-start(f32[104,128]{1,0:T(8,128)S(1)} %get-tuple-element.47), channel_id=1, source_target_pairs={{0,4},{4,0},{8,12},{12,8},{1,5},{5,1},{9,13},{13,9},{2,6},{6,2},{1... | collective-permute-start | bytes 159752 | tf_op jit(solution)/shard_map/ppermute | solution.py:388
  61.5 1.2 collective-permute-start.15
  62.7 4.0 %shard_map.53.refs_0_ = f32[2,5,3,10,8,128]{5,4,3,2,1,0:T(8,128)S(1)} custom-call(f32[2,5,3,10,8,128]{5,4,3,2,1,0:T(8,128)S(1)} %get-tuple-element.44.refs_0_, f32[2,5,3,10,8,128]{5,4,3,2,1,0:T(8,128)S(1)} %get-tuple-element.39.refs_0_.refs_1_, f32[5,3,10,8,128]{4,3,2,1,0:T(8,128)S(1)} %get-tuple-element.34.refs_2_, f32[1,1]{1,0:T(1,128)} %bitcast.12.refs_3_, ...), custom_call_target="tpu_custom_call" | custom-call | flops 4000000 | bytes 4000000 | tf_op jit(solution)/shard_map/pallas_call | solution.py:424
  68.3 13.7 %all_to_all.15 = f32[4,512,128]{2,1,0:T(8,128)S(1)} all-to-all(f32[4,512,128]{2,1,0:T(8,128)S(1)} %bitcast.24), channel_id=1, replica_groups=mesh['dx'=16,'dy'=4,'band'=4] {'band'}, dimensions={0} | all-to-all | bytes 2097152 | tf_op jit(solution)/shard_map/all_to_all | solution.py:398
  82.0 1.0 shard_map.55
  83.0 27.5 %all_to_all.16.sums_ref = f32[256,1,128]{2,1,0:T(1,128)S(1)} all-to-all(f32[256,1,128]{2,1,0:T(1,128)S(1)} %shard_map.55), channel_id=1, replica_groups=mesh['dx'=16,'dy'=4,'band'=4] {'dy','band','dx'}, dimensions={0} | all-to-all | bytes 262144 | tf_op jit(solution)/shard_map/all_to_all | solution.py:440
  111.3 16.6 %all_to_all.17 = f32[4,512,128]{2,1,0:T(8,128)S(1)} all-to-all(f32[4,512,128]{2,1,0:T(8,128)S(1)} %bitcast.25), channel_id=1, replica_groups=mesh['dx'=16,'dy'=4,'band'=4] {'band'}, dimensions={0} | all-to-all | bytes 2097152 | tf_op jit(solution)/shard_map/all_to_all | solution.py:398
  127.9 1.2 shard_map.57
  (27 shorter events, 5.7 us)
Async XLA Ops:
  0.0 1.3 copy-start
  1.3 13.1 %copy-start.1 = (f32[5,80,320]{2,1,0:T(8,128)S(1)}, f32[5,80,320]{2,1,0:T(8,128)}, u32[]{:S(2)}) copy-start(f32[5,80,320]{2,1,0:T(8,128)} %refs_1_.1) | copy-start | bytes 1536004
  1.7 16.8 %collective-permute-start = (f32[2,4,25,8,128]{4,3,2,1,0:T(8,128)S(1)}, f32[2,4,25,8,128]{4,3,2,1,0:T(8,128)S(1)}, u32[]{:S(2)}, u32[]{:S(2)}) collective-permute-start(f32[2,4,25,8,128]{4,3,2,1,0:T(8,128)S(1)} %get-tuple-element.29), channel_id=1, source_target_pairs={{0,240},{16,32},{32,16},{48,64},{64,48},{80,96},{96,80},{112,128},... | collective-permute-start | bytes 2457608 | tf_op jit(solution)/shard_map/ppermute | solution.py:388
  4.4 14.1 %collective-permute-start.1 = (f32[2,4,25,8,128]{4,3,2,1,0:T(8,128)S(1)}, f32[2,4,25,8,128]{4,3,2,1,0:T(8,128)S(1)}, u32[]{:S(2)}, u32[]{:S(2)}) collective-permute-start(f32[2,4,25,8,128]{4,3,2,1,0:T(8,128)S(1)} %get-tuple-element.30), channel_id=1, source_target_pairs={{0,16},{16,0},{32,48},{48,32},{64,80},{80,64},{96,112},{112,96},{1... | collective-permute-start | bytes 2457608 | tf_op jit(solution)/shard_map/ppermute | solution.py:388
  6.8 11.6 %collective-permute-start.2 = (f32[104,128]{1,0:T(8,128)S(1)}, f32[104,128]{1,0:T(8,128)S(1)}, u32[]{:S(2)}, u32[]{:S(2)}) collective-permute-start(f32[104,128]{1,0:T(8,128)S(1)} %get-tuple-element.31), channel_id=1, source_target_pairs={{0,4},{4,0},{8,12},{12,8},{1,5},{5,1},{9,13},{13,9},{2,6},{6,2},{1... | collective-permute-start | bytes 159752 | tf_op jit(solution)/shard_map/ppermute | solution.py:388
  9.8 8.6 %collective-permute-start.3 = (f32[104,128]{1,0:T(8,128)S(1)}, f32[104,128]{1,0:T(8,128)S(1)}, u32[]{:S(2)}, u32[]{:S(2)}) collective-permute-start(f32[104,128]{1,0:T(8,128)S(1)} %get-tuple-element.32), channel_id=1, source_target_pairs={{0,12},{4,8},{8,4},{12,0},{1,13},{5,9},{9,5},{13,1},{2,14},{6,10},... | collective-permute-start | bytes 159752 | tf_op jit(solution)/shard_map/ppermute | solution.py:388
  19.3 14.5 %collective-permute-start.4 = (f32[2,4,25,8,128]{4,3,2,1,0:T(8,128)S(1)}, f32[2,4,25,8,128]{4,3,2,1,0:T(8,128)S(1)}, u32[]{:S(2)}, u32[]{:S(2)}) collective-permute-start(f32[2,4,25,8,128]{4,3,2,1,0:T(8,128)S(1)} %get-tuple-element.35), channel_id=1, source_target_pairs={{0,240},{16,32},{32,16},{48,64},{64,48},{80,96},{96,80},{112,128},... | collective-permute-start | bytes 2457608 | tf_op jit(solution)/shard_map/ppermute | solution.py:388
  20.0 13.8 %collective-permute-start.5 = (f32[2,4,25,8,128]{4,3,2,1,0:T(8,128)S(1)}, f32[2,4,25,8,128]{4,3,2,1,0:T(8,128)S(1)}, u32[]{:S(2)}, u32[]{:S(2)}) collective-permute-start(f32[2,4,25,8,128]{4,3,2,1,0:T(8,128)S(1)} %get-tuple-element.36), channel_id=1, source_target_pairs={{0,16},{16,0},{32,48},{48,32},{64,80},{80,64},{96,112},{112,96},{1... | collective-permute-start | bytes 2457608 | tf_op jit(solution)/shard_map/ppermute | solution.py:388
  25.9 7.8 %collective-permute-start.6 = (f32[104,128]{1,0:T(8,128)S(1)}, f32[104,128]{1,0:T(8,128)S(1)}, u32[]{:S(2)}, u32[]{:S(2)}) collective-permute-start(f32[104,128]{1,0:T(8,128)S(1)} %get-tuple-element.37), channel_id=1, source_target_pairs={{0,4},{4,0},{8,12},{12,8},{1,5},{5,1},{9,13},{13,9},{2,6},{6,2},{1... | collective-permute-start | bytes 159752 | tf_op jit(solution)/shard_map/ppermute | solution.py:388
  27.3 6.6 %collective-permute-start.7 = (f32[104,128]{1,0:T(8,128)S(1)}, f32[104,128]{1,0:T(8,128)S(1)}, u32[]{:S(2)}, u32[]{:S(2)}) collective-permute-start(f32[104,128]{1,0:T(8,128)S(1)} %get-tuple-element.38), channel_id=1, source_target_pairs={{0,12},{4,8},{8,4},{12,0},{1,13},{5,9},{9,5},{13,1},{2,14},{6,10},... | collective-permute-start | bytes 159752 | tf_op jit(solution)/shard_map/ppermute | solution.py:388
  34.7 15.6 %collective-permute-start.8 = (f32[2,4,25,8,128]{4,3,2,1,0:T(8,128)S(1)}, f32[2,4,25,8,128]{4,3,2,1,0:T(8,128)S(1)}, u32[]{:S(2)}, u32[]{:S(2)}) collective-permute-start(f32[2,4,25,8,128]{4,3,2,1,0:T(8,128)S(1)} %get-tuple-element.40), channel_id=1, source_target_pairs={{0,240},{16,32},{32,16},{48,64},{64,48},{80,96},{96,80},{112,128},... | collective-permute-start | bytes 2457608 | tf_op jit(solution)/shard_map/ppermute | solution.py:388
  34.8 15.5 %collective-permute-start.9 = (f32[2,4,25,8,128]{4,3,2,1,0:T(8,128)S(1)}, f32[2,4,25,8,128]{4,3,2,1,0:T(8,128)S(1)}, u32[]{:S(2)}, u32[]{:S(2)}) collective-permute-start(f32[2,4,25,8,128]{4,3,2,1,0:T(8,128)S(1)} %get-tuple-element.41), channel_id=1, source_target_pairs={{0,16},{16,0},{32,48},{48,32},{64,80},{80,64},{96,112},{112,96},{1... | collective-permute-start | bytes 2457608 | tf_op jit(solution)/shard_map/ppermute | solution.py:388
  42.4 7.8 %collective-permute-start.10 = (f32[104,128]{1,0:T(8,128)S(1)}, f32[104,128]{1,0:T(8,128)S(1)}, u32[]{:S(2)}, u32[]{:S(2)}) collective-permute-start(f32[104,128]{1,0:T(8,128)S(1)} %get-tuple-element.42), channel_id=1, source_target_pairs={{0,4},{4,0},{8,12},{12,8},{1,5},{5,1},{9,13},{13,9},{2,6},{6,2},{1... | collective-permute-start | bytes 159752 | tf_op jit(solution)/shard_map/ppermute | solution.py:388
  44.0 6.3 %collective-permute-start.11 = (f32[104,128]{1,0:T(8,128)S(1)}, f32[104,128]{1,0:T(8,128)S(1)}, u32[]{:S(2)}, u32[]{:S(2)}) collective-permute-start(f32[104,128]{1,0:T(8,128)S(1)} %get-tuple-element.43), channel_id=1, source_target_pairs={{0,12},{4,8},{8,4},{12,0},{1,13},{5,9},{9,5},{13,1},{2,14},{6,10},... | collective-permute-start | bytes 159752 | tf_op jit(solution)/shard_map/ppermute | solution.py:388
  51.1 16.4 %collective-permute-start.12 = (f32[2,4,25,8,128]{4,3,2,1,0:T(8,128)S(1)}, f32[2,4,25,8,128]{4,3,2,1,0:T(8,128)S(1)}, u32[]{:S(2)}, u32[]{:S(2)}) collective-permute-start(f32[2,4,25,8,128]{4,3,2,1,0:T(8,128)S(1)} %get-tuple-element.45), channel_id=1, source_target_pairs={{0,240},{16,32},{32,16},{48,64},{64,48},{80,96},{96,80},{112,128},... | collective-permute-start | bytes 2457608 | tf_op jit(solution)/shard_map/ppermute | solution.py:388
  51.2 16.3 %collective-permute-start.13 = (f32[2,4,25,8,128]{4,3,2,1,0:T(8,128)S(1)}, f32[2,4,25,8,128]{4,3,2,1,0:T(8,128)S(1)}, u32[]{:S(2)}, u32[]{:S(2)}) collective-permute-start(f32[2,4,25,8,128]{4,3,2,1,0:T(8,128)S(1)} %get-tuple-element.46), channel_id=1, source_target_pairs={{0,16},{16,0},{32,48},{48,32},{64,80},{80,64},{96,112},{112,96},{1... | collective-permute-start | bytes 2457608 | tf_op jit(solution)/shard_map/ppermute | solution.py:388
  60.0 6.7 %collective-permute-start.14 = (f32[104,128]{1,0:T(8,128)S(1)}, f32[104,128]{1,0:T(8,128)S(1)}, u32[]{:S(2)}, u32[]{:S(2)}) collective-permute-start(f32[104,128]{1,0:T(8,128)S(1)} %get-tuple-element.47), channel_id=1, source_target_pairs={{0,4},{4,0},{8,12},{12,8},{1,5},{5,1},{9,13},{13,9},{2,6},{6,2},{1... | collective-permute-start | bytes 159752 | tf_op jit(solution)/shard_map/ppermute | solution.py:388
  61.5 6.0 %collective-permute-start.15 = (f32[104,128]{1,0:T(8,128)S(1)}, f32[104,128]{1,0:T(8,128)S(1)}, u32[]{:S(2)}, u32[]{:S(2)}) collective-permute-start(f32[104,128]{1,0:T(8,128)S(1)} %get-tuple-element.48), channel_id=1, source_target_pairs={{0,12},{4,8},{8,4},{12,0},{1,13},{5,9},{9,5},{13,1},{2,14},{6,10},... | collective-permute-start | bytes 159752 | tf_op jit(solution)/shard_map/ppermute | solution.py:388

commit v3 on v2

--- a/solution.py
+++ b/solution.py
@@ -19,7 +19,7 @@
 SIDE = (BANDS, WIDTH, 25, 8, 128)
 EDGE = (104, 128)
 EDGE_ROWS = 50
-WHOLE = (GROUPS, BANDS, 32, 8, 128)
+PIECE = (BANDS, 32, 8, 128)
 
 
 def call(kernel, outs, scratch=(), semaphores=0, **kwargs):
@@ -212,7 +212,7 @@
 def outer_kernel(first, last, *refs):
     part_ref, far_in_ref, near_in_ref, inner_in_ref, outer_in_ref, cutoff_ref, upper_ref, *refs = refs
     if last:
-        whole_ref, rim_ref = refs
+        *piece_refs, rim_ref, whole_ref = refs
         state_ref, far_ref, near_ref, edge_ref = None, None, None, None
     else:
         state_ref, far_ref, near_ref, inner_ref, outer_ref, rim_ref, edge_ref = refs
@@ -243,7 +243,9 @@
         add_outside(weights, part_ref, rim_ref, low, high, state_ref, edge_ref, whole_ref)
 
     by_parity("dx", body, (far_in_ref, far_ref), (near_in_ref, near_ref))
-    if not last:
+    if last:
+        deal(whole_ref, piece_refs)
+    else:
         hand_edges(edge_ref, inner_ref, outer_ref)
 
 
@@ -297,10 +299,23 @@
     lax.fori_loop(0, BANDS, one_band, 0)
 
 
+def deal(whole_ref, piece_refs):
+    for step, piece_ref in enumerate(piece_refs):
+        piece_ref[...] = whole_ref[lax.axis_index("band") ^ step]
+
+
+def collect(piece_refs, whole_ref):
+    for step, piece_ref in enumerate(piece_refs):
+        whole_ref[lax.axis_index("band") ^ step] = piece_ref[...]
+
+
 PAIRS = [(a, b) for a in range(GROUPS * BANDS) for b in range(a + 1)]
 
 
-def overlap_kernel(whole_ref, sums_ref, row_ref):
+def overlap_kernel(*refs):
+    *piece_refs, whole_ref, sums_ref, row_ref = refs
+    collect(piece_refs, whole_ref)
+
     def accumulate(at, totals):
         cells = [whole_ref[a // BANDS, a % BANDS, at] for a in range(GROUPS * BANDS)]
         return tuple(total + cells[a] * cells[b] for total, (a, b) in zip(totals, PAIRS))
@@ -319,7 +334,8 @@
     sums_ref[...] = jnp.broadcast_to(sums[0:1].reshape(1, 1, 128), sums_ref.shape)
 
 
-def rotate_kernel(cell_count, whole_ref, sums_ref, turned_ref):
+def rotate_kernel(cell_count, whole_ref, sums_ref, *refs):
+    *piece_refs, turned_ref = refs
     count = sums_ref.shape[0] // 8
     parts = [jnp.sum(sums_ref[i * count : (i + 1) * count], axis=0) for i in range(8)]
     while len(parts) > 1:
@@ -360,9 +376,13 @@
         return carry
 
     lax.fori_loop(0, 32, turn, 0)
-
-
-def merge_kernel(whole_ref, out_ref, stage_ref, plane_ref, sems):
+    deal(turned_ref, piece_refs)
+
+
+def merge_kernel(*refs):
+    *piece_refs, out_ref, whole_ref, stage_ref, plane_ref, sems = refs
+    collect(piece_refs, whole_ref)
+
     def copy_out(at):
         return pltpu.make_async_copy(plane_ref.at[at], out_ref.at[at // LAYERS, at % LAYERS], sems.at[at])
 
@@ -393,9 +413,9 @@
     return swapped(array, axis, lambda i: (i + (offset if i % 2 == 0 else -offset)) % count)
 
 
-def exchange(whole):
-    flat = whole.reshape(GROUPS, BANDS * 32 * 8, 128)
-    return lax.all_to_all(flat, "band", 0, 0).reshape(whole.shape)
+def exchange(pieces):
+    moved = {step: swapped(pieces[step], "band", lambda i: i ^ step) for step in (2, 1, 3)}
+    return [pieces[0], moved[1], moved[2], moved[3]]
 
 
 def local(band_fields, potential, cutoff, upper_bound):
@@ -428,26 +448,32 @@
         arguments = (part, far, near, inner, outer, cutoff, upper_bound)
         rim = (BANDS, 2, 4, 24, 128)
         if last:
-            (whole,) = call(functools.partial(outer_kernel, first, last), (WHOLE,), scratch=(rim,))(*arguments)
+            pieces = call(
+                functools.partial(outer_kernel, first, last),
+                (PIECE,) * 4,
+                scratch=(rim, (GROUPS,) + PIECE),
+            )(*arguments)
         else:
             state, far, near, inner, outer = call(
                 functools.partial(outer_kernel, first, last),
                 (STATE, SIDE, SIDE, EDGE, EDGE),
                 scratch=(rim, edges),
             )(*arguments)
-    whole = exchange(whole)
-    (sums,) = call(overlap_kernel, ((devices, 1, 128),), scratch=((128, 128),))(whole)
+    pieces = exchange(pieces)
+    whole, sums = call(overlap_kernel, ((GROUPS,) + PIECE, (devices, 1, 128)), scratch=((128, 128),))(*pieces)
     sums = lax.all_to_all(sums, ("dy", "band", "dx"), 0, 0)
-    (turned,) = call(functools.partial(rotate_kernel, cell_count), (WHOLE,))(whole, sums)
-    turned = exchange(turned)
+    pieces = call(
+        functools.partial(rotate_kernel, cell_count), (PIECE,) * 4, scratch=((GROUPS,) + PIECE,)
+    )(whole, sums)
+    pieces = exchange(pieces)
     planes = BANDS * LAYERS
     (rotated,) = call(
         merge_kernel,
         ((BANDS, LAYERS, 80, 320),),
-        scratch=(stage, (planes, 80, 320)),
+        scratch=((GROUPS,) + PIECE, stage, (planes, 80, 320)),
         semaphores=planes,
         out_specs=(pl.BlockSpec(memory_space=pl.ANY),),
-    )(turned)
+    )(*pieces)
     return rotated
 
 

time: 129 us -> 128 us (level)
  blocking collectives: 57.8 us -> 27 us
  waiting for transfers between devices: 1.18 us -> 21.9 us
  starting transfers between devices: 44.7 us -> 52.7 us
    all_to_all x2 -> x0, blocking collectives: 30.3 us -> none  [exchange(): return lax.all_to_all(flat, 'band', 0, 0).reshape(whole.shape)]
    ppermute x16 -> x22, waiting for transfers between devices: 1.18 us -> 21.9 us  [swapped(): lax.ppermute(array, axis, [(i, partner(i)) for i in range(lax.axis_size(a...]
    ppermute x16 -> x22, starting transfers between devices: 44.7 us -> 52.7 us  [swapped(): lax.ppermute(array, axis, [(i, partner(i)) for i in range(lax.axis_size(a...]
  transfers between devices with their start and end apart: 16 -> 22, of which waited for: 3 -> 9; matrix products, arithmetic and copies ran while one was open for 0% -> 0% of each run, Pallas kernels for 12% -> 13%
where the time goes in v3:
time: 128 us; the launch traced here: 127 us
  starting transfers between devices  52.7 us (41%)
  blocking collectives  27 us (21%)
  Pallas kernels  23 us (18%)
  waiting for transfers between devices  21.9 us (17%)
  between operations  1.63 us (1%)
  local copies, waits for them, and re-layouts  1.29 us (1%)
    ppermute x22, starting transfers between devices, swapped(): lax.ppermute(array, axis, [(i, partner(i)) for i in range(lax.axis_size(a...  52.7 us
    all_to_all x1, blocking collectives, local(): sums = lax.all_to_all(sums, ('dy', 'band', 'dx'), 0, 0)  27 us
    ppermute x22, waiting for transfers between devices, swapped(): lax.ppermute(array, axis, [(i, partner(i)) for i in range(lax.axis_size(a...  21.9 us
    pallas_call x3, Pallas kernels, local(): call(functools.partial(inner_kernel, False), (STATE,), scratch=(wide,))  12 us
    pallas_call x1, Pallas kernels, local(): call(functools.partial(inner_kernel, True), (STATE, STATE[1:]), scratch=(...  4.02 us
  transfers between devices with their start and end apart: 22, of which 9 were waited for; matrix products, arithmetic and copies ran while one was open for 0% of the time, Pallas kernels for 13%

profile of v3, /device:TPU:1, one launch (start us, length us, event | category | flops | bytes accessed | tf_op | source)
XLA Modules:
  0.0 127.4 jit_solution(14562699076776435549)
XLA Ops:
  1.7 2.7 %collective-permute-start = (f32[2,4,25,8,128]{4,3,2,1,0:T(8,128)S(1)}, f32[2,4,25,8,128]{4,3,2,1,0:T(8,128)S(1)}, u32[]{:S(2)}, u32[]{:S(2)}) collective-permute-start(f32[2,4,25,8,128]{4,3,2,1,0:T(8,128)S(1)} %get-tuple-element.39), channel_id=1, source_target_pairs={{0,240},{16,32},{32,16},{48,64},{64,48},{80,96},{96,80},{112,128},... | collective-permute-start | bytes 2457608 | tf_op jit(solution)/shard_map/ppermute | solution.py:408
  4.4 2.5 %collective-permute-start.1 = (f32[2,4,25,8,128]{4,3,2,1,0:T(8,128)S(1)}, f32[2,4,25,8,128]{4,3,2,1,0:T(8,128)S(1)}, u32[]{:S(2)}, u32[]{:S(2)}) collective-permute-start(f32[2,4,25,8,128]{4,3,2,1,0:T(8,128)S(1)} %get-tuple-element.40), channel_id=1, source_target_pairs={{0,16},{16,0},{32,48},{48,32},{64,80},{80,64},{96,112},{112,96},{1... | collective-permute-start | bytes 2457608 | tf_op jit(solution)/shard_map/ppermute | solution.py:408
  6.8 3.0 %collective-permute-start.2 = (f32[104,128]{1,0:T(8,128)S(1)}, f32[104,128]{1,0:T(8,128)S(1)}, u32[]{:S(2)}, u32[]{:S(2)}) collective-permute-start(f32[104,128]{1,0:T(8,128)S(1)} %get-tuple-element.41), channel_id=1, source_target_pairs={{0,4},{4,0},{8,12},{12,8},{1,5},{5,1},{9,13},{13,9},{2,6},{6,2},{1... | collective-permute-start | bytes 159752 | tf_op jit(solution)/shard_map/ppermute | solution.py:408
  9.8 3.3 %collective-permute-start.3 = (f32[104,128]{1,0:T(8,128)S(1)}, f32[104,128]{1,0:T(8,128)S(1)}, u32[]{:S(2)}, u32[]{:S(2)}) collective-permute-start(f32[104,128]{1,0:T(8,128)S(1)} %get-tuple-element.42), channel_id=1, source_target_pairs={{0,12},{4,8},{8,4},{12,0},{1,13},{5,9},{9,5},{13,1},{2,14},{6,10},... | collective-permute-start | bytes 159752 | tf_op jit(solution)/shard_map/ppermute | solution.py:408
  14.4 4.0 %shard_map.47 = (f32[2,5,3,10,8,128]{5,4,3,2,1,0:T(8,128)S(1)}, f32[5,3,10,8,128]{4,3,2,1,0:T(8,128)S(1)}) custom-call(f32[2,5,3,10,8,128]{5,4,3,2,1,0:T(8,128)S(1)} %get-tuple-element.37.refs_0_.refs_1_, f32[5,80,320]{2,1,0:T(8,128)S(1)} %copy-done.1, f32[1,1]{1,0:T(1,128)} %bitcast.2.refs_2_, f32[1,1]{1,0:T(1,128)} %bitcast.10.refs_3_), custom_call_target="tpu_custom_call" | custom-call | flops 4000000 | bytes 4000000 | tf_op jit(solution)/shard_map/pallas_call | solution.py:440
  20.0 5.8 %collective-permute-start.5 = (f32[2,4,25,8,128]{4,3,2,1,0:T(8,128)S(1)}, f32[2,4,25,8,128]{4,3,2,1,0:T(8,128)S(1)}, u32[]{:S(2)}, u32[]{:S(2)}) collective-permute-start(f32[2,4,25,8,128]{4,3,2,1,0:T(8,128)S(1)} %get-tuple-element.46), channel_id=1, source_target_pairs={{0,16},{16,0},{32,48},{48,32},{64,80},{80,64},{96,112},{112,96},{1... | collective-permute-start | bytes 2457608 | tf_op jit(solution)/shard_map/ppermute | solution.py:408
  27.3 2.3 %collective-permute-start.7 = (f32[104,128]{1,0:T(8,128)S(1)}, f32[104,128]{1,0:T(8,128)S(1)}, u32[]{:S(2)}, u32[]{:S(2)}) collective-permute-start(f32[104,128]{1,0:T(8,128)S(1)} %get-tuple-element.48), channel_id=1, source_target_pairs={{0,12},{4,8},{8,4},{12,0},{1,13},{5,9},{9,5},{13,1},{2,14},{6,10},... | collective-permute-start | bytes 159752 | tf_op jit(solution)/shard_map/ppermute | solution.py:408
  29.6 4.0 %shard_map.49.refs_0_ = f32[2,5,3,10,8,128]{5,4,3,2,1,0:T(8,128)S(1)} custom-call(f32[2,5,3,10,8,128]{5,4,3,2,1,0:T(8,128)S(1)} %get-tuple-element.43.refs_0_.refs_1_, f32[2,5,3,10,8,128]{5,4,3,2,1,0:T(8,128)S(1)} %get-tuple-element.37.refs_0_.refs_1_, f32[5,3,10,8,128]{4,3,2,1,0:T(8,128)S(1)} %get-tuple-element.44.refs_2_, f32[1,1]{1,0:T(1,128)} %bitcast.4.refs_3_, ...), custom_call_target="tpu_custom_call" | custom-call | flops 4000000 | bytes 4000000 | tf_op jit(solution)/shard_map/pallas_call | solution.py:444
  34.8 7.6 %collective-permute-start.9 = (f32[2,4,25,8,128]{4,3,2,1,0:T(8,128)S(1)}, f32[2,4,25,8,128]{4,3,2,1,0:T(8,128)S(1)}, u32[]{:S(2)}, u32[]{:S(2)}) collective-permute-start(f32[2,4,25,8,128]{4,3,2,1,0:T(8,128)S(1)} %get-tuple-element.51), channel_id=1, source_target_pairs={{0,16},{16,0},{32,48},{48,32},{64,80},{80,64},{96,112},{112,96},{1... | collective-permute-start | bytes 2457608 | tf_op jit(solution)/shard_map/ppermute | solution.py:408
  42.4 1.6 %collective-permute-start.10 = (f32[104,128]{1,0:T(8,128)S(1)}, f32[104,128]{1,0:T(8,128)S(1)}, u32[]{:S(2)}, u32[]{:S(2)}) collective-permute-start(f32[104,128]{1,0:T(8,128)S(1)} %get-tuple-element.52), channel_id=1, source_target_pairs={{0,4},{4,0},{8,12},{12,8},{1,5},{5,1},{9,13},{13,9},{2,6},{6,2},{1... | collective-permute-start | bytes 159752 | tf_op jit(solution)/shard_map/ppermute | solution.py:408
  44.0 2.1 %collective-permute-start.11 = (f32[104,128]{1,0:T(8,128)S(1)}, f32[104,128]{1,0:T(8,128)S(1)}, u32[]{:S(2)}, u32[]{:S(2)}) collective-permute-start(f32[104,128]{1,0:T(8,128)S(1)} %get-tuple-element.53), channel_id=1, source_target_pairs={{0,12},{4,8},{8,4},{12,0},{1,13},{5,9},{9,5},{13,1},{2,14},{6,10},... | collective-permute-start | bytes 159752 | tf_op jit(solution)/shard_map/ppermute | solution.py:408
  46.1 4.0 %shard_map.51.refs_0_ = f32[2,5,3,10,8,128]{5,4,3,2,1,0:T(8,128)S(1)} custom-call(f32[2,5,3,10,8,128]{5,4,3,2,1,0:T(8,128)S(1)} %get-tuple-element.49.refs_0_.refs_1_, f32[2,5,3,10,8,128]{5,4,3,2,1,0:T(8,128)S(1)} %get-tuple-element.43.refs_0_.refs_1_, f32[5,3,10,8,128]{4,3,2,1,0:T(8,128)S(1)} %get-tuple-element.44.refs_2_, f32[1,1]{1,0:T(1,128)} %bitcast.6.refs_3_, ...), custom_call_target="tpu_custom_call" | custom-call | flops 4000000 | bytes 4000000 | tf_op jit(solution)/shard_map/pallas_call | solution.py:444
  51.2 8.8 %collective-permute-start.13 = (f32[2,4,25,8,128]{4,3,2,1,0:T(8,128)S(1)}, f32[2,4,25,8,128]{4,3,2,1,0:T(8,128)S(1)}, u32[]{:S(2)}, u32[]{:S(2)}) collective-permute-start(f32[2,4,25,8,128]{4,3,2,1,0:T(8,128)S(1)} %get-tuple-element.56), channel_id=1, source_target_pairs={{0,16},{16,0},{32,48},{48,32},{64,80},{80,64},{96,112},{112,96},{1... | collective-permute-start | bytes 2457608 | tf_op jit(solution)/shard_map/ppermute | solution.py:408
  62.7 4.0 %shard_map.53.refs_0_ = f32[2,5,3,10,8,128]{5,4,3,2,1,0:T(8,128)S(1)} custom-call(f32[2,5,3,10,8,128]{5,4,3,2,1,0:T(8,128)S(1)} %get-tuple-element.54.refs_0_, f32[2,5,3,10,8,128]{5,4,3,2,1,0:T(8,128)S(1)} %get-tuple-element.49.refs_0_.refs_1_, f32[5,3,10,8,128]{4,3,2,1,0:T(8,128)S(1)} %get-tuple-element.44.refs_2_, f32[1,1]{1,0:T(1,128)} %bitcast.8.refs_3_, ...), custom_call_target="tpu_custom_call" | custom-call | flops 4000000 | bytes 4000000 | tf_op jit(solution)/shard_map/pallas_call | solution.py:444
  69.8 2.6 %collective-permute-start.17 = (f32[2,32,8,128]{3,2,1,0:T(8,128)S(1)}, f32[2,32,8,128]{3,2,1,0:T(8,128)S(1)}, u32[]{:S(2)}, u32[]{:S(2)}) collective-permute-start(f32[2,32,8,128]{3,2,1,0:T(8,128)S(1)} %get-tuple-element.61), channel_id=1, source_target_pairs={{0,2},{1,3},{2,0},{3,1},{4,6},{5,7},{6,4},{7,5},{8,10},{9,11},{10,... | collective-permute-start | bytes 786440 | tf_op jit(solution)/shard_map/ppermute | solution.py:408
  72.4 1.6 %collective-permute-done.16.refs_1_ = f32[2,32,8,128]{3,2,1,0:T(8,128)S(1)} collective-permute-done((f32[2,32,8,128]{3,2,1,0:T(8,128)S(1)}, f32[2,32,8,128]{3,2,1,0:T(8,128)S(1)}, u32[]{:S(2)}, u32[]{:S(2)}) %collective-permute-start.16) | collective-permute-done | bytes 262176 | tf_op jit(solution)/shard_map/ppermute | solution.py:408
  74.0 5.1 %collective-permute-done.17.refs_2_ = f32[2,32,8,128]{3,2,1,0:T(8,128)S(1)} collective-permute-done((f32[2,32,8,128]{3,2,1,0:T(8,128)S(1)}, f32[2,32,8,128]{3,2,1,0:T(8,128)S(1)}, u32[]{:S(2)}, u32[]{:S(2)}) %collective-permute-start.17) | collective-permute-done | bytes 262176 | tf_op jit(solution)/shard_map/ppermute | solution.py:408
  79.1 2.6 %collective-permute-done.18.refs_3_ = f32[2,32,8,128]{3,2,1,0:T(8,128)S(1)} collective-permute-done((f32[2,32,8,128]{3,2,1,0:T(8,128)S(1)}, f32[2,32,8,128]{3,2,1,0:T(8,128)S(1)}, u32[]{:S(2)}, u32[]{:S(2)}) %collective-permute-start.18) | collective-permute-done | bytes 262176 | tf_op jit(solution)/shard_map/ppermute | solution.py:408
  82.7 27.0 %all_to_all.5.sums_ref = f32[256,1,128]{2,1,0:T(1,128)S(1)} all-to-all(f32[256,1,128]{2,1,0:T(1,128)S(1)} %get-tuple-element.64), channel_id=1, replica_groups=mesh['dx'=16,'dy'=4,'band'=4] {'dy','band','dx'}, dimensions={0} | all-to-all | bytes 262144 | tf_op jit(solution)/shard_map/all_to_all | solution.py:464
  110.9 1.5 %collective-permute-start.20 = (f32[2,32,8,128]{3,2,1,0:T(8,128)S(1)}, f32[2,32,8,128]{3,2,1,0:T(8,128)S(1)}, u32[]{:S(2)}, u32[]{:S(2)}) collective-permute-start(f32[2,32,8,128]{3,2,1,0:T(8,128)S(1)} %get-tuple-element.67), channel_id=1, source_target_pairs={{0,2},{1,3},{2,0},{3,1},{4,6},{5,7},{6,4},{7,5},{8,10},{9,11},{10,... | collective-permute-start | bytes 786440 | tf_op jit(solution)/shard_map/ppermute | solution.py:408
  112.5 2.0 %collective-permute-start.21 = (f32[2,32,8,128]{3,2,1,0:T(8,128)S(1)}, f32[2,32,8,128]{3,2,1,0:T(8,128)S(1)}, u32[]{:S(2)}, u32[]{:S(2)}) collective-permute-start(f32[2,32,8,128]{3,2,1,0:T(8,128)S(1)} %get-tuple-element.68), channel_id=1, source_target_pairs={{0,3},{1,2},{2,1},{3,0},{4,7},{5,6},{6,5},{7,4},{8,11},{9,10},{10,... | collective-permute-start | bytes 786440 | tf_op jit(solution)/shard_map/ppermute | solution.py:408
  114.5 3.2 %collective-permute-done.19.refs_1_ = f32[2,32,8,128]{3,2,1,0:T(8,128)S(1)} collective-permute-done((f32[2,32,8,128]{3,2,1,0:T(8,128)S(1)}, f32[2,32,8,128]{3,2,1,0:T(8,128)S(1)}, u32[]{:S(2)}, u32[]{:S(2)}) %collective-permute-start.19) | collective-permute-done | bytes 262176 | tf_op jit(solution)/shard_map/ppermute | solution.py:408
  117.6 6.3 %collective-permute-done.20.refs_2_ = f32[2,32,8,128]{3,2,1,0:T(8,128)S(1)} collective-permute-done((f32[2,32,8,128]{3,2,1,0:T(8,128)S(1)}, f32[2,32,8,128]{3,2,1,0:T(8,128)S(1)}, u32[]{:S(2)}, u32[]{:S(2)}) %collective-permute-start.20) | collective-permute-done | bytes 262176 | tf_op jit(solution)/shard_map/ppermute | solution.py:408
  124.0 2.0 %collective-permute-done.21.refs_3_ = f32[2,32,8,128]{3,2,1,0:T(8,128)S(1)} collective-permute-done((f32[2,32,8,128]{3,2,1,0:T(8,128)S(1)}, f32[2,32,8,128]{3,2,1,0:T(8,128)S(1)}, u32[]{:S(2)}, u32[]{:S(2)}) %collective-permute-start.21) | collective-permute-done | bytes 262176 | tf_op jit(solution)/shard_map/ppermute | solution.py:408
  (37 shorter events, 16.2 us)
Async XLA Ops:
  0.0 1.3 %copy-start = (f32[2,5,80,320]{3,2,1,0:T(8,128)S(1)}, f32[2,5,80,320]{3,2,1,0:T(8,128)}, u32[]{:S(2)}) copy-start(f32[2,5,80,320]{3,2,1,0:T(8,128)} %field_ref.1) | copy-start | bytes 3072004
  1.3 13.1 %copy-start.1 = (f32[5,80,320]{2,1,0:T(8,128)S(1)}, f32[5,80,320]{2,1,0:T(8,128)}, u32[]{:S(2)}) copy-start(f32[5,80,320]{2,1,0:T(8,128)} %refs_1_.1) | copy-start | bytes 1536004
  1.7 16.8 %collective-permute-start = (f32[2,4,25,8,128]{4,3,2,1,0:T(8,128)S(1)}, f32[2,4,25,8,128]{4,3,2,1,0:T(8,128)S(1)}, u32[]{:S(2)}, u32[]{:S(2)}) collective-permute-start(f32[2,4,25,8,128]{4,3,2,1,0:T(8,128)S(1)} %get-tuple-element.39), channel_id=1, source_target_pairs={{0,240},{16,32},{32,16},{48,64},{64,48},{80,96},{96,80},{112,128},... | collective-permute-start | bytes 2457608 | tf_op jit(solution)/shard_map/ppermute | solution.py:408
  4.4 14.1 %collective-permute-start.1 = (f32[2,4,25,8,128]{4,3,2,1,0:T(8,128)S(1)}, f32[2,4,25,8,128]{4,3,2,1,0:T(8,128)S(1)}, u32[]{:S(2)}, u32[]{:S(2)}) collective-permute-start(f32[2,4,25,8,128]{4,3,2,1,0:T(8,128)S(1)} %get-tuple-element.40), channel_id=1, source_target_pairs={{0,16},{16,0},{32,48},{48,32},{64,80},{80,64},{96,112},{112,96},{1... | collective-permute-start | bytes 2457608 | tf_op jit(solution)/shard_map/ppermute | solution.py:408
  6.8 11.6 %collective-permute-start.2 = (f32[104,128]{1,0:T(8,128)S(1)}, f32[104,128]{1,0:T(8,128)S(1)}, u32[]{:S(2)}, u32[]{:S(2)}) collective-permute-start(f32[104,128]{1,0:T(8,128)S(1)} %get-tuple-element.41), channel_id=1, source_target_pairs={{0,4},{4,0},{8,12},{12,8},{1,5},{5,1},{9,13},{13,9},{2,6},{6,2},{1... | collective-permute-start | bytes 159752 | tf_op jit(solution)/shard_map/ppermute | solution.py:408
  9.8 8.6 %collective-permute-start.3 = (f32[104,128]{1,0:T(8,128)S(1)}, f32[104,128]{1,0:T(8,128)S(1)}, u32[]{:S(2)}, u32[]{:S(2)}) collective-permute-start(f32[104,128]{1,0:T(8,128)S(1)} %get-tuple-element.42), channel_id=1, source_target_pairs={{0,12},{4,8},{8,4},{12,0},{1,13},{5,9},{9,5},{13,1},{2,14},{6,10},... | collective-permute-start | bytes 159752 | tf_op jit(solution)/shard_map/ppermute | solution.py:408
  19.3 14.5 %collective-permute-start.4 = (f32[2,4,25,8,128]{4,3,2,1,0:T(8,128)S(1)}, f32[2,4,25,8,128]{4,3,2,1,0:T(8,128)S(1)}, u32[]{:S(2)}, u32[]{:S(2)}) collective-permute-start(f32[2,4,25,8,128]{4,3,2,1,0:T(8,128)S(1)} %get-tuple-element.45), channel_id=1, source_target_pairs={{0,240},{16,32},{32,16},{48,64},{64,48},{80,96},{96,80},{112,128},... | collective-permute-start | bytes 2457608 | tf_op jit(solution)/shard_map/ppermute | solution.py:408
  20.0 13.8 %collective-permute-start.5 = (f32[2,4,25,8,128]{4,3,2,1,0:T(8,128)S(1)}, f32[2,4,25,8,128]{4,3,2,1,0:T(8,128)S(1)}, u32[]{:S(2)}, u32[]{:S(2)}) collective-permute-start(f32[2,4,25,8,128]{4,3,2,1,0:T(8,128)S(1)} %get-tuple-element.46), channel_id=1, source_target_pairs={{0,16},{16,0},{32,48},{48,32},{64,80},{80,64},{96,112},{112,96},{1... | collective-permute-start | bytes 2457608 | tf_op jit(solution)/shard_map/ppermute | solution.py:408
  25.9 7.8 %collective-permute-start.6 = (f32[104,128]{1,0:T(8,128)S(1)}, f32[104,128]{1,0:T(8,128)S(1)}, u32[]{:S(2)}, u32[]{:S(2)}) collective-permute-start(f32[104,128]{1,0:T(8,128)S(1)} %get-tuple-element.47), channel_id=1, source_target_pairs={{0,4},{4,0},{8,12},{12,8},{1,5},{5,1},{9,13},{13,9},{2,6},{6,2},{1... | collective-permute-start | bytes 159752 | tf_op jit(solution)/shard_map/ppermute | solution.py:408
  27.3 6.6 %collective-permute-start.7 = (f32[104,128]{1,0:T(8,128)S(1)}, f32[104,128]{1,0:T(8,128)S(1)}, u32[]{:S(2)}, u32[]{:S(2)}) collective-permute-start(f32[104,128]{1,0:T(8,128)S(1)} %get-tuple-element.48), channel_id=1, source_target_pairs={{0,12},{4,8},{8,4},{12,0},{1,13},{5,9},{9,5},{13,1},{2,14},{6,10},... | collective-permute-start | bytes 159752 | tf_op jit(solution)/shard_map/ppermute | solution.py:408
  34.7 15.6 %collective-permute-start.8 = (f32[2,4,25,8,128]{4,3,2,1,0:T(8,128)S(1)}, f32[2,4,25,8,128]{4,3,2,1,0:T(8,128)S(1)}, u32[]{:S(2)}, u32[]{:S(2)}) collective-permute-start(f32[2,4,25,8,128]{4,3,2,1,0:T(8,128)S(1)} %get-tuple-element.50), channel_id=1, source_target_pairs={{0,240},{16,32},{32,16},{48,64},{64,48},{80,96},{96,80},{112,128},... | collective-permute-start | bytes 2457608 | tf_op jit(solution)/shard_map/ppermute | solution.py:408
  34.8 15.5 %collective-permute-start.9 = (f32[2,4,25,8,128]{4,3,2,1,0:T(8,128)S(1)}, f32[2,4,25,8,128]{4,3,2,1,0:T(8,128)S(1)}, u32[]{:S(2)}, u32[]{:S(2)}) collective-permute-start(f32[2,4,25,8,128]{4,3,2,1,0:T(8,128)S(1)} %get-tuple-element.51), channel_id=1, source_target_pairs={{0,16},{16,0},{32,48},{48,32},{64,80},{80,64},{96,112},{112,96},{1... | collective-permute-start | bytes 2457608 | tf_op jit(solution)/shard_map/ppermute | solution.py:408
  42.4 7.8 %collective-permute-start.10 = (f32[104,128]{1,0:T(8,128)S(1)}, f32[104,128]{1,0:T(8,128)S(1)}, u32[]{:S(2)}, u32[]{:S(2)}) collective-permute-start(f32[104,128]{1,0:T(8,128)S(1)} %get-tuple-element.52), channel_id=1, source_target_pairs={{0,4},{4,0},{8,12},{12,8},{1,5},{5,1},{9,13},{13,9},{2,6},{6,2},{1... | collective-permute-start | bytes 159752 | tf_op jit(solution)/shard_map/ppermute | solution.py:408
  44.0 6.3 %collective-permute-start.11 = (f32[104,128]{1,0:T(8,128)S(1)}, f32[104,128]{1,0:T(8,128)S(1)}, u32[]{:S(2)}, u32[]{:S(2)}) collective-permute-start(f32[104,128]{1,0:T(8,128)S(1)} %get-tuple-element.53), channel_id=1, source_target_pairs={{0,12},{4,8},{8,4},{12,0},{1,13},{5,9},{9,5},{13,1},{2,14},{6,10},... | collective-permute-start | bytes 159752 | tf_op jit(solution)/shard_map/ppermute | solution.py:408
  51.1 16.4 %collective-permute-start.12 = (f32[2,4,25,8,128]{4,3,2,1,0:T(8,128)S(1)}, f32[2,4,25,8,128]{4,3,2,1,0:T(8,128)S(1)}, u32[]{:S(2)}, u32[]{:S(2)}) collective-permute-start(f32[2,4,25,8,128]{4,3,2,1,0:T(8,128)S(1)} %get-tuple-element.55), channel_id=1, source_target_pairs={{0,240},{16,32},{32,16},{48,64},{64,48},{80,96},{96,80},{112,128},... | collective-permute-start | bytes 2457608 | tf_op jit(solution)/shard_map/ppermute | solution.py:408
  51.2 16.3 %collective-permute-start.13 = (f32[2,4,25,8,128]{4,3,2,1,0:T(8,128)S(1)}, f32[2,4,25,8,128]{4,3,2,1,0:T(8,128)S(1)}, u32[]{:S(2)}, u32[]{:S(2)}) collective-permute-start(f32[2,4,25,8,128]{4,3,2,1,0:T(8,128)S(1)} %get-tuple-element.56), channel_id=1, source_target_pairs={{0,16},{16,0},{32,48},{48,32},{64,80},{80,64},{96,112},{112,96},{1... | collective-permute-start | bytes 2457608 | tf_op jit(solution)/shard_map/ppermute | solution.py:408
  60.0 6.7 %collective-permute-start.14 = (f32[104,128]{1,0:T(8,128)S(1)}, f32[104,128]{1,0:T(8,128)S(1)}, u32[]{:S(2)}, u32[]{:S(2)}) collective-permute-start(f32[104,128]{1,0:T(8,128)S(1)} %get-tuple-element.57), channel_id=1, source_target_pairs={{0,4},{4,0},{8,12},{12,8},{1,5},{5,1},{9,13},{13,9},{2,6},{6,2},{1... | collective-permute-start | bytes 159752 | tf_op jit(solution)/shard_map/ppermute | solution.py:408
  61.5 6.0 %collective-permute-start.15 = (f32[104,128]{1,0:T(8,128)S(1)}, f32[104,128]{1,0:T(8,128)S(1)}, u32[]{:S(2)}, u32[]{:S(2)}) collective-permute-start(f32[104,128]{1,0:T(8,128)S(1)} %get-tuple-element.58), channel_id=1, source_target_pairs={{0,12},{4,8},{8,4},{12,0},{1,13},{5,9},{9,5},{13,1},{2,14},{6,10},... | collective-permute-start | bytes 159752 | tf_op jit(solution)/shard_map/ppermute | solution.py:408
  68.4 5.6 %collective-permute-start.16 = (f32[2,32,8,128]{3,2,1,0:T(8,128)S(1)}, f32[2,32,8,128]{3,2,1,0:T(8,128)S(1)}, u32[]{:S(2)}, u32[]{:S(2)}) collective-permute-start(f32[2,32,8,128]{3,2,1,0:T(8,128)S(1)} %get-tuple-element.60), channel_id=1, source_target_pairs={{0,1},{1,0},{2,3},{3,2},{4,5},{5,4},{6,7},{7,6},{8,9},{9,8},{10,11... | collective-permute-start | bytes 786440 | tf_op jit(solution)/shard_map/ppermute | solution.py:408
  69.8 9.3 %collective-permute-start.17 = (f32[2,32,8,128]{3,2,1,0:T(8,128)S(1)}, f32[2,32,8,128]{3,2,1,0:T(8,128)S(1)}, u32[]{:S(2)}, u32[]{:S(2)}) collective-permute-start(f32[2,32,8,128]{3,2,1,0:T(8,128)S(1)} %get-tuple-element.61), channel_id=1, source_target_pairs={{0,2},{1,3},{2,0},{3,1},{4,6},{5,7},{6,4},{7,5},{8,10},{9,11},{10,... | collective-permute-start | bytes 786440 | tf_op jit(solution)/shard_map/ppermute | solution.py:408
  72.4 9.2 %collective-permute-start.18 = (f32[2,32,8,128]{3,2,1,0:T(8,128)S(1)}, f32[2,32,8,128]{3,2,1,0:T(8,128)S(1)}, u32[]{:S(2)}, u32[]{:S(2)}) collective-permute-start(f32[2,32,8,128]{3,2,1,0:T(8,128)S(1)} %get-tuple-element.62), channel_id=1, source_target_pairs={{0,3},{1,2},{2,1},{3,0},{4,7},{5,6},{6,5},{7,4},{8,11},{9,10},{10,... | collective-permute-start | bytes 786440 | tf_op jit(solution)/shard_map/ppermute | solution.py:408
  110.5 7.1 %collective-permute-start.19 = (f32[2,32,8,128]{3,2,1,0:T(8,128)S(1)}, f32[2,32,8,128]{3,2,1,0:T(8,128)S(1)}, u32[]{:S(2)}, u32[]{:S(2)}) collective-permute-start(f32[2,32,8,128]{3,2,1,0:T(8,128)S(1)} %get-tuple-element.66), channel_id=1, source_target_pairs={{0,1},{1,0},{2,3},{3,2},{4,5},{5,4},{6,7},{7,6},{8,9},{9,8},{10,11... | collective-permute-start | bytes 786440 | tf_op jit(solution)/shard_map/ppermute | solution.py:408
  110.9 13.0 %collective-permute-start.20 = (f32[2,32,8,128]{3,2,1,0:T(8,128)S(1)}, f32[2,32,8,128]{3,2,1,0:T(8,128)S(1)}, u32[]{:S(2)}, u32[]{:S(2)}) collective-permute-start(f32[2,32,8,128]{3,2,1,0:T(8,128)S(1)} %get-tuple-element.67), channel_id=1, source_target_pairs={{0,2},{1,3},{2,0},{3,1},{4,6},{5,7},{6,4},{7,5},{8,10},{9,11},{10,... | collective-permute-start | bytes 786440 | tf_op jit(solution)/shard_map/ppermute | solution.py:408
  112.5 13.5 %collective-permute-start.21 = (f32[2,32,8,128]{3,2,1,0:T(8,128)S(1)}, f32[2,32,8,128]{3,2,1,0:T(8,128)S(1)}, u32[]{:S(2)}, u32[]{:S(2)}) collective-permute-start(f32[2,32,8,128]{3,2,1,0:T(8,128)S(1)} %get-tuple-element.68), channel_id=1, source_target_pairs={{0,3},{1,2},{2,1},{3,0},{4,7},{5,6},{6,5},{7,4},{8,11},{9,10},{10,... | collective-permute-start | bytes 786440 | tf_op jit(solution)/shard_map/ppermute | solution.py:408

commit v4 on v3

--- a/solution.py
+++ b/solution.py
@@ -316,11 +316,13 @@
     *piece_refs, whole_ref, sums_ref, row_ref = refs
     collect(piece_refs, whole_ref)
 
-    def accumulate(at, totals):
-        cells = [whole_ref[a // BANDS, a % BANDS, at] for a in range(GROUPS * BANDS)]
-        return tuple(total + cells[a] * cells[b] for total, (a, b) in zip(totals, PAIRS))
-
-    totals = lax.fori_loop(0, 32, accumulate, tuple(jnp.zeros((8, 128), F32) for _ in PAIRS))
+    def accumulate(quad, totals):
+        for part in range(4):
+            cells = [whole_ref[a // BANDS, a % BANDS, quad * 4 + part] for a in range(GROUPS * BANDS)]
+            totals = tuple(total + cells[a] * cells[b] for total, (a, b) in zip(totals, PAIRS))
+        return totals
+
+    totals = lax.fori_loop(0, 8, accumulate, tuple(jnp.zeros((8, 128), F32) for _ in PAIRS))
     row_ref[...] = jnp.zeros_like(row_ref)
     for at, total in enumerate(totals):
         row_ref[at : at + 1, :] = jnp.sum(total, axis=0, keepdims=True)
@@ -366,16 +368,18 @@
                 running = running + factor[target, source] * inverse[source, a]
             inverse[target, a] = -running * scale[target]
 
-    def turn(at, carry):
-        cells = [whole_ref[a // BANDS, a % BANDS, at] for a in range(extent)]
-        for j in range(extent):
-            total = inverse[j, 0] * cells[0]
-            for a in range(1, j + 1):
-                total = total + inverse[j, a] * cells[a]
-            turned_ref[j // BANDS, j % BANDS, at] = total
+    def turn(quad, carry):
+        for part in range(4):
+            at = quad * 4 + part
+            cells = [whole_ref[a // BANDS, a % BANDS, at] for a in range(extent)]
+            for j in range(extent):
+                total = inverse[j, 0] * cells[0]
+                for a in range(1, j + 1):
+                    total = total + inverse[j, a] * cells[a]
+                turned_ref[j // BANDS, j % BANDS, at] = total
         return carry
 
-    lax.fori_loop(0, 32, turn, 0)
+    lax.fori_loop(0, 8, turn, 0)
     deal(turned_ref, piece_refs)
 
 

time: 128 us -> 127 us (level)
  no operation moved by 1% of the time
where the time goes in v4:
time: 127 us
  starting transfers between devices  52.7 us (41%)
  blocking collectives  27 us (21%)
  Pallas kernels  22.5 us (18%)
  waiting for transfers between devices  21.9 us (17%)
  between operations  1.63 us (1%)
  local copies, waits for them, and re-layouts  1.29 us (1%)
    ppermute x22, starting transfers between devices, swapped(): lax.ppermute(array, axis, [(i, partner(i)) for i in range(lax.axis_size(a...  52.7 us
    all_to_all x1, blocking collectives, local(): sums = lax.all_to_all(sums, ('dy', 'band', 'dx'), 0, 0)  27 us
    ppermute x22, waiting for transfers between devices, swapped(): lax.ppermute(array, axis, [(i, partner(i)) for i in range(lax.axis_size(a...  21.9 us
    pallas_call x3, Pallas kernels, local(): call(functools.partial(inner_kernel, False), (STATE,), scratch=(wide,))  12 us
    pallas_call x1, Pallas kernels, local(): call(functools.partial(inner_kernel, True), (STATE, STATE[1:]), scratch=(...  4.02 us
  transfers between devices with their start and end apart: 22, of which 9 were waited for; matrix products, arithmetic and copies ran while one was open for 0% of the time, Pallas kernels for 13%

profile of v4, /device:TPU:1, one launch (start us, length us, event | category | flops | bytes accessed | tf_op | source)
XLA Modules:
  0.0 127.0 jit_solution(15135529956604699958)
XLA Ops:
  1.7 2.7 %collective-permute-start = (f32[2,4,25,8,128]{4,3,2,1,0:T(8,128)S(1)}, f32[2,4,25,8,128]{4,3,2,1,0:T(8,128)S(1)}, u32[]{:S(2)}, u32[]{:S(2)}) collective-permute-start(f32[2,4,25,8,128]{4,3,2,1,0:T(8,128)S(1)} %get-tuple-element.39), channel_id=1, source_target_pairs={{0,240},{16,32},{32,16},{48,64},{64,48},{80,96},{96,80},{112,128},... | collective-permute-start | bytes 2457608 | tf_op jit(solution)/shard_map/ppermute | solution.py:412
  4.4 2.5 %collective-permute-start.1 = (f32[2,4,25,8,128]{4,3,2,1,0:T(8,128)S(1)}, f32[2,4,25,8,128]{4,3,2,1,0:T(8,128)S(1)}, u32[]{:S(2)}, u32[]{:S(2)}) collective-permute-start(f32[2,4,25,8,128]{4,3,2,1,0:T(8,128)S(1)} %get-tuple-element.40), channel_id=1, source_target_pairs={{0,16},{16,0},{32,48},{48,32},{64,80},{80,64},{96,112},{112,96},{1... | collective-permute-start | bytes 2457608 | tf_op jit(solution)/shard_map/ppermute | solution.py:412
  6.8 3.0 %collective-permute-start.2 = (f32[104,128]{1,0:T(8,128)S(1)}, f32[104,128]{1,0:T(8,128)S(1)}, u32[]{:S(2)}, u32[]{:S(2)}) collective-permute-start(f32[104,128]{1,0:T(8,128)S(1)} %get-tuple-element.41), channel_id=1, source_target_pairs={{0,4},{4,0},{8,12},{12,8},{1,5},{5,1},{9,13},{13,9},{2,6},{6,2},{1... | collective-permute-start | bytes 159752 | tf_op jit(solution)/shard_map/ppermute | solution.py:412
  9.8 3.3 %collective-permute-start.3 = (f32[104,128]{1,0:T(8,128)S(1)}, f32[104,128]{1,0:T(8,128)S(1)}, u32[]{:S(2)}, u32[]{:S(2)}) collective-permute-start(f32[104,128]{1,0:T(8,128)S(1)} %get-tuple-element.42), channel_id=1, source_target_pairs={{0,12},{4,8},{8,4},{12,0},{1,13},{5,9},{9,5},{13,1},{2,14},{6,10},... | collective-permute-start | bytes 159752 | tf_op jit(solution)/shard_map/ppermute | solution.py:412
  14.4 4.0 %shard_map.47 = (f32[2,5,3,10,8,128]{5,4,3,2,1,0:T(8,128)S(1)}, f32[5,3,10,8,128]{4,3,2,1,0:T(8,128)S(1)}) custom-call(f32[2,5,3,10,8,128]{5,4,3,2,1,0:T(8,128)S(1)} %get-tuple-element.37.refs_0_.refs_1_, f32[5,80,320]{2,1,0:T(8,128)S(1)} %copy-done.1, f32[1,1]{1,0:T(1,128)} %bitcast.2.refs_2_, f32[1,1]{1,0:T(1,128)} %bitcast.10.refs_3_), custom_call_target="tpu_custom_call" | custom-call | flops 4000000 | bytes 4000000 | tf_op jit(solution)/shard_map/pallas_call | solution.py:444
  20.0 5.8 %collective-permute-start.5 = (f32[2,4,25,8,128]{4,3,2,1,0:T(8,128)S(1)}, f32[2,4,25,8,128]{4,3,2,1,0:T(8,128)S(1)}, u32[]{:S(2)}, u32[]{:S(2)}) collective-permute-start(f32[2,4,25,8,128]{4,3,2,1,0:T(8,128)S(1)} %get-tuple-element.46), channel_id=1, source_target_pairs={{0,16},{16,0},{32,48},{48,32},{64,80},{80,64},{96,112},{112,96},{1... | collective-permute-start | bytes 2457608 | tf_op jit(solution)/shard_map/ppermute | solution.py:412
  27.3 2.3 %collective-permute-start.7 = (f32[104,128]{1,0:T(8,128)S(1)}, f32[104,128]{1,0:T(8,128)S(1)}, u32[]{:S(2)}, u32[]{:S(2)}) collective-permute-start(f32[104,128]{1,0:T(8,128)S(1)} %get-tuple-element.48), channel_id=1, source_target_pairs={{0,12},{4,8},{8,4},{12,0},{1,13},{5,9},{9,5},{13,1},{2,14},{6,10},... | collective-permute-start | bytes 159752 | tf_op jit(solution)/shard_map/ppermute | solution.py:412
  29.6 4.0 %shard_map.49.refs_0_ = f32[2,5,3,10,8,128]{5,4,3,2,1,0:T(8,128)S(1)} custom-call(f32[2,5,3,10,8,128]{5,4,3,2,1,0:T(8,128)S(1)} %get-tuple-element.43.refs_0_.refs_1_, f32[2,5,3,10,8,128]{5,4,3,2,1,0:T(8,128)S(1)} %get-tuple-element.37.refs_0_.refs_1_, f32[5,3,10,8,128]{4,3,2,1,0:T(8,128)S(1)} %get-tuple-element.44.refs_2_, f32[1,1]{1,0:T(1,128)} %bitcast.4.refs_3_, ...), custom_call_target="tpu_custom_call" | custom-call | flops 4000000 | bytes 4000000 | tf_op jit(solution)/shard_map/pallas_call | solution.py:448
  34.8 7.6 %collective-permute-start.9 = (f32[2,4,25,8,128]{4,3,2,1,0:T(8,128)S(1)}, f32[2,4,25,8,128]{4,3,2,1,0:T(8,128)S(1)}, u32[]{:S(2)}, u32[]{:S(2)}) collective-permute-start(f32[2,4,25,8,128]{4,3,2,1,0:T(8,128)S(1)} %get-tuple-element.51), channel_id=1, source_target_pairs={{0,16},{16,0},{32,48},{48,32},{64,80},{80,64},{96,112},{112,96},{1... | collective-permute-start | bytes 2457608 | tf_op jit(solution)/shard_map/ppermute | solution.py:412
  42.4 1.6 %collective-permute-start.10 = (f32[104,128]{1,0:T(8,128)S(1)}, f32[104,128]{1,0:T(8,128)S(1)}, u32[]{:S(2)}, u32[]{:S(2)}) collective-permute-start(f32[104,128]{1,0:T(8,128)S(1)} %get-tuple-element.52), channel_id=1, source_target_pairs={{0,4},{4,0},{8,12},{12,8},{1,5},{5,1},{9,13},{13,9},{2,6},{6,2},{1... | collective-permute-start | bytes 159752 | tf_op jit(solution)/shard_map/ppermute | solution.py:412
  44.0 2.1 %collective-permute-start.11 = (f32[104,128]{1,0:T(8,128)S(1)}, f32[104,128]{1,0:T(8,128)S(1)}, u32[]{:S(2)}, u32[]{:S(2)}) collective-permute-start(f32[104,128]{1,0:T(8,128)S(1)} %get-tuple-element.53), channel_id=1, source_target_pairs={{0,12},{4,8},{8,4},{12,0},{1,13},{5,9},{9,5},{13,1},{2,14},{6,10},... | collective-permute-start | bytes 159752 | tf_op jit(solution)/shard_map/ppermute | solution.py:412
  46.1 4.0 %shard_map.51.refs_0_ = f32[2,5,3,10,8,128]{5,4,3,2,1,0:T(8,128)S(1)} custom-call(f32[2,5,3,10,8,128]{5,4,3,2,1,0:T(8,128)S(1)} %get-tuple-element.49.refs_0_.refs_1_, f32[2,5,3,10,8,128]{5,4,3,2,1,0:T(8,128)S(1)} %get-tuple-element.43.refs_0_.refs_1_, f32[5,3,10,8,128]{4,3,2,1,0:T(8,128)S(1)} %get-tuple-element.44.refs_2_, f32[1,1]{1,0:T(1,128)} %bitcast.6.refs_3_, ...), custom_call_target="tpu_custom_call" | custom-call | flops 4000000 | bytes 4000000 | tf_op jit(solution)/shard_map/pallas_call | solution.py:448
  51.2 8.8 %collective-permute-start.13 = (f32[2,4,25,8,128]{4,3,2,1,0:T(8,128)S(1)}, f32[2,4,25,8,128]{4,3,2,1,0:T(8,128)S(1)}, u32[]{:S(2)}, u32[]{:S(2)}) collective-permute-start(f32[2,4,25,8,128]{4,3,2,1,0:T(8,128)S(1)} %get-tuple-element.56), channel_id=1, source_target_pairs={{0,16},{16,0},{32,48},{48,32},{64,80},{80,64},{96,112},{112,96},{1... | collective-permute-start | bytes 2457608 | tf_op jit(solution)/shard_map/ppermute | solution.py:412
  62.7 4.0 %shard_map.53.refs_0_ = f32[2,5,3,10,8,128]{5,4,3,2,1,0:T(8,128)S(1)} custom-call(f32[2,5,3,10,8,128]{5,4,3,2,1,0:T(8,128)S(1)} %get-tuple-element.54.refs_0_, f32[2,5,3,10,8,128]{5,4,3,2,1,0:T(8,128)S(1)} %get-tuple-element.49.refs_0_.refs_1_, f32[5,3,10,8,128]{4,3,2,1,0:T(8,128)S(1)} %get-tuple-element.44.refs_2_, f32[1,1]{1,0:T(1,128)} %bitcast.8.refs_3_, ...), custom_call_target="tpu_custom_call" | custom-call | flops 4000000 | bytes 4000000 | tf_op jit(solution)/shard_map/pallas_call | solution.py:448
  69.8 2.6 %collective-permute-start.17 = (f32[2,32,8,128]{3,2,1,0:T(8,128)S(1)}, f32[2,32,8,128]{3,2,1,0:T(8,128)S(1)}, u32[]{:S(2)}, u32[]{:S(2)}) collective-permute-start(f32[2,32,8,128]{3,2,1,0:T(8,128)S(1)} %get-tuple-element.61), channel_id=1, source_target_pairs={{0,2},{1,3},{2,0},{3,1},{4,6},{5,7},{6,4},{7,5},{8,10},{9,11},{10,... | collective-permute-start | bytes 786440 | tf_op jit(solution)/shard_map/ppermute | solution.py:412
  72.4 1.6 %collective-permute-done.16.refs_1_ = f32[2,32,8,128]{3,2,1,0:T(8,128)S(1)} collective-permute-done((f32[2,32,8,128]{3,2,1,0:T(8,128)S(1)}, f32[2,32,8,128]{3,2,1,0:T(8,128)S(1)}, u32[]{:S(2)}, u32[]{:S(2)}) %collective-permute-start.16) | collective-permute-done | bytes 262176 | tf_op jit(solution)/shard_map/ppermute | solution.py:412
  74.0 5.1 %collective-permute-done.17.refs_2_ = f32[2,32,8,128]{3,2,1,0:T(8,128)S(1)} collective-permute-done((f32[2,32,8,128]{3,2,1,0:T(8,128)S(1)}, f32[2,32,8,128]{3,2,1,0:T(8,128)S(1)}, u32[]{:S(2)}, u32[]{:S(2)}) %collective-permute-start.17) | collective-permute-done | bytes 262176 | tf_op jit(solution)/shard_map/ppermute | solution.py:412
  79.1 2.6 %collective-permute-done.18.refs_3_ = f32[2,32,8,128]{3,2,1,0:T(8,128)S(1)} collective-permute-done((f32[2,32,8,128]{3,2,1,0:T(8,128)S(1)}, f32[2,32,8,128]{3,2,1,0:T(8,128)S(1)}, u32[]{:S(2)}, u32[]{:S(2)}) %collective-permute-start.18) | collective-permute-done | bytes 262176 | tf_op jit(solution)/shard_map/ppermute | solution.py:412
  82.4 27.0 %all_to_all.5.sums_ref = f32[256,1,128]{2,1,0:T(1,128)S(1)} all-to-all(f32[256,1,128]{2,1,0:T(1,128)S(1)} %get-tuple-element.64), channel_id=1, replica_groups=mesh['dx'=16,'dy'=4,'band'=4] {'dy','band','dx'}, dimensions={0} | all-to-all | bytes 262144 | tf_op jit(solution)/shard_map/all_to_all | solution.py:468
  110.5 1.5 %collective-permute-start.20 = (f32[2,32,8,128]{3,2,1,0:T(8,128)S(1)}, f32[2,32,8,128]{3,2,1,0:T(8,128)S(1)}, u32[]{:S(2)}, u32[]{:S(2)}) collective-permute-start(f32[2,32,8,128]{3,2,1,0:T(8,128)S(1)} %get-tuple-element.67), channel_id=1, source_target_pairs={{0,2},{1,3},{2,0},{3,1},{4,6},{5,7},{6,4},{7,5},{8,10},{9,11},{10,... | collective-permute-start | bytes 786440 | tf_op jit(solution)/shard_map/ppermute | solution.py:412
  112.0 2.0 %collective-permute-start.21 = (f32[2,32,8,128]{3,2,1,0:T(8,128)S(1)}, f32[2,32,8,128]{3,2,1,0:T(8,128)S(1)}, u32[]{:S(2)}, u32[]{:S(2)}) collective-permute-start(f32[2,32,8,128]{3,2,1,0:T(8,128)S(1)} %get-tuple-element.68), channel_id=1, source_target_pairs={{0,3},{1,2},{2,1},{3,0},{4,7},{5,6},{6,5},{7,4},{8,11},{9,10},{10,... | collective-permute-start | bytes 786440 | tf_op jit(solution)/shard_map/ppermute | solution.py:412
  114.1 3.2 %collective-permute-done.19.refs_1_ = f32[2,32,8,128]{3,2,1,0:T(8,128)S(1)} collective-permute-done((f32[2,32,8,128]{3,2,1,0:T(8,128)S(1)}, f32[2,32,8,128]{3,2,1,0:T(8,128)S(1)}, u32[]{:S(2)}, u32[]{:S(2)}) %collective-permute-start.19) | collective-permute-done | bytes 262176 | tf_op jit(solution)/shard_map/ppermute | solution.py:412
  117.2 6.3 %collective-permute-done.20.refs_2_ = f32[2,32,8,128]{3,2,1,0:T(8,128)S(1)} collective-permute-done((f32[2,32,8,128]{3,2,1,0:T(8,128)S(1)}, f32[2,32,8,128]{3,2,1,0:T(8,128)S(1)}, u32[]{:S(2)}, u32[]{:S(2)}) %collective-permute-start.20) | collective-permute-done | bytes 262176 | tf_op jit(solution)/shard_map/ppermute | solution.py:412
  123.5 2.0 %collective-permute-done.21.refs_3_ = f32[2,32,8,128]{3,2,1,0:T(8,128)S(1)} collective-permute-done((f32[2,32,8,128]{3,2,1,0:T(8,128)S(1)}, f32[2,32,8,128]{3,2,1,0:T(8,128)S(1)}, u32[]{:S(2)}, u32[]{:S(2)}) %collective-permute-start.21) | collective-permute-done | bytes 262176 | tf_op jit(solution)/shard_map/ppermute | solution.py:412
  (37 shorter events, 15.7 us)
Async XLA Ops:
  0.0 1.3 %copy-start = (f32[2,5,80,320]{3,2,1,0:T(8,128)S(1)}, f32[2,5,80,320]{3,2,1,0:T(8,128)}, u32[]{:S(2)}) copy-start(f32[2,5,80,320]{3,2,1,0:T(8,128)} %field_ref.1) | copy-start | bytes 3072004
  1.3 13.1 %copy-start.1 = (f32[5,80,320]{2,1,0:T(8,128)S(1)}, f32[5,80,320]{2,1,0:T(8,128)}, u32[]{:S(2)}) copy-start(f32[5,80,320]{2,1,0:T(8,128)} %refs_1_.1) | copy-start | bytes 1536004
  1.7 16.8 %collective-permute-start = (f32[2,4,25,8,128]{4,3,2,1,0:T(8,128)S(1)}, f32[2,4,25,8,128]{4,3,2,1,0:T(8,128)S(1)}, u32[]{:S(2)}, u32[]{:S(2)}) collective-permute-start(f32[2,4,25,8,128]{4,3,2,1,0:T(8,128)S(1)} %get-tuple-element.39), channel_id=1, source_target_pairs={{0,240},{16,32},{32,16},{48,64},{64,48},{80,96},{96,80},{112,128},... | collective-permute-start | bytes 2457608 | tf_op jit(solution)/shard_map/ppermute | solution.py:412
  4.4 14.1 %collective-permute-start.1 = (f32[2,4,25,8,128]{4,3,2,1,0:T(8,128)S(1)}, f32[2,4,25,8,128]{4,3,2,1,0:T(8,128)S(1)}, u32[]{:S(2)}, u32[]{:S(2)}) collective-permute-start(f32[2,4,25,8,128]{4,3,2,1,0:T(8,128)S(1)} %get-tuple-element.40), channel_id=1, source_target_pairs={{0,16},{16,0},{32,48},{48,32},{64,80},{80,64},{96,112},{112,96},{1... | collective-permute-start | bytes 2457608 | tf_op jit(solution)/shard_map/ppermute | solution.py:412
  6.8 11.6 %collective-permute-start.2 = (f32[104,128]{1,0:T(8,128)S(1)}, f32[104,128]{1,0:T(8,128)S(1)}, u32[]{:S(2)}, u32[]{:S(2)}) collective-permute-start(f32[104,128]{1,0:T(8,128)S(1)} %get-tuple-element.41), channel_id=1, source_target_pairs={{0,4},{4,0},{8,12},{12,8},{1,5},{5,1},{9,13},{13,9},{2,6},{6,2},{1... | collective-permute-start | bytes 159752 | tf_op jit(solution)/shard_map/ppermute | solution.py:412
  9.8 8.6 %collective-permute-start.3 = (f32[104,128]{1,0:T(8,128)S(1)}, f32[104,128]{1,0:T(8,128)S(1)}, u32[]{:S(2)}, u32[]{:S(2)}) collective-permute-start(f32[104,128]{1,0:T(8,128)S(1)} %get-tuple-element.42), channel_id=1, source_target_pairs={{0,12},{4,8},{8,4},{12,0},{1,13},{5,9},{9,5},{13,1},{2,14},{6,10},... | collective-permute-start | bytes 159752 | tf_op jit(solution)/shard_map/ppermute | solution.py:412
  19.3 14.5 %collective-permute-start.4 = (f32[2,4,25,8,128]{4,3,2,1,0:T(8,128)S(1)}, f32[2,4,25,8,128]{4,3,2,1,0:T(8,128)S(1)}, u32[]{:S(2)}, u32[]{:S(2)}) collective-permute-start(f32[2,4,25,8,128]{4,3,2,1,0:T(8,128)S(1)} %get-tuple-element.45), channel_id=1, source_target_pairs={{0,240},{16,32},{32,16},{48,64},{64,48},{80,96},{96,80},{112,128},... | collective-permute-start | bytes 2457608 | tf_op jit(solution)/shard_map/ppermute | solution.py:412
  20.0 13.8 %collective-permute-start.5 = (f32[2,4,25,8,128]{4,3,2,1,0:T(8,128)S(1)}, f32[2,4,25,8,128]{4,3,2,1,0:T(8,128)S(1)}, u32[]{:S(2)}, u32[]{:S(2)}) collective-permute-start(f32[2,4,25,8,128]{4,3,2,1,0:T(8,128)S(1)} %get-tuple-element.46), channel_id=1, source_target_pairs={{0,16},{16,0},{32,48},{48,32},{64,80},{80,64},{96,112},{112,96},{1... | collective-permute-start | bytes 2457608 | tf_op jit(solution)/shard_map/ppermute | solution.py:412
  25.9 7.8 %collective-permute-start.6 = (f32[104,128]{1,0:T(8,128)S(1)}, f32[104,128]{1,0:T(8,128)S(1)}, u32[]{:S(2)}, u32[]{:S(2)}) collective-permute-start(f32[104,128]{1,0:T(8,128)S(1)} %get-tuple-element.47), channel_id=1, source_target_pairs={{0,4},{4,0},{8,12},{12,8},{1,5},{5,1},{9,13},{13,9},{2,6},{6,2},{1... | collective-permute-start | bytes 159752 | tf_op jit(solution)/shard_map/ppermute | solution.py:412
  27.3 6.6 %collective-permute-start.7 = (f32[104,128]{1,0:T(8,128)S(1)}, f32[104,128]{1,0:T(8,128)S(1)}, u32[]{:S(2)}, u32[]{:S(2)}) collective-permute-start(f32[104,128]{1,0:T(8,128)S(1)} %get-tuple-element.48), channel_id=1, source_target_pairs={{0,12},{4,8},{8,4},{12,0},{1,13},{5,9},{9,5},{13,1},{2,14},{6,10},... | collective-permute-start | bytes 159752 | tf_op jit(solution)/shard_map/ppermute | solution.py:412
  34.7 15.6 %collective-permute-start.8 = (f32[2,4,25,8,128]{4,3,2,1,0:T(8,128)S(1)}, f32[2,4,25,8,128]{4,3,2,1,0:T(8,128)S(1)}, u32[]{:S(2)}, u32[]{:S(2)}) collective-permute-start(f32[2,4,25,8,128]{4,3,2,1,0:T(8,128)S(1)} %get-tuple-element.50), channel_id=1, source_target_pairs={{0,240},{16,32},{32,16},{48,64},{64,48},{80,96},{96,80},{112,128},... | collective-permute-start | bytes 2457608 | tf_op jit(solution)/shard_map/ppermute | solution.py:412
  34.8 15.5 %collective-permute-start.9 = (f32[2,4,25,8,128]{4,3,2,1,0:T(8,128)S(1)}, f32[2,4,25,8,128]{4,3,2,1,0:T(8,128)S(1)}, u32[]{:S(2)}, u32[]{:S(2)}) collective-permute-start(f32[2,4,25,8,128]{4,3,2,1,0:T(8,128)S(1)} %get-tuple-element.51), channel_id=1, source_target_pairs={{0,16},{16,0},{32,48},{48,32},{64,80},{80,64},{96,112},{112,96},{1... | collective-permute-start | bytes 2457608 | tf_op jit(solution)/shard_map/ppermute | solution.py:412
  42.4 7.8 %collective-permute-start.10 = (f32[104,128]{1,0:T(8,128)S(1)}, f32[104,128]{1,0:T(8,128)S(1)}, u32[]{:S(2)}, u32[]{:S(2)}) collective-permute-start(f32[104,128]{1,0:T(8,128)S(1)} %get-tuple-element.52), channel_id=1, source_target_pairs={{0,4},{4,0},{8,12},{12,8},{1,5},{5,1},{9,13},{13,9},{2,6},{6,2},{1... | collective-permute-start | bytes 159752 | tf_op jit(solution)/shard_map/ppermute | solution.py:412
  44.0 6.3 %collective-permute-start.11 = (f32[104,128]{1,0:T(8,128)S(1)}, f32[104,128]{1,0:T(8,128)S(1)}, u32[]{:S(2)}, u32[]{:S(2)}) collective-permute-start(f32[104,128]{1,0:T(8,128)S(1)} %get-tuple-element.53), channel_id=1, source_target_pairs={{0,12},{4,8},{8,4},{12,0},{1,13},{5,9},{9,5},{13,1},{2,14},{6,10},... | collective-permute-start | bytes 159752 | tf_op jit(solution)/shard_map/ppermute | solution.py:412
  51.1 16.4 %collective-permute-start.12 = (f32[2,4,25,8,128]{4,3,2,1,0:T(8,128)S(1)}, f32[2,4,25,8,128]{4,3,2,1,0:T(8,128)S(1)}, u32[]{:S(2)}, u32[]{:S(2)}) collective-permute-start(f32[2,4,25,8,128]{4,3,2,1,0:T(8,128)S(1)} %get-tuple-element.55), channel_id=1, source_target_pairs={{0,240},{16,32},{32,16},{48,64},{64,48},{80,96},{96,80},{112,128},... | collective-permute-start | bytes 2457608 | tf_op jit(solution)/shard_map/ppermute | solution.py:412
  51.2 16.3 %collective-permute-start.13 = (f32[2,4,25,8,128]{4,3,2,1,0:T(8,128)S(1)}, f32[2,4,25,8,128]{4,3,2,1,0:T(8,128)S(1)}, u32[]{:S(2)}, u32[]{:S(2)}) collective-permute-start(f32[2,4,25,8,128]{4,3,2,1,0:T(8,128)S(1)} %get-tuple-element.56), channel_id=1, source_target_pairs={{0,16},{16,0},{32,48},{48,32},{64,80},{80,64},{96,112},{112,96},{1... | collective-permute-start | bytes 2457608 | tf_op jit(solution)/shard_map/ppermute | solution.py:412
  60.0 6.7 %collective-permute-start.14 = (f32[104,128]{1,0:T(8,128)S(1)}, f32[104,128]{1,0:T(8,128)S(1)}, u32[]{:S(2)}, u32[]{:S(2)}) collective-permute-start(f32[104,128]{1,0:T(8,128)S(1)} %get-tuple-element.57), channel_id=1, source_target_pairs={{0,4},{4,0},{8,12},{12,8},{1,5},{5,1},{9,13},{13,9},{2,6},{6,2},{1... | collective-permute-start | bytes 159752 | tf_op jit(solution)/shard_map/ppermute | solution.py:412
  61.5 6.0 %collective-permute-start.15 = (f32[104,128]{1,0:T(8,128)S(1)}, f32[104,128]{1,0:T(8,128)S(1)}, u32[]{:S(2)}, u32[]{:S(2)}) collective-permute-start(f32[104,128]{1,0:T(8,128)S(1)} %get-tuple-element.58), channel_id=1, source_target_pairs={{0,12},{4,8},{8,4},{12,0},{1,13},{5,9},{9,5},{13,1},{2,14},{6,10},... | collective-permute-start | bytes 159752 | tf_op jit(solution)/shard_map/ppermute | solution.py:412
  68.4 5.6 %collective-permute-start.16 = (f32[2,32,8,128]{3,2,1,0:T(8,128)S(1)}, f32[2,32,8,128]{3,2,1,0:T(8,128)S(1)}, u32[]{:S(2)}, u32[]{:S(2)}) collective-permute-start(f32[2,32,8,128]{3,2,1,0:T(8,128)S(1)} %get-tuple-element.60), channel_id=1, source_target_pairs={{0,1},{1,0},{2,3},{3,2},{4,5},{5,4},{6,7},{7,6},{8,9},{9,8},{10,11... | collective-permute-start | bytes 786440 | tf_op jit(solution)/shard_map/ppermute | solution.py:412
  69.8 9.3 %collective-permute-start.17 = (f32[2,32,8,128]{3,2,1,0:T(8,128)S(1)}, f32[2,32,8,128]{3,2,1,0:T(8,128)S(1)}, u32[]{:S(2)}, u32[]{:S(2)}) collective-permute-start(f32[2,32,8,128]{3,2,1,0:T(8,128)S(1)} %get-tuple-element.61), channel_id=1, source_target_pairs={{0,2},{1,3},{2,0},{3,1},{4,6},{5,7},{6,4},{7,5},{8,10},{9,11},{10,... | collective-permute-start | bytes 786440 | tf_op jit(solution)/shard_map/ppermute | solution.py:412
  72.4 9.2 %collective-permute-start.18 = (f32[2,32,8,128]{3,2,1,0:T(8,128)S(1)}, f32[2,32,8,128]{3,2,1,0:T(8,128)S(1)}, u32[]{:S(2)}, u32[]{:S(2)}) collective-permute-start(f32[2,32,8,128]{3,2,1,0:T(8,128)S(1)} %get-tuple-element.62), channel_id=1, source_target_pairs={{0,3},{1,2},{2,1},{3,0},{4,7},{5,6},{6,5},{7,4},{8,11},{9,10},{10,... | collective-permute-start | bytes 786440 | tf_op jit(solution)/shard_map/ppermute | solution.py:412
  110.1 7.1 %collective-permute-start.19 = (f32[2,32,8,128]{3,2,1,0:T(8,128)S(1)}, f32[2,32,8,128]{3,2,1,0:T(8,128)S(1)}, u32[]{:S(2)}, u32[]{:S(2)}) collective-permute-start(f32[2,32,8,128]{3,2,1,0:T(8,128)S(1)} %get-tuple-element.66), channel_id=1, source_target_pairs={{0,1},{1,0},{2,3},{3,2},{4,5},{5,4},{6,7},{7,6},{8,9},{9,8},{10,11... | collective-permute-start | bytes 786440 | tf_op jit(solution)/shard_map/ppermute | solution.py:412
  110.5 13.0 %collective-permute-start.20 = (f32[2,32,8,128]{3,2,1,0:T(8,128)S(1)}, f32[2,32,8,128]{3,2,1,0:T(8,128)S(1)}, u32[]{:S(2)}, u32[]{:S(2)}) collective-permute-start(f32[2,32,8,128]{3,2,1,0:T(8,128)S(1)} %get-tuple-element.67), channel_id=1, source_target_pairs={{0,2},{1,3},{2,0},{3,1},{4,6},{5,7},{6,4},{7,5},{8,10},{9,11},{10,... | collective-permute-start | bytes 786440 | tf_op jit(solution)/shard_map/ppermute | solution.py:412
  112.0 13.5 %collective-permute-start.21 = (f32[2,32,8,128]{3,2,1,0:T(8,128)S(1)}, f32[2,32,8,128]{3,2,1,0:T(8,128)S(1)}, u32[]{:S(2)}, u32[]{:S(2)}) collective-permute-start(f32[2,32,8,128]{3,2,1,0:T(8,128)S(1)} %get-tuple-element.68), channel_id=1, source_target_pairs={{0,3},{1,2},{2,1},{3,0},{4,7},{5,6},{6,5},{7,4},{8,11},{9,10},{10,... | collective-permute-start | bytes 786440 | tf_op jit(solution)/shard_map/ppermute | solution.py:412

commit v5 on v4

--- a/solution.py
+++ b/solution.py
@@ -353,7 +353,8 @@
         running = matrix[b, b]
         for s in range(b):
             running = running - factor[b, s] * factor[b, s]
-        scale.append(1.0 / jnp.sqrt(running))
+        guess = lax.rsqrt(running)
+        scale.append(guess * (1.5 - (0.5 * running * guess) * guess))
         for a in range(b + 1, extent):
             running = matrix[a, b]
             for s in range(b):
@@ -396,13 +397,13 @@
             place = layer * 25 + v
             cell = whole_ref[place // 32, band, place % 32]
             if v < 20:
-                stage_ref[v // 10, pl.ds(v % 10, 8, stride=10), :] = cell
+                stage_ref[at, v // 10, pl.ds(v % 10, 8, stride=10), :] = cell
             else:
-                stage_ref[2, pl.ds(v - 20, 8, stride=10), :] = cell
-                stage_ref[2, pl.ds(v - 15, 8, stride=10), :] = pltpu.roll(cell, 64, 1)
+                stage_ref[at, 2, pl.ds(v - 20, 8, stride=10), :] = cell
+                stage_ref[at, 2, pl.ds(v - 15, 8, stride=10), :] = pltpu.roll(cell, 64, 1)
         for tile in range(2):
-            plane_ref[at, :, tile * 128 : tile * 128 + 128] = stage_ref[tile]
-        plane_ref[at, :, 256:320] = stage_ref[2, :, 0:64]
+            plane_ref[at, :, tile * 128 : tile * 128 + 128] = stage_ref[at, tile]
+        plane_ref[at, :, 256:320] = stage_ref[at, 2, :, 0:64]
         copy_out(at).start()
     for at in range(BANDS * LAYERS):
         copy_out(at).wait()
@@ -474,7 +475,7 @@
     (rotated,) = call(
         merge_kernel,
         ((BANDS, LAYERS, 80, 320),),
-        scratch=((GROUPS,) + PIECE, stage, (planes, 80, 320)),
+        scratch=((GROUPS,) + PIECE, (planes,) + stage, (planes, 80, 320)),
         semaphores=planes,
         out_specs=(pl.BlockSpec(memory_space=pl.ANY),),
     )(*pieces)

time: 127 us -> 127 us (level)
  no operation moved by 1% of the time
where the time goes in v5:
time: 127 us
  starting transfers between devices  52.7 us (41%)
  blocking collectives  27 us (21%)
  Pallas kernels  22.5 us (18%)
  waiting for transfers between devices  21.9 us (17%)
  between operations  1.63 us (1%)
  local copies, waits for them, and re-layouts  1.29 us (1%)
    ppermute x22, starting transfers between devices, swapped(): lax.ppermute(array, axis, [(i, partner(i)) for i in range(lax.axis_size(a...  52.7 us
    all_to_all x1, blocking collectives, local(): sums = lax.all_to_all(sums, ('dy', 'band', 'dx'), 0, 0)  27 us
    ppermute x22, waiting for transfers between devices, swapped(): lax.ppermute(array, axis, [(i, partner(i)) for i in range(lax.axis_size(a...  21.9 us
    pallas_call x3, Pallas kernels, local(): call(functools.partial(inner_kernel, False), (STATE,), scratch=(wide,))  12 us
    pallas_call x1, Pallas kernels, local(): call(functools.partial(inner_kernel, True), (STATE, STATE[1:]), scratch=(...  4.02 us
  transfers between devices with their start and end apart: 22, of which 9 were waited for; matrix products, arithmetic and copies ran while one was open for 0% of the time, Pallas kernels for 13%

profile of v5, /device:TPU:1, one launch (start us, length us, event | category | flops | bytes accessed | tf_op | source)
XLA Modules:
  0.0 126.9 jit_solution(1958756010161766327)
XLA Ops:
  1.7 2.7 %collective-permute-start = (f32[2,4,25,8,128]{4,3,2,1,0:T(8,128)S(1)}, f32[2,4,25,8,128]{4,3,2,1,0:T(8,128)S(1)}, u32[]{:S(2)}, u32[]{:S(2)}) collective-permute-start(f32[2,4,25,8,128]{4,3,2,1,0:T(8,128)S(1)} %get-tuple-element.39), channel_id=1, source_target_pairs={{0,240},{16,32},{32,16},{48,64},{64,48},{80,96},{96,80},{112,128},... | collective-permute-start | bytes 2457608 | tf_op jit(solution)/shard_map/ppermute | solution.py:413
  4.4 2.5 %collective-permute-start.1 = (f32[2,4,25,8,128]{4,3,2,1,0:T(8,128)S(1)}, f32[2,4,25,8,128]{4,3,2,1,0:T(8,128)S(1)}, u32[]{:S(2)}, u32[]{:S(2)}) collective-permute-start(f32[2,4,25,8,128]{4,3,2,1,0:T(8,128)S(1)} %get-tuple-element.40), channel_id=1, source_target_pairs={{0,16},{16,0},{32,48},{48,32},{64,80},{80,64},{96,112},{112,96},{1... | collective-permute-start | bytes 2457608 | tf_op jit(solution)/shard_map/ppermute | solution.py:413
  6.8 3.0 %collective-permute-start.2 = (f32[104,128]{1,0:T(8,128)S(1)}, f32[104,128]{1,0:T(8,128)S(1)}, u32[]{:S(2)}, u32[]{:S(2)}) collective-permute-start(f32[104,128]{1,0:T(8,128)S(1)} %get-tuple-element.41), channel_id=1, source_target_pairs={{0,4},{4,0},{8,12},{12,8},{1,5},{5,1},{9,13},{13,9},{2,6},{6,2},{1... | collective-permute-start | bytes 159752 | tf_op jit(solution)/shard_map/ppermute | solution.py:413
  9.8 3.3 %collective-permute-start.3 = (f32[104,128]{1,0:T(8,128)S(1)}, f32[104,128]{1,0:T(8,128)S(1)}, u32[]{:S(2)}, u32[]{:S(2)}) collective-permute-start(f32[104,128]{1,0:T(8,128)S(1)} %get-tuple-element.42), channel_id=1, source_target_pairs={{0,12},{4,8},{8,4},{12,0},{1,13},{5,9},{9,5},{13,1},{2,14},{6,10},... | collective-permute-start | bytes 159752 | tf_op jit(solution)/shard_map/ppermute | solution.py:413
  14.4 4.0 %shard_map.47 = (f32[2,5,3,10,8,128]{5,4,3,2,1,0:T(8,128)S(1)}, f32[5,3,10,8,128]{4,3,2,1,0:T(8,128)S(1)}) custom-call(f32[2,5,3,10,8,128]{5,4,3,2,1,0:T(8,128)S(1)} %get-tuple-element.37.refs_0_.refs_1_, f32[5,80,320]{2,1,0:T(8,128)S(1)} %copy-done.1, f32[1,1]{1,0:T(1,128)} %bitcast.2.refs_2_, f32[1,1]{1,0:T(1,128)} %bitcast.10.refs_3_), custom_call_target="tpu_custom_call" | custom-call | flops 4000000 | bytes 4000000 | tf_op jit(solution)/shard_map/pallas_call | solution.py:445
  20.0 5.8 %collective-permute-start.5 = (f32[2,4,25,8,128]{4,3,2,1,0:T(8,128)S(1)}, f32[2,4,25,8,128]{4,3,2,1,0:T(8,128)S(1)}, u32[]{:S(2)}, u32[]{:S(2)}) collective-permute-start(f32[2,4,25,8,128]{4,3,2,1,0:T(8,128)S(1)} %get-tuple-element.46), channel_id=1, source_target_pairs={{0,16},{16,0},{32,48},{48,32},{64,80},{80,64},{96,112},{112,96},{1... | collective-permute-start | bytes 2457608 | tf_op jit(solution)/shard_map/ppermute | solution.py:413
  27.3 2.3 %collective-permute-start.7 = (f32[104,128]{1,0:T(8,128)S(1)}, f32[104,128]{1,0:T(8,128)S(1)}, u32[]{:S(2)}, u32[]{:S(2)}) collective-permute-start(f32[104,128]{1,0:T(8,128)S(1)} %get-tuple-element.48), channel_id=1, source_target_pairs={{0,12},{4,8},{8,4},{12,0},{1,13},{5,9},{9,5},{13,1},{2,14},{6,10},... | collective-permute-start | bytes 159752 | tf_op jit(solution)/shard_map/ppermute | solution.py:413
  29.6 4.0 %shard_map.49.refs_0_ = f32[2,5,3,10,8,128]{5,4,3,2,1,0:T(8,128)S(1)} custom-call(f32[2,5,3,10,8,128]{5,4,3,2,1,0:T(8,128)S(1)} %get-tuple-element.43.refs_0_.refs_1_, f32[2,5,3,10,8,128]{5,4,3,2,1,0:T(8,128)S(1)} %get-tuple-element.37.refs_0_.refs_1_, f32[5,3,10,8,128]{4,3,2,1,0:T(8,128)S(1)} %get-tuple-element.44.refs_2_, f32[1,1]{1,0:T(1,128)} %bitcast.4.refs_3_, ...), custom_call_target="tpu_custom_call" | custom-call | flops 4000000 | bytes 4000000 | tf_op jit(solution)/shard_map/pallas_call | solution.py:449
  34.8 7.6 %collective-permute-start.9 = (f32[2,4,25,8,128]{4,3,2,1,0:T(8,128)S(1)}, f32[2,4,25,8,128]{4,3,2,1,0:T(8,128)S(1)}, u32[]{:S(2)}, u32[]{:S(2)}) collective-permute-start(f32[2,4,25,8,128]{4,3,2,1,0:T(8,128)S(1)} %get-tuple-element.51), channel_id=1, source_target_pairs={{0,16},{16,0},{32,48},{48,32},{64,80},{80,64},{96,112},{112,96},{1... | collective-permute-start | bytes 2457608 | tf_op jit(solution)/shard_map/ppermute | solution.py:413
  42.4 1.6 %collective-permute-start.10 = (f32[104,128]{1,0:T(8,128)S(1)}, f32[104,128]{1,0:T(8,128)S(1)}, u32[]{:S(2)}, u32[]{:S(2)}) collective-permute-start(f32[104,128]{1,0:T(8,128)S(1)} %get-tuple-element.52), channel_id=1, source_target_pairs={{0,4},{4,0},{8,12},{12,8},{1,5},{5,1},{9,13},{13,9},{2,6},{6,2},{1... | collective-permute-start | bytes 159752 | tf_op jit(solution)/shard_map/ppermute | solution.py:413
  44.0 2.1 %collective-permute-start.11 = (f32[104,128]{1,0:T(8,128)S(1)}, f32[104,128]{1,0:T(8,128)S(1)}, u32[]{:S(2)}, u32[]{:S(2)}) collective-permute-start(f32[104,128]{1,0:T(8,128)S(1)} %get-tuple-element.53), channel_id=1, source_target_pairs={{0,12},{4,8},{8,4},{12,0},{1,13},{5,9},{9,5},{13,1},{2,14},{6,10},... | collective-permute-start | bytes 159752 | tf_op jit(solution)/shard_map/ppermute | solution.py:413
  46.1 4.0 %shard_map.51.refs_0_ = f32[2,5,3,10,8,128]{5,4,3,2,1,0:T(8,128)S(1)} custom-call(f32[2,5,3,10,8,128]{5,4,3,2,1,0:T(8,128)S(1)} %get-tuple-element.49.refs_0_.refs_1_, f32[2,5,3,10,8,128]{5,4,3,2,1,0:T(8,128)S(1)} %get-tuple-element.43.refs_0_.refs_1_, f32[5,3,10,8,128]{4,3,2,1,0:T(8,128)S(1)} %get-tuple-element.44.refs_2_, f32[1,1]{1,0:T(1,128)} %bitcast.6.refs_3_, ...), custom_call_target="tpu_custom_call" | custom-call | flops 4000000 | bytes 4000000 | tf_op jit(solution)/shard_map/pallas_call | solution.py:449
  51.2 8.8 %collective-permute-start.13 = (f32[2,4,25,8,128]{4,3,2,1,0:T(8,128)S(1)}, f32[2,4,25,8,128]{4,3,2,1,0:T(8,128)S(1)}, u32[]{:S(2)}, u32[]{:S(2)}) collective-permute-start(f32[2,4,25,8,128]{4,3,2,1,0:T(8,128)S(1)} %get-tuple-element.56), channel_id=1, source_target_pairs={{0,16},{16,0},{32,48},{48,32},{64,80},{80,64},{96,112},{112,96},{1... | collective-permute-start | bytes 2457608 | tf_op jit(solution)/shard_map/ppermute | solution.py:413
  62.7 4.0 %shard_map.53.refs_0_ = f32[2,5,3,10,8,128]{5,4,3,2,1,0:T(8,128)S(1)} custom-call(f32[2,5,3,10,8,128]{5,4,3,2,1,0:T(8,128)S(1)} %get-tuple-element.54.refs_0_, f32[2,5,3,10,8,128]{5,4,3,2,1,0:T(8,128)S(1)} %get-tuple-element.49.refs_0_.refs_1_, f32[5,3,10,8,128]{4,3,2,1,0:T(8,128)S(1)} %get-tuple-element.44.refs_2_, f32[1,1]{1,0:T(1,128)} %bitcast.8.refs_3_, ...), custom_call_target="tpu_custom_call" | custom-call | flops 4000000 | bytes 4000000 | tf_op jit(solution)/shard_map/pallas_call | solution.py:449
  69.8 2.6 %collective-permute-start.17 = (f32[2,32,8,128]{3,2,1,0:T(8,128)S(1)}, f32[2,32,8,128]{3,2,1,0:T(8,128)S(1)}, u32[]{:S(2)}, u32[]{:S(2)}) collective-permute-start(f32[2,32,8,128]{3,2,1,0:T(8,128)S(1)} %get-tuple-element.61), channel_id=1, source_target_pairs={{0,2},{1,3},{2,0},{3,1},{4,6},{5,7},{6,4},{7,5},{8,10},{9,11},{10,... | collective-permute-start | bytes 786440 | tf_op jit(solution)/shard_map/ppermute | solution.py:413
  72.4 1.6 %collective-permute-done.16.refs_1_ = f32[2,32,8,128]{3,2,1,0:T(8,128)S(1)} collective-permute-done((f32[2,32,8,128]{3,2,1,0:T(8,128)S(1)}, f32[2,32,8,128]{3,2,1,0:T(8,128)S(1)}, u32[]{:S(2)}, u32[]{:S(2)}) %collective-permute-start.16) | collective-permute-done | bytes 262176 | tf_op jit(solution)/shard_map/ppermute | solution.py:413
  74.0 5.1 %collective-permute-done.17.refs_2_ = f32[2,32,8,128]{3,2,1,0:T(8,128)S(1)} collective-permute-done((f32[2,32,8,128]{3,2,1,0:T(8,128)S(1)}, f32[2,32,8,128]{3,2,1,0:T(8,128)S(1)}, u32[]{:S(2)}, u32[]{:S(2)}) %collective-permute-start.17) | collective-permute-done | bytes 262176 | tf_op jit(solution)/shard_map/ppermute | solution.py:413
  79.1 2.6 %collective-permute-done.18.refs_3_ = f32[2,32,8,128]{3,2,1,0:T(8,128)S(1)} collective-permute-done((f32[2,32,8,128]{3,2,1,0:T(8,128)S(1)}, f32[2,32,8,128]{3,2,1,0:T(8,128)S(1)}, u32[]{:S(2)}, u32[]{:S(2)}) %collective-permute-start.18) | collective-permute-done | bytes 262176 | tf_op jit(solution)/shard_map/ppermute | solution.py:413
  82.4 27.0 %all_to_all.5.sums_ref = f32[256,1,128]{2,1,0:T(1,128)S(1)} all-to-all(f32[256,1,128]{2,1,0:T(1,128)S(1)} %get-tuple-element.64), channel_id=1, replica_groups=mesh['dx'=16,'dy'=4,'band'=4] {'dy','band','dx'}, dimensions={0} | all-to-all | bytes 262144 | tf_op jit(solution)/shard_map/all_to_all | solution.py:469
  110.5 1.5 %collective-permute-start.20 = (f32[2,32,8,128]{3,2,1,0:T(8,128)S(1)}, f32[2,32,8,128]{3,2,1,0:T(8,128)S(1)}, u32[]{:S(2)}, u32[]{:S(2)}) collective-permute-start(f32[2,32,8,128]{3,2,1,0:T(8,128)S(1)} %get-tuple-element.67), channel_id=1, source_target_pairs={{0,2},{1,3},{2,0},{3,1},{4,6},{5,7},{6,4},{7,5},{8,10},{9,11},{10,... | collective-permute-start | bytes 786440 | tf_op jit(solution)/shard_map/ppermute | solution.py:413
  112.0 2.0 %collective-permute-start.21 = (f32[2,32,8,128]{3,2,1,0:T(8,128)S(1)}, f32[2,32,8,128]{3,2,1,0:T(8,128)S(1)}, u32[]{:S(2)}, u32[]{:S(2)}) collective-permute-start(f32[2,32,8,128]{3,2,1,0:T(8,128)S(1)} %get-tuple-element.68), channel_id=1, source_target_pairs={{0,3},{1,2},{2,1},{3,0},{4,7},{5,6},{6,5},{7,4},{8,11},{9,10},{10,... | collective-permute-start | bytes 786440 | tf_op jit(solution)/shard_map/ppermute | solution.py:413
  114.0 3.2 %collective-permute-done.19.refs_1_ = f32[2,32,8,128]{3,2,1,0:T(8,128)S(1)} collective-permute-done((f32[2,32,8,128]{3,2,1,0:T(8,128)S(1)}, f32[2,32,8,128]{3,2,1,0:T(8,128)S(1)}, u32[]{:S(2)}, u32[]{:S(2)}) %collective-permute-start.19) | collective-permute-done | bytes 262176 | tf_op jit(solution)/shard_map/ppermute | solution.py:413
  117.2 6.3 %collective-permute-done.20.refs_2_ = f32[2,32,8,128]{3,2,1,0:T(8,128)S(1)} collective-permute-done((f32[2,32,8,128]{3,2,1,0:T(8,128)S(1)}, f32[2,32,8,128]{3,2,1,0:T(8,128)S(1)}, u32[]{:S(2)}, u32[]{:S(2)}) %collective-permute-start.20) | collective-permute-done | bytes 262176 | tf_op jit(solution)/shard_map/ppermute | solution.py:413
  123.5 2.0 %collective-permute-done.21.refs_3_ = f32[2,32,8,128]{3,2,1,0:T(8,128)S(1)} collective-permute-done((f32[2,32,8,128]{3,2,1,0:T(8,128)S(1)}, f32[2,32,8,128]{3,2,1,0:T(8,128)S(1)}, u32[]{:S(2)}, u32[]{:S(2)}) %collective-permute-start.21) | collective-permute-done | bytes 262176 | tf_op jit(solution)/shard_map/ppermute | solution.py:413
  (37 shorter events, 15.7 us)
Async XLA Ops:
  0.0 1.3 %copy-start = (f32[2,5,80,320]{3,2,1,0:T(8,128)S(1)}, f32[2,5,80,320]{3,2,1,0:T(8,128)}, u32[]{:S(2)}) copy-start(f32[2,5,80,320]{3,2,1,0:T(8,128)} %field_ref.1) | copy-start | bytes 3072004
  1.3 13.1 %copy-start.1 = (f32[5,80,320]{2,1,0:T(8,128)S(1)}, f32[5,80,320]{2,1,0:T(8,128)}, u32[]{:S(2)}) copy-start(f32[5,80,320]{2,1,0:T(8,128)} %refs_1_.1) | copy-start | bytes 1536004
  1.7 16.8 %collective-permute-start = (f32[2,4,25,8,128]{4,3,2,1,0:T(8,128)S(1)}, f32[2,4,25,8,128]{4,3,2,1,0:T(8,128)S(1)}, u32[]{:S(2)}, u32[]{:S(2)}) collective-permute-start(f32[2,4,25,8,128]{4,3,2,1,0:T(8,128)S(1)} %get-tuple-element.39), channel_id=1, source_target_pairs={{0,240},{16,32},{32,16},{48,64},{64,48},{80,96},{96,80},{112,128},... | collective-permute-start | bytes 2457608 | tf_op jit(solution)/shard_map/ppermute | solution.py:413
  4.4 14.1 %collective-permute-start.1 = (f32[2,4,25,8,128]{4,3,2,1,0:T(8,128)S(1)}, f32[2,4,25,8,128]{4,3,2,1,0:T(8,128)S(1)}, u32[]{:S(2)}, u32[]{:S(2)}) collective-permute-start(f32[2,4,25,8,128]{4,3,2,1,0:T(8,128)S(1)} %get-tuple-element.40), channel_id=1, source_target_pairs={{0,16},{16,0},{32,48},{48,32},{64,80},{80,64},{96,112},{112,96},{1... | collective-permute-start | bytes 2457608 | tf_op jit(solution)/shard_map/ppermute | solution.py:413
  6.8 11.6 %collective-permute-start.2 = (f32[104,128]{1,0:T(8,128)S(1)}, f32[104,128]{1,0:T(8,128)S(1)}, u32[]{:S(2)}, u32[]{:S(2)}) collective-permute-start(f32[104,128]{1,0:T(8,128)S(1)} %get-tuple-element.41), channel_id=1, source_target_pairs={{0,4},{4,0},{8,12},{12,8},{1,5},{5,1},{9,13},{13,9},{2,6},{6,2},{1... | collective-permute-start | bytes 159752 | tf_op jit(solution)/shard_map/ppermute | solution.py:413
  9.8 8.6 %collective-permute-start.3 = (f32[104,128]{1,0:T(8,128)S(1)}, f32[104,128]{1,0:T(8,128)S(1)}, u32[]{:S(2)}, u32[]{:S(2)}) collective-permute-start(f32[104,128]{1,0:T(8,128)S(1)} %get-tuple-element.42), channel_id=1, source_target_pairs={{0,12},{4,8},{8,4},{12,0},{1,13},{5,9},{9,5},{13,1},{2,14},{6,10},... | collective-permute-start | bytes 159752 | tf_op jit(solution)/shard_map/ppermute | solution.py:413
  19.3 14.5 %collective-permute-start.4 = (f32[2,4,25,8,128]{4,3,2,1,0:T(8,128)S(1)}, f32[2,4,25,8,128]{4,3,2,1,0:T(8,128)S(1)}, u32[]{:S(2)}, u32[]{:S(2)}) collective-permute-start(f32[2,4,25,8,128]{4,3,2,1,0:T(8,128)S(1)} %get-tuple-element.45), channel_id=1, source_target_pairs={{0,240},{16,32},{32,16},{48,64},{64,48},{80,96},{96,80},{112,128},... | collective-permute-start | bytes 2457608 | tf_op jit(solution)/shard_map/ppermute | solution.py:413
  20.0 13.8 %collective-permute-start.5 = (f32[2,4,25,8,128]{4,3,2,1,0:T(8,128)S(1)}, f32[2,4,25,8,128]{4,3,2,1,0:T(8,128)S(1)}, u32[]{:S(2)}, u32[]{:S(2)}) collective-permute-start(f32[2,4,25,8,128]{4,3,2,1,0:T(8,128)S(1)} %get-tuple-element.46), channel_id=1, source_target_pairs={{0,16},{16,0},{32,48},{48,32},{64,80},{80,64},{96,112},{112,96},{1... | collective-permute-start | bytes 2457608 | tf_op jit(solution)/shard_map/ppermute | solution.py:413
  25.9 7.8 %collective-permute-start.6 = (f32[104,128]{1,0:T(8,128)S(1)}, f32[104,128]{1,0:T(8,128)S(1)}, u32[]{:S(2)}, u32[]{:S(2)}) collective-permute-start(f32[104,128]{1,0:T(8,128)S(1)} %get-tuple-element.47), channel_id=1, source_target_pairs={{0,4},{4,0},{8,12},{12,8},{1,5},{5,1},{9,13},{13,9},{2,6},{6,2},{1... | collective-permute-start | bytes 159752 | tf_op jit(solution)/shard_map/ppermute | solution.py:413
  27.3 6.6 %collective-permute-start.7 = (f32[104,128]{1,0:T(8,128)S(1)}, f32[104,128]{1,0:T(8,128)S(1)}, u32[]{:S(2)}, u32[]{:S(2)}) collective-permute-start(f32[104,128]{1,0:T(8,128)S(1)} %get-tuple-element.48), channel_id=1, source_target_pairs={{0,12},{4,8},{8,4},{12,0},{1,13},{5,9},{9,5},{13,1},{2,14},{6,10},... | collective-permute-start | bytes 159752 | tf_op jit(solution)/shard_map/ppermute | solution.py:413
  34.7 15.6 %collective-permute-start.8 = (f32[2,4,25,8,128]{4,3,2,1,0:T(8,128)S(1)}, f32[2,4,25,8,128]{4,3,2,1,0:T(8,128)S(1)}, u32[]{:S(2)}, u32[]{:S(2)}) collective-permute-start(f32[2,4,25,8,128]{4,3,2,1,0:T(8,128)S(1)} %get-tuple-element.50), channel_id=1, source_target_pairs={{0,240},{16,32},{32,16},{48,64},{64,48},{80,96},{96,80},{112,128},... | collective-permute-start | bytes 2457608 | tf_op jit(solution)/shard_map/ppermute | solution.py:413
  34.8 15.5 %collective-permute-start.9 = (f32[2,4,25,8,128]{4,3,2,1,0:T(8,128)S(1)}, f32[2,4,25,8,128]{4,3,2,1,0:T(8,128)S(1)}, u32[]{:S(2)}, u32[]{:S(2)}) collective-permute-start(f32[2,4,25,8,128]{4,3,2,1,0:T(8,128)S(1)} %get-tuple-element.51), channel_id=1, source_target_pairs={{0,16},{16,0},{32,48},{48,32},{64,80},{80,64},{96,112},{112,96},{1... | collective-permute-start | bytes 2457608 | tf_op jit(solution)/shard_map/ppermute | solution.py:413
  42.4 7.8 %collective-permute-start.10 = (f32[104,128]{1,0:T(8,128)S(1)}, f32[104,128]{1,0:T(8,128)S(1)}, u32[]{:S(2)}, u32[]{:S(2)}) collective-permute-start(f32[104,128]{1,0:T(8,128)S(1)} %get-tuple-element.52), channel_id=1, source_target_pairs={{0,4},{4,0},{8,12},{12,8},{1,5},{5,1},{9,13},{13,9},{2,6},{6,2},{1... | collective-permute-start | bytes 159752 | tf_op jit(solution)/shard_map/ppermute | solution.py:413
  44.0 6.3 %collective-permute-start.11 = (f32[104,128]{1,0:T(8,128)S(1)}, f32[104,128]{1,0:T(8,128)S(1)}, u32[]{:S(2)}, u32[]{:S(2)}) collective-permute-start(f32[104,128]{1,0:T(8,128)S(1)} %get-tuple-element.53), channel_id=1, source_target_pairs={{0,12},{4,8},{8,4},{12,0},{1,13},{5,9},{9,5},{13,1},{2,14},{6,10},... | collective-permute-start | bytes 159752 | tf_op jit(solution)/shard_map/ppermute | solution.py:413
  51.1 16.4 %collective-permute-start.12 = (f32[2,4,25,8,128]{4,3,2,1,0:T(8,128)S(1)}, f32[2,4,25,8,128]{4,3,2,1,0:T(8,128)S(1)}, u32[]{:S(2)}, u32[]{:S(2)}) collective-permute-start(f32[2,4,25,8,128]{4,3,2,1,0:T(8,128)S(1)} %get-tuple-element.55), channel_id=1, source_target_pairs={{0,240},{16,32},{32,16},{48,64},{64,48},{80,96},{96,80},{112,128},... | collective-permute-start | bytes 2457608 | tf_op jit(solution)/shard_map/ppermute | solution.py:413
  51.2 16.3 %collective-permute-start.13 = (f32[2,4,25,8,128]{4,3,2,1,0:T(8,128)S(1)}, f32[2,4,25,8,128]{4,3,2,1,0:T(8,128)S(1)}, u32[]{:S(2)}, u32[]{:S(2)}) collective-permute-start(f32[2,4,25,8,128]{4,3,2,1,0:T(8,128)S(1)} %get-tuple-element.56), channel_id=1, source_target_pairs={{0,16},{16,0},{32,48},{48,32},{64,80},{80,64},{96,112},{112,96},{1... | collective-permute-start | bytes 2457608 | tf_op jit(solution)/shard_map/ppermute | solution.py:413
  60.0 6.7 %collective-permute-start.14 = (f32[104,128]{1,0:T(8,128)S(1)}, f32[104,128]{1,0:T(8,128)S(1)}, u32[]{:S(2)}, u32[]{:S(2)}) collective-permute-start(f32[104,128]{1,0:T(8,128)S(1)} %get-tuple-element.57), channel_id=1, source_target_pairs={{0,4},{4,0},{8,12},{12,8},{1,5},{5,1},{9,13},{13,9},{2,6},{6,2},{1... | collective-permute-start | bytes 159752 | tf_op jit(solution)/shard_map/ppermute | solution.py:413
  61.5 6.0 %collective-permute-start.15 = (f32[104,128]{1,0:T(8,128)S(1)}, f32[104,128]{1,0:T(8,128)S(1)}, u32[]{:S(2)}, u32[]{:S(2)}) collective-permute-start(f32[104,128]{1,0:T(8,128)S(1)} %get-tuple-element.58), channel_id=1, source_target_pairs={{0,12},{4,8},{8,4},{12,0},{1,13},{5,9},{9,5},{13,1},{2,14},{6,10},... | collective-permute-start | bytes 159752 | tf_op jit(solution)/shard_map/ppermute | solution.py:413
  68.4 5.6 %collective-permute-start.16 = (f32[2,32,8,128]{3,2,1,0:T(8,128)S(1)}, f32[2,32,8,128]{3,2,1,0:T(8,128)S(1)}, u32[]{:S(2)}, u32[]{:S(2)}) collective-permute-start(f32[2,32,8,128]{3,2,1,0:T(8,128)S(1)} %get-tuple-element.60), channel_id=1, source_target_pairs={{0,1},{1,0},{2,3},{3,2},{4,5},{5,4},{6,7},{7,6},{8,9},{9,8},{10,11... | collective-permute-start | bytes 786440 | tf_op jit(solution)/shard_map/ppermute | solution.py:413
  69.8 9.3 %collective-permute-start.17 = (f32[2,32,8,128]{3,2,1,0:T(8,128)S(1)}, f32[2,32,8,128]{3,2,1,0:T(8,128)S(1)}, u32[]{:S(2)}, u32[]{:S(2)}) collective-permute-start(f32[2,32,8,128]{3,2,1,0:T(8,128)S(1)} %get-tuple-element.61), channel_id=1, source_target_pairs={{0,2},{1,3},{2,0},{3,1},{4,6},{5,7},{6,4},{7,5},{8,10},{9,11},{10,... | collective-permute-start | bytes 786440 | tf_op jit(solution)/shard_map/ppermute | solution.py:413
  72.4 9.2 %collective-permute-start.18 = (f32[2,32,8,128]{3,2,1,0:T(8,128)S(1)}, f32[2,32,8,128]{3,2,1,0:T(8,128)S(1)}, u32[]{:S(2)}, u32[]{:S(2)}) collective-permute-start(f32[2,32,8,128]{3,2,1,0:T(8,128)S(1)} %get-tuple-element.62), channel_id=1, source_target_pairs={{0,3},{1,2},{2,1},{3,0},{4,7},{5,6},{6,5},{7,4},{8,11},{9,10},{10,... | collective-permute-start | bytes 786440 | tf_op jit(solution)/shard_map/ppermute | solution.py:413
  110.1 7.1 %collective-permute-start.19 = (f32[2,32,8,128]{3,2,1,0:T(8,128)S(1)}, f32[2,32,8,128]{3,2,1,0:T(8,128)S(1)}, u32[]{:S(2)}, u32[]{:S(2)}) collective-permute-start(f32[2,32,8,128]{3,2,1,0:T(8,128)S(1)} %get-tuple-element.66), channel_id=1, source_target_pairs={{0,1},{1,0},{2,3},{3,2},{4,5},{5,4},{6,7},{7,6},{8,9},{9,8},{10,11... | collective-permute-start | bytes 786440 | tf_op jit(solution)/shard_map/ppermute | solution.py:413
  110.5 13.0 %collective-permute-start.20 = (f32[2,32,8,128]{3,2,1,0:T(8,128)S(1)}, f32[2,32,8,128]{3,2,1,0:T(8,128)S(1)}, u32[]{:S(2)}, u32[]{:S(2)}) collective-permute-start(f32[2,32,8,128]{3,2,1,0:T(8,128)S(1)} %get-tuple-element.67), channel_id=1, source_target_pairs={{0,2},{1,3},{2,0},{3,1},{4,6},{5,7},{6,4},{7,5},{8,10},{9,11},{10,... | collective-permute-start | bytes 786440 | tf_op jit(solution)/shard_map/ppermute | solution.py:413
  112.0 13.5 %collective-permute-start.21 = (f32[2,32,8,128]{3,2,1,0:T(8,128)S(1)}, f32[2,32,8,128]{3,2,1,0:T(8,128)S(1)}, u32[]{:S(2)}, u32[]{:S(2)}) collective-permute-start(f32[2,32,8,128]{3,2,1,0:T(8,128)S(1)} %get-tuple-element.68), channel_id=1, source_target_pairs={{0,3},{1,2},{2,1},{3,0},{4,7},{5,6},{6,5},{7,4},{8,11},{9,10},{10,... | collective-permute-start | bytes 786440 | tf_op jit(solution)/shard_map/ppermute | solution.py:413
